TPU v7x, 32 devices: a whole 2x2x4 slice. The times are simulated.
32 devices in a mesh: dp: 8 (over z, x), tensor: 4 (over y, core).
Axes of the slice: x: 2, y: 2, z: 4, core: 2. Of those that a mesh axis runs over, the one named last changes fastest.
Arguments:
- resid: float32 [8192, 768], P('dp'), may hold values from -6 to 6
- cotangent: float32 [8192, 768], P('dp'), may hold values from -6 to 6
- master_in: float32 [1, 768, 7, 768], P(None, 'dp', None, 'tensor'), may hold values from -0.21875 to 0.21875
- moment1_in: float32 [1, 768, 7, 768], P(None, 'dp', None, 'tensor'), may hold values from -8192 to 8192
- moment2_in: float32 [1, 768, 7, 768], P(None, 'dp', None, 'tensor'), may hold values from 0 to 8192
- master_out: float32 [1, 5, 768, 768], P(None, None, 'tensor', 'dp'), may hold values from -0.875 to 0.875
- moment1_out: float32 [1, 5, 768, 768], P(None, None, 'tensor', 'dp'), may hold values from -8192 to 8192
- moment2_out: float32 [1, 5, 768, 768], P(None, None, 'tensor', 'dp'), may hold values from 0 to 8192
- master_bias: float32 [1, 6, 768], P(None, None, 'tensor'), may hold values from -3 to 3
- moment1_bias: float32 [1, 6, 768], P(None, None, 'tensor'), may hold values from -8192 to 8192
- moment2_bias: float32 [1, 6, 768], P(None, None, 'tensor'), may hold values from 0 to 8192
- master_vec: float32 [1, 6, 768], replicated, may hold values from -1.2 to 1.3, as said below
- moment1_vec: float32 [1, 6, 768], replicated, may hold values from -8192 to 8192
- moment2_vec: float32 [1, 6, 768], replicated, may hold values from 0 to 8192
Outputs:
- out_stream: float32 [8192, 768], P(('dp', 'tensor'))
- grad_stream: float32 [8192, 768], P(('dp', 'tensor'))
- new_moment1_in: float32 [1, 768, 7, 768], P(None, 'dp', None, 'tensor')
- new_moment2_in: float32 [1, 768, 7, 768], P(None, 'dp', None, 'tensor')
- new_master_in: float32 [1, 768, 7, 768], P(None, 'dp', None, 'tensor')
- new_moment1_out: float32 [1, 5, 768, 768], P(None, None, 'tensor', 'dp')
- new_moment2_out: float32 [1, 5, 768, 768], P(None, None, 'tensor', 'dp')
- new_master_out: float32 [1, 5, 768, 768], P(None, None, 'tensor', 'dp')
- new_moment1_bias: float32 [1, 6, 768], P(None, None, 'tensor')
- new_moment2_bias: float32 [1, 6, 768], P(None, None, 'tensor')
- new_master_bias: float32 [1, 6, 768], P(None, None, 'tensor')
- new_moment1_vec: float32 [1, 6, 768], replicated
- new_moment2_vec: float32 [1, 6, 768], replicated
- new_master_vec: float32 [1, 6, 768], replicated
Inputs may be any that keep to these rules, and one draw needn't show every extreme that they name: `master_vec`: rows 0 and 2 of each block lie within 0.7 to 1.3.
All inputs are finite; a program needn't handle non-finite values.
Results may differ from a plain program's by a relative error of at most 0.014.
Values may be sent and summed in bfloat16 or wider, within the bound.
A program may use at most 128 MiB of HBM per device.

v0:
```python
import jax
import jax.numpy as jnp
from jax import lax
from jax.sharding import PartitionSpec as P

D = 768
HD = 64
LEN = 1024
LAYERS = 1
STEP = 10


EPS = 1e-05
BRANCH_SCALE = 48 ** (-0.5)
BETA_ONE = 0.9
BETA_TWO = 0.95
ADAM_EPS = 1e-08
DECAY = 0.1
SMALL_RATE = 0.3
MASKED = -1e30


def norm_rows(stream, gain, shift):
    center = stream - jnp.mean(stream, -1, keepdims=True)
    inverse = lax.rsqrt(jnp.mean(center * center, -1, keepdims=True) + EPS)
    scaled = center * inverse
    return (scaled * gain + shift, scaled, inverse)


def norm_back(grad_out, scaled, inverse, gain):
    weighted = grad_out * gain
    centered = weighted - jnp.mean(weighted, -1, keepdims=True)
    return inverse * (centered - scaled * jnp.mean(weighted * scaled, -1, keepdims=True))


def plain_dot(left, right):
    return jnp.dot(left, right, preferred_element_type=jnp.float32)


def left_dot(left, right):
    return lax.dot_general(
        left, right, (((0,), (0,)), ((), ())), preferred_element_type=jnp.float32
    )


def right_dot(left, right):
    return lax.dot_general(
        left, right, (((1,), (1,)), ((), ())), preferred_element_type=jnp.float32
    )


def smooth_gate(values_in):
    return jax.nn.gelu(values_in, approximate=True)


def tensor_rows(array_in):
    quarter = array_in.shape[0] // lax.axis_size("tensor")
    return lax.dynamic_slice_in_dim(array_in, lax.axis_index("tensor") * quarter, quarter, 0)


def own_rows(array_in):
    return tensor_rows(array_in)


def branch_total(partial_sum):
    return lax.psum(partial_sum.astype(jnp.bfloat16), "tensor").astype(jnp.float32)


def grad_total(partial_sum):
    return lax.psum(partial_sum.astype(jnp.bfloat16), "tensor").astype(jnp.float32)


def causal_scores(queries, key_rows, first, last):
    block_rows = last - first
    scores = jnp.einsum(
        "qhd,khd->hqk", queries[first:last], key_rows[:last], preferred_element_type=jnp.float32
    ) * HD ** (-0.5)
    query_pos = lax.broadcasted_iota(jnp.int32, (block_rows, last), 0) + first
    key_pos = lax.broadcasted_iota(jnp.int32, (block_rows, last), 1)
    return jnp.where(query_pos >= key_pos, scores, MASKED)


def attend_sequence(operands):
    queries, key_rows, value_rows = operands
    block_rows = min(512, LEN)
    outputs = []
    totals = []
    for block_idx in range(LEN // block_rows):
        first = block_idx * block_rows
        last = first + block_rows
        scores = causal_scores(queries, key_rows, first, last)
        highest = jnp.max(scores, -1, keepdims=True)
        expo = jnp.exp(scores - highest)
        summed = jnp.sum(expo, -1, keepdims=True)
        weights = (expo / summed).astype(jnp.bfloat16)
        mixed = jnp.einsum(
            "hqk,khd->qhd", weights, value_rows[:last], preferred_element_type=jnp.float32
        )
        outputs.append(mixed.astype(jnp.bfloat16))
        totals.append((highest + jnp.log(summed))[..., 0])
    return (jnp.concatenate(outputs, 0), jnp.concatenate(totals, 1))


def attend_back(operands):
    queries, key_rows, value_rows, log_total, grad_mixed = operands
    block_rows = min(512, LEN)
    d_keys = jnp.zeros(key_rows.shape, jnp.float32)
    d_values = jnp.zeros(value_rows.shape, jnp.float32)
    d_queries = []
    for block_idx in range(LEN // block_rows):
        first = block_idx * block_rows
        last = first + block_rows
        scores = causal_scores(queries, key_rows, first, last)
        probs = jnp.exp(scores - log_total[:, first:last, None])
        d_probs = jnp.einsum(
            "qhd,khd->hqk",
            grad_mixed[first:last],
            value_rows[:last],
            preferred_element_type=jnp.float32,
        )
        inner = jnp.sum(probs * d_probs, -1, keepdims=True)
        d_scores = (probs * (d_probs - inner)).astype(jnp.bfloat16)
        d_queries.append(
            jnp.einsum(
                "hqk,khd->qhd", d_scores, key_rows[:last], preferred_element_type=jnp.float32
            )
            * HD ** (-0.5)
        )
        key_part = jnp.einsum(
            "hqk,qhd->khd", d_scores, queries[first:last], preferred_element_type=jnp.float32
        ) * HD ** (-0.5)
        value_part = jnp.einsum(
            "hqk,qhd->khd",
            probs.astype(jnp.bfloat16),
            grad_mixed[first:last],
            preferred_element_type=jnp.float32,
        )
        d_keys = d_keys.at[:last].add(key_part)
        d_values = d_values.at[:last].add(value_part)
    return (jnp.concatenate(d_queries, 0), d_keys, d_values)


def layer_forward(stream, w_in, w_out, bias, vector):
    model_width = w_in.shape[0]
    head_cols = w_in.shape[2]
    heads_here = head_cols // HD
    normed, scaled_one, inverse_one = norm_rows(stream, vector[0], vector[1])
    normed_low = normed.astype(jnp.bfloat16)
    seq_count = normed_low.shape[0] // LEN
    shape4 = (seq_count, LEN, heads_here, HD)
    w_qkv = w_in[:, 0:3].reshape(model_width, 3 * head_cols)
    projected = plain_dot(normed_low, w_qkv)
    queries = (projected[:, :head_cols] + bias[0]).astype(jnp.bfloat16).reshape(shape4)
    key_rows = projected[:, head_cols : 2 * head_cols].astype(jnp.bfloat16).reshape(shape4)
    value_rows = (projected[:, 2 * head_cols :] + bias[1]).astype(jnp.bfloat16).reshape(shape4)
    mixed, log_total = lax.map(attend_sequence, (queries, key_rows, value_rows))
    mixed_low = mixed.reshape(-1, head_cols)
    attended = branch_total(plain_dot(mixed_low, w_out[0])) + vector[4]
    middle = stream + BRANCH_SCALE * attended
    hidden, scaled_two, inverse_two = norm_rows(middle, vector[2], vector[3])
    hidden_low = hidden.astype(jnp.bfloat16)
    w_up = w_in[:, 3:].reshape(model_width, 4 * head_cols)
    pre_act = plain_dot(hidden_low, w_up) + bias[2:].reshape(4 * head_cols)
    act_low = smooth_gate(pre_act).astype(jnp.bfloat16)
    w_down = w_out[1:].reshape(4 * head_cols, model_width)
    mlp_out = branch_total(plain_dot(act_low, w_down)) + vector[5]
    result = middle + BRANCH_SCALE * mlp_out
    kept = (
        scaled_one,
        inverse_one,
        normed_low,
        queries,
        key_rows,
        value_rows,
        log_total,
        mixed_low,
        scaled_two,
        inverse_two,
        hidden_low,
        pre_act,
        act_low,
    )
    return (result, kept)


def layer_backward(gradient, w_in, w_out, vector, kept):
    (
        scaled_one,
        inverse_one,
        normed_low,
        queries,
        key_rows,
        value_rows,
        log_total,
        mixed_low,
        scaled_two,
        inverse_two,
        hidden_low,
        pre_act,
        act_low,
    ) = kept
    model_width = w_in.shape[0]
    head_cols = w_in.shape[2]
    w_qkv = w_in[:, 0:3].reshape(model_width, 3 * head_cols)
    w_up = w_in[:, 3:].reshape(model_width, 4 * head_cols)
    w_down = w_out[1:].reshape(4 * head_cols, model_width)
    d_mlp = (BRANCH_SCALE * gradient).astype(jnp.bfloat16)
    g_bdown = jnp.sum(own_rows(d_mlp).astype(jnp.float32), 0)
    g_down = left_dot(act_low, d_mlp).reshape(4, head_cols, model_width)
    d_act = right_dot(d_mlp, w_down).astype(jnp.bfloat16)
    gate_value, gate_pull = jax.vjp(smooth_gate, pre_act)
    d_pre = gate_pull(d_act.astype(jnp.float32))[0].astype(jnp.bfloat16)
    g_bup = jnp.sum(d_pre.astype(jnp.float32), 0)
    g_up = left_dot(hidden_low, d_pre).reshape(model_width, 4, head_cols)
    d_hidden = grad_total(right_dot(d_pre, w_up))
    g_gain_two = jnp.sum(own_rows(d_hidden * scaled_two), 0)
    g_shift_two = jnp.sum(own_rows(d_hidden), 0)
    d_middle = gradient + norm_back(d_hidden, scaled_two, inverse_two, vector[2])
    d_attn = (BRANCH_SCALE * d_middle).astype(jnp.bfloat16)
    g_bproj = jnp.sum(own_rows(d_attn).astype(jnp.float32), 0)
    g_proj = left_dot(mixed_low, d_attn)
    d_mixed = right_dot(d_attn, w_out[0]).astype(jnp.bfloat16)
    d_queries, d_keys, d_values = lax.map(
        attend_back, (queries, key_rows, value_rows, log_total, d_mixed.reshape(queries.shape))
    )
    d_qkv = jnp.concatenate(
        [
            d_queries.reshape(-1, head_cols),
            d_keys.reshape(-1, head_cols),
            d_values.reshape(-1, head_cols),
        ],
        1,
    ).astype(jnp.bfloat16)
    g_qkv = left_dot(normed_low, d_qkv).reshape(model_width, 3, head_cols)
    g_bq = jnp.sum(d_qkv[:, :head_cols].astype(jnp.float32), 0)
    g_bv = jnp.sum(d_qkv[:, 2 * head_cols :].astype(jnp.float32), 0)
    d_normed = grad_total(right_dot(d_qkv, w_qkv))
    g_gain_one = jnp.sum(own_rows(d_normed * scaled_one), 0)
    g_shift_one = jnp.sum(own_rows(d_normed), 0)
    d_stream = d_middle + norm_back(d_normed, scaled_one, inverse_one, vector[0])
    g_in = jnp.concatenate([g_qkv, g_up], 1)
    g_out = jnp.concatenate([g_proj[None], g_down], 0)
    g_bias = jnp.concatenate([g_bq[None], g_bv[None], g_bup.reshape(4, head_cols)], 0)
    g_vector = jnp.stack([g_gain_one, g_shift_one, g_gain_two, g_shift_two, g_bproj, g_bdown])
    return (d_stream, g_in, g_out, g_bias, g_vector)


def adam_step(master, first, second, gradient, rate, decay):
    first_new = BETA_ONE * first + (1 - BETA_ONE) * gradient
    second_new = BETA_TWO * second + (1 - BETA_TWO) * gradient * gradient
    direction = (
        first_new / (1 - BETA_ONE**STEP) / (jnp.sqrt(second_new / (1 - BETA_TWO**STEP)) + ADAM_EPS)
    )
    return (first_new, second_new, master - rate * (direction + decay * master))


def shards(
    resid,
    cotangent,
    master_in,
    moment1_in,
    moment2_in,
    master_out,
    moment1_out,
    moment2_out,
    master_bias,
    moment1_bias,
    moment2_bias,
    master_vec,
    moment1_vec,
    moment2_vec,
):
    weights_in, weights_out = (
        lax.all_gather(master_in.astype(jnp.bfloat16), "dp", axis=1, tiled=True),
        lax.all_gather(master_out.astype(jnp.bfloat16), "dp", axis=3, tiled=True),
    )
    stream = resid
    gradient = cotangent
    layer_idx = 0
    stream, kept = layer_forward(
        stream,
        weights_in[layer_idx],
        weights_out[layer_idx],
        master_bias[layer_idx],
        master_vec[layer_idx],
    )
    kept_list = [kept]
    list_in = [None] * LAYERS
    list_out = [None] * LAYERS
    list_bias = [None] * LAYERS
    list_vector = [None] * LAYERS
    layer_idx = 0
    gradient, g_in, g_out, g_bias, g_vector = layer_backward(
        gradient,
        weights_in[layer_idx],
        weights_out[layer_idx],
        master_vec[layer_idx],
        kept_list[layer_idx],
    )
    list_in[layer_idx] = g_in
    list_out[layer_idx] = g_out
    list_bias[layer_idx] = g_bias
    list_vector[layer_idx] = g_vector
    summed_in = jnp.stack(list_in)
    summed_out = jnp.stack(list_out)
    summed_in, summed_out = (
        lax.psum_scatter(summed_in, "dp", scatter_dimension=1, tiled=True),
        lax.psum_scatter(summed_out, "dp", scatter_dimension=3, tiled=True),
    )
    summed_bias = lax.psum(jnp.stack(list_bias), "dp")
    summed_vector = lax.psum(jnp.stack(list_vector), ("dp", "tensor"))
    first_in, second_in, new_in = adam_step(
        master_in, moment1_in, moment2_in, summed_in, 0.5 * D ** (-0.5), DECAY
    )
    first_out, second_out, new_out = adam_step(
        master_out, moment1_out, moment2_out, summed_out, 2.0 * D ** (-0.5), DECAY
    )
    first_bias, second_bias, new_bias = adam_step(
        master_bias, moment1_bias, moment2_bias, summed_bias, SMALL_RATE, 0.0
    )
    first_vec, second_vec, new_vec = adam_step(
        master_vec, moment1_vec, moment2_vec, summed_vector, SMALL_RATE, 0.0
    )
    return (
        own_rows(stream),
        own_rows(gradient),
        first_in,
        second_in,
        new_in,
        first_out,
        second_out,
        new_out,
        first_bias,
        second_bias,
        new_bias,
        first_vec,
        second_vec,
        new_vec,
    )


def solution(mesh):
    return jax.shard_map(
        shards,
        mesh=mesh,
        in_specs=(
            P("dp", None),
            P("dp", None),
            P(None, "dp", None, "tensor"),
            P(None, "dp", None, "tensor"),
            P(None, "dp", None, "tensor"),
            P(None, None, "tensor", "dp"),
            P(None, None, "tensor", "dp"),
            P(None, None, "tensor", "dp"),
            P(None, None, "tensor"),
            P(None, None, "tensor"),
            P(None, None, "tensor"),
            P(),
            P(),
            P(),
        ),
        out_specs=(
            P(("dp", "tensor"), None),
            P(("dp", "tensor"), None),
            P(None, "dp", None, "tensor"),
            P(None, "dp", None, "tensor"),
            P(None, "dp", None, "tensor"),
            P(None, None, "tensor", "dp"),
            P(None, None, "tensor", "dp"),
            P(None, None, "tensor", "dp"),
            P(None, None, "tensor"),
            P(None, None, "tensor"),
            P(None, None, "tensor"),
            P(),
            P(),
            P(),
        ),
        check_vma=False,
    )
```

profile of v0, /device:TPU:0, one launch (start us, length us, event | category | flops | bytes accessed | tf_op | source)
XLA Modules:
  0.0 542.8 jit_solution(16660682184328722629)
XLA Ops:
  15.8 2.0 subtract_multiply_fusion.1
  17.8 56.1 %all-gather.5.cloned.1.call-done = bf16[1,5,192,768]{2,1,0,3:T(8,128)(2,1)} async-done(((bf16[1,5,192,96]{2,1,0,3:T(8,128)(2,1)}), bf16[1,5,192,768]{2,1,0,3:T(8,128)(2,1)}) %all-gather.5.cloned.1.call-update) | async-done | bytes 1474576 | tf_op jit(solution)/shard_map/all_gather | solution.py:275
  74.0 2.4 slice.262
  78.0 57.8 %all-gather.3.cloned.1.call-done = bf16[1,768,7,192]{3,2,0,1:T(8,128)(2,1)} async-done(((bf16[1,96,7,192]{3,2,0,1:T(8,128)(2,1)}), bf16[1,768,7,192]{3,2,0,1:T(8,128)(2,1)}) %all-gather.3.cloned.1.call-update) | async-done | bytes 2064400 | tf_op jit(solution)/shard_map/all_gather | solution.py:274
  135.8 4.8 copy.62
  160.7 2.0 slice.264
  162.7 3.6 copy.79
  167.5 29.4 %all-reduce.7.cloned.1.call-done = bf16[1024,768]{1,0:T(8,128)(2,1)} async-done(((bf16[1024,768]{1,0:T(8,128)(2,1)}), bf16[1024,768]{1,0:T(8,128)(2,1)}) %all-reduce.7.cloned.1.call-update) | async-done | bytes 1572880 | tf_op jit(solution)/shard_map/psum | solution.py:66
  196.9 2.9 fusion.69
  203.8 4.3 convert_reduce_fusion
  209.3 2.6 convolution_convert_fusion.1
  213.6 5.5 %convolution_convert_fusion.3 = bf16[1024,768]{1,0:T(8,128)(2,1)} fusion(bf16[768,768]{1,0:T(8,128)(2,1)} %bitcast.129, f32[1024,768]{1,0:T(8,128)} %copy-done.76, f32[768]{0:T(1024)} %add.279), kind=kOutput, calls=%fused_computation.54 | convolution fusion | flops 1216610304 | bytes 5901312 | tf_op jit(solution)/shard_map/dot_general | solution.py:37
  219.1 35.9 %all-reduce.9.cloned.1.call-done = bf16[1024,768]{1,0:T(8,128)(2,1)} async-done(((bf16[1024,768]{1,0:T(8,128)(2,1)}), bf16[1024,768]{1,0:T(8,128)(2,1)}) %all-reduce.9.cloned.1.call-update) | async-done | bytes 1572880 | tf_op jit(solution)/shard_map/psum | solution.py:70
  255.0 2.6 multiply_reduce_fusion.6
  257.9 2.5 multiply_convert_fusion.2
  272.9 2.6 convolution_convert_fusion
  276.2 4.4 fusion.64
  282.9 6.0 %copy.76 = f32[1,5,192,768]{2,1,0,3:T(8,128)} copy(f32[1,5,192,768]{3,2,1,0:T(8,128)} %maximum_bitcast_fusion.1) | data formatting | bytes 5898240
  288.9 6.1 %reshape.332 = f32[768,960]{1,0:T(8,128)} reshape(f32[768,1,5,192]{3,2,1,0:T(8,128)} %bitcast.96) | data formatting | bytes 5898240
  295.7 5.3 fusion.56
  301.1 3.5 copy.71
  304.5 4.6 fusion.54
  309.1 2.9 copy.70
  312.1 5.5 %maximum_bitcast_fusion = f32[1,768,7,192]{3,1,2,0:T(8,128)} fusion(f32[768,4,192]{2,0,1:T(8,128)} %copy.71, f32[768,3,192]{2,0,1:T(8,128)} %copy.70), kind=kLoop, calls=%fused_computation.7 | loop fusion | flops 1032192 | bytes 8257536 | tf_op jit(solution)/shard_map/stack | solution.py:304
  325.9 21.6 %psum.46 = f32[1,6,192]{2,0,1:T(1,128)S(1)} all-reduce(f32[1,6,192]{2,0,1:T(1,128)S(1)} %stack.35), channel_id=1, replica_groups=mesh['dp'=8,'tensor'=4] {'dp'}, use_global_device_ids=true, to_apply=%region_23.24 | all-reduce | flops 1152 | bytes 9216 | tf_op jit(solution)/shard_map/psum | solution.py:310
  353.1 2.5 dynamic-slice_reduce_fusion.1
  355.8 38.8 %psum.47 = f32[1,6,768]{2,0,1:T(1,128)S(1)} all-reduce(f32[1,6,768]{2,0,1:T(1,128)S(1)} %stack.43), channel_id=1, replica_groups=mesh['dp'=8,'tensor'=4] {'dp','tensor'}, use_global_device_ids=true, to_apply=%region_30.31 | all-reduce | flops 4608 | bytes 36864 | tf_op jit(solution)/shard_map/psum | solution.py:311
  395.3 2.0 dynamic-slice_add_fusion.1
  397.3 26.1 %reduce-scatter.7.cloned.1.call-done = f32[96,960]{1,0:T(8,128)} async-done(((f32[768,960]{1,0:T(8,128)}), f32[96,960]{1,0:T(8,128)}) %reduce-scatter.7.cloned.1.call-update) | async-done | bytes 368656
  424.9 2.7 multiply_subtract_fusion.1
  427.6 105.0 %reduce-scatter.5.cloned.1.call-done = f32[1,96,7,192]{3,1,2,0:T(8,128)} async-done(((f32[1,768,7,192]{3,1,2,0:T(8,128)}), f32[1,96,7,192]{3,1,2,0:T(8,128)}) %reduce-scatter.5.cloned.1.call-update) | async-done | bytes 516112 | tf_op jit(solution)/shard_map/reduce_scatter | solution.py:307
  532.6 2.9 multiply_subtract_fusion
  (259 shorter events, 70.2 us)
Async XLA Ops:
  7.2 4.6 copy-start.1
  7.2 66.8 %all-gather.5.cloned.1.call-start = ((), (), s32[]{:S(2)}) async-start(), calls=%async_computation.3 | async-start | bytes 3538944 | tf_op jit(solution)/shard_map/all_gather | solution.py:275
  8.5 3.6 copy-start.45
  9.6 126.3 %all-gather.3.cloned.1.call-start = ((), (), s32[]{:S(2)}) async-start(), calls=%async_computation.2 | async-start | bytes 3538944 | tf_op jit(solution)/shard_map/all_gather | solution.py:274
  11.7 185.2 %all-reduce.7.cloned.1.call-start = ((), (), s32[]{:S(2)}) async-start(), calls=%async_computation.4 | async-start | bytes 3145728 | tf_op jit(solution)/shard_map/psum | solution.py:66
  12.7 129.2 %copy-start.54 = (f32[768]{0:T(1024)}, f32[768]{0:T(1024)S(1)}, u32[]{:S(2)}) copy-start(f32[768]{0:T(1024)S(1)} %get-tuple-element.155) | copy-start | bytes 9220
  12.7 129.2 %copy-start.64 = (f32[768]{0:T(1024)}, f32[768]{0:T(1024)S(1)}, u32[]{:S(2)}) copy-start(f32[768]{0:T(1024)S(1)} %get-tuple-element.154) | copy-start | bytes 9220
  12.7 188.3 %copy-start.56 = (f32[768]{0:T(1024)}, f32[768]{0:T(1024)S(1)}, u32[]{:S(2)}) copy-start(f32[768]{0:T(1024)S(1)} %get-tuple-element.151) | copy-start | bytes 9220
  78.0 63.9 %copy-start.5 = (f32[1024,768]{1,0:T(8,128)S(1)}, f32[1024,768]{1,0:T(8,128)}, u32[]{:S(2)}) copy-start(f32[1024,768]{1,0:T(8,128)} %subtract_multiply_fusion.1) | copy-start | bytes 9437188
  143.3 6.5 %copy-start.19 = (bf16[1024,192]{0,1:T(8,128)(2,1)}, bf16[1024,192]{0,1:T(8,128)(2,1)S(1)}, u32[]{:S(2)}) copy-start(bf16[1024,192]{0,1:T(8,128)(2,1)S(1)} %get-tuple-element.177) | copy-start | bytes 1179652
  143.3 3.2 copy-start.22
  152.6 5.6 %copy-start.7 = (f32[1024,768]{1,0:T(8,128)S(1)}, f32[1024,768]{1,0:T(8,128)}, u32[]{:S(2)}) copy-start(f32[1024,768]{1,0:T(8,128)} %param.27) | copy-start | bytes 9437188
  155.3 99.7 %all-reduce.9.cloned.1.call-start = ((), (), s32[]{:S(2)}) async-start(), calls=%async_computation.5 | async-start | bytes 3145728 | tf_op jit(solution)/shard_map/psum | solution.py:70
  160.7 5.6 %copy-start.9 = (bf16[1,768,7,192]{1,3,2,0:T(8,128)(2,1)S(1)}, bf16[1,768,7,192]{1,3,2,0:T(8,128)(2,1)}, u32[]{:S(2)}) copy-start(bf16[1,768,7,192]{1,3,2,0:T(8,128)(2,1)} %copy.62) | copy-start | bytes 6193156
  203.1 5.0 copy-start.76
  211.9 136.9 %all-reduce.11.cloned.1.call-start = ((), (), s32[]{:S(2)}) async-start(), calls=%async_computation.8 | async-start | bytes 6291456 | tf_op jit(solution)/shard_map/psum | solution.py:66
  268.8 3.3 copy-start.30
  275.5 5.1 copy-start.15
  275.5 147.9 %reduce-scatter.7.cloned.1.call-start = ((), (), s32[]{:S(2)}) async-start(), calls=%async_computation.7 | async-start | bytes 3538944
  276.2 4.4 copy-start.11
  295.0 237.5 %reduce-scatter.5.cloned.1.call-start = ((), (), s32[]{:S(2)}) async-start(), calls=%async_computation.6 | async-start | bytes 6193152 | tf_op jit(solution)/shard_map/reduce_scatter | solution.py:307
  301.0 3.5 copy-start.31
  301.0 3.5 copy-start.55
  301.1 3.5 copy-start.65
  319.0 6.7 %copy-start.33 = (bf16[1024,3,64]{0,2,1:T(8,128)(2,1)S(1)}, bf16[1024,3,64]{0,2,1:T(8,128)(2,1)}, u32[]{:S(2)}) copy-start(bf16[1024,3,64]{0,2,1:T(8,128)(2,1)} %copy-done.32) | copy-start | bytes 1179652
  323.2 27.5 %copy-start.49 = (f32[1024]{0:T(1024)S(1)}, f32[1024]{0:T(1024)}, u32[]{:S(2)}) copy-start(f32[1024]{0:T(1024)} %copy-done.48) | copy-start | bytes 12292
  352.9 41.6 %copy-start.46 = (f32[1,6,768]{2,0,1:T(1,128)S(1)}, f32[1,6,768]{2,0,1:T(1,128)}, u32[]{:S(2)}) copy-start(f32[1,6,768]{2,0,1:T(1,128)} %param.37) | copy-start | bytes 55300
  352.9 41.6 %copy-start.61 = (f32[1,6,768]{2,0,1:T(1,128)S(1)}, f32[1,6,768]{2,0,1:T(1,128)}, u32[]{:S(2)}) copy-start(f32[1,6,768]{2,0,1:T(1,128)} %param.39) | copy-start | bytes 55300
  352.9 41.6 %copy-start.62 = (f32[1,6,768]{2,0,1:T(1,128)S(1)}, f32[1,6,768]{2,0,1:T(1,128)}, u32[]{:S(2)}) copy-start(f32[1,6,768]{2,0,1:T(1,128)} %param.38) | copy-start | bytes 55300
  353.0 42.4 %copy-start.63 = (f32[768]{0:T(1024)S(1)}, f32[768]{0:T(1024)}, u32[]{:S(2)}) copy-start(f32[768]{0:T(1024)} %get-tuple-element.156) | copy-start | bytes 9220
  397.3 135.3 %copy-start.18 = (f32[1,96,7,192]{3,1,2,0:T(8,128)S(1)}, f32[1,96,7,192]{3,1,2,0:T(8,128)}, u32[]{:S(2)}) copy-start(f32[1,96,7,192]{3,1,2,0:T(8,128)} %param.28) | copy-start | bytes 1548292
  397.3 135.3 %copy-start.42 = (f32[1,96,7,192]{3,1,2,0:T(8,128)S(1)}, f32[1,96,7,192]{3,1,2,0:T(8,128)}, u32[]{:S(2)}) copy-start(f32[1,96,7,192]{3,1,2,0:T(8,128)} %param.30) | copy-start | bytes 1548292
  (55 other events, 98.3 us)
Sparse Core Ops, SparseCore 0:
  10.8 63.1 all-gather.4
  76.7 59.0 all-gather.2
  155.4 41.4 all-reduce.6
  212.1 42.8 all-reduce.8
  275.6 68.6 all-reduce.10
  347.8 75.5 reduce-scatter.6
  427.0 105.4 reduce-scatter.4
where the time goes:
time: 552 us; the launch traced here: 543 us
  waiting for transfers between devices  310 us (56%)
  blocking collectives  60.4 us (11%)
  local copies, waits for them, and re-layouts  58.6 us (11%)
  other arithmetic  50.2 us (9%)
  matrix products  46.7 us (8%)
  between operations  15.6 us (3%)
    reduce_scatter x1, waiting for transfers between devices, shards(): lax.psum_scatter(summed_in, 'dp', scatter_dimension=1, tiled=True)  105 us
    all_gather x1, waiting for transfers between devices, shards(): lax.all_gather(master_in.astype(jnp.bfloat16), 'dp', axis=1, tiled=True)  57.8 us
    all_gather x1, waiting for transfers between devices, shards(): lax.all_gather(master_out.astype(jnp.bfloat16), 'dp', axis=3, tiled=True)  56.1 us
    psum x1, blocking collectives, shards(): summed_vector = lax.psum(jnp.stack(list_vector), ('dp', 'tensor'))  38.8 us
    psum x1, waiting for transfers between devices, grad_total(): lax.psum(partial_sum.astype(jnp.bfloat16), 'tensor').astype(jnp.float32)  35.9 us
    unnamed x166, local copies, waits for them, and re-layouts  31.2 us
    psum x2, waiting for transfers between devices, branch_total(): lax.psum(partial_sum.astype(jnp.bfloat16), 'tensor').astype(jnp.float32)  29.4 us
    unnamed x8, waiting for transfers between devices  26.2 us
  transfers between devices with their start and end apart: 7, of which 6 were waited for; matrix products, arithmetic and copies ran while one was open for 17% of the time, Pallas kernels for 0%

commit v1 on v0

--- a/solution.py
+++ b/solution.py
@@ -1,6 +1,10 @@
+import functools
+
 import jax
 import jax.numpy as jnp
 from jax import lax
+from jax.experimental import pallas as pl
+from jax.experimental.pallas import tpu as pltpu
 from jax.sharding import PartitionSpec as P
 
 D = 768
@@ -339,9 +343,720 @@
     )
 
 
+MESH_IDS = pl.DeviceIdType.MESH
+F32 = jnp.float32
+BF16 = jnp.bfloat16
+NN = (((1,), (0,)), ((), ()))
+NT = (((1,), (1,)), ((), ()))
+TN = (((0,), (0,)), ((), ()))
+GELU_A = (2.0 / 3.141592653589793) ** 0.5
+GELU_B = 0.044715
+
+
+def mm(left, right, dims=NN):
+    return lax.dot_general(left, right, dims, preferred_element_type=F32)
+
+
+def rows_at(start, size, align):
+    return pl.ds(pl.multiple_of(start, align), size)
+
+
+def block_kernel(
+    sizes,
+    resid_h,
+    cot_h,
+    win,
+    wout,
+    bias,
+    vec,
+    out_o,
+    grad_o,
+    gsum_o,
+    small_o,
+    resid,
+    cot,
+    inv1,
+    normed,
+    dmlp,
+    w,
+    q_s,
+    k_s,
+    v_s,
+    e_s,
+    linv,
+    mixed,
+    ps,
+    crecv,
+    fin,
+    ysend,
+    yrecv,
+    mid,
+    xhat2,
+    inv2,
+    hidden,
+    act_s,
+    dpre,
+    dattn,
+    dk_s,
+    dv_s,
+    dqkv,
+    gmat,
+    xr,
+    zs,
+    zr,
+    sm,
+    smx,
+    smz,
+    smy,
+    smc,
+    lsem,
+    ssem,
+    rsem,
+):
+    tokens, width, quarter, heads, shard = sizes
+    dp = lax.axis_index("dp")
+    ten = lax.axis_index("tensor")
+    z = lax.div(dp, 2)
+    x = lax.rem(dp, 2)
+    y = lax.div(ten, 2)
+    c = lax.rem(ten, 2)
+    x_dev = (dp + 1 - 2 * x, ten)
+    c_dev = (dp, ten + 1 - 2 * c)
+    y_dev = (dp, ten + 2 - 4 * y)
+
+    def z_other(j):
+        if j == 1:
+            return z + 1 - 2 * lax.rem(z, 2)
+        if j == 2:
+            return lax.rem(z + 2, 4)
+        return 3 - z
+
+    def z_dev(j):
+        return (2 * z_other(j) + x, ten)
+
+    def rcopy(src, dst, idx, dev):
+        return pltpu.make_async_remote_copy(
+            src_ref=src,
+            dst_ref=dst,
+            send_sem=ssem.at[idx],
+            recv_sem=rsem.at[idx],
+            device_id=dev,
+            device_id_type=MESH_IDS,
+        )
+
+    barrier = pltpu.get_barrier_semaphore()
+    peers = [x_dev, c_dev, y_dev, z_dev(1), z_dev(2), z_dev(3)]
+    for dev in peers:
+        pl.semaphore_signal(barrier, inc=1, device_id=dev, device_id_type=MESH_IDS)
+    load_resid = pltpu.make_async_copy(resid_h, resid, lsem.at[0])
+    load_cot = pltpu.make_async_copy(cot_h, cot, lsem.at[1])
+    load_resid.start()
+    load_cot.start()
+
+    mine = rows_at(dp * shard, shard, shard)
+    wout_t = [jnp.transpose(wout[i]) for i in range(5)]
+    w[0, mine, :] = jnp.concatenate([win[0], win[1], win[2], wout_t[0]], 1).astype(BF16)
+    w[1, mine, :] = jnp.concatenate([win[3 + i] for i in range(4)], 1).astype(BF16)
+    w[2, mine, :] = jnp.concatenate(wout_t[1:], 1).astype(BF16)
+
+    pl.semaphore_wait(barrier, len(peers))
+
+    def piece(b, owner):
+        return w.at[b, rows_at(owner * shard, shard, shard), :]
+
+    def ag_x(b):
+        return rcopy(piece(b, dp), piece(b, dp), b, x_dev)
+
+    def ag_z(b, j):
+        return rcopy(piece(b, dp), piece(b, dp), 3 + 3 * b + j - 1, z_dev(j))
+
+    def ag_f(b, j):
+        owner = 2 * z_other(j) + x
+        return rcopy(piece(b, owner), piece(b, owner), 12 + 3 * b + j - 1, x_dev)
+
+    def ag_start(b):
+        for j in (1, 2, 3):
+            ag_z(b, j).start()
+        ag_x(b).start()
+
+    def ag_forward(b):
+        for j in (1, 2, 3):
+            ag_z(b, j).wait_recv()
+            ag_f(b, j).start()
+
+    def ag_finish(b):
+        ag_x(b).wait_recv()
+        for j in (1, 2, 3):
+            ag_f(b, j).wait_recv()
+
+    def ag_drain(b):
+        ag_x(b).wait_send()
+        for j in (1, 2, 3):
+            ag_z(b, j).wait_send()
+            ag_f(b, j).wait_send()
+
+    ag_start(0)
+
+    load_resid.wait()
+    load_cot.wait()
+    gain_one, shift_one = vec[0:1, :], vec[1:2, :]
+
+    own = rows_at(ten * quarter, quarter, quarter)
+    mid[...] = resid[own, :]
+    xhat = resid
+
+    def first_norm(r, carry):
+        rows = rows_at(r * 128, 128, 128)
+        part = resid[rows, :]
+        center = part - jnp.mean(part, -1, keepdims=True)
+        inverse = lax.rsqrt(jnp.mean(center * center, -1, keepdims=True) + EPS)
+        scaled = center * inverse
+        xhat[rows, :] = scaled
+        inv1[rows, :] = inverse
+        normed[rows, :] = (scaled * gain_one + shift_one).astype(BF16)
+        dmlp[rows, :] = (cot[rows, :] * BRANCH_SCALE).astype(BF16)
+        return carry
+
+    lax.fori_loop(0, tokens // 128, first_norm, 0)
+    sm[...] = jnp.zeros_like(sm)
+    sm[5:6, :] = jnp.sum(dmlp[own, :].astype(F32), 0, keepdims=True)
+    mixed[...] = jnp.zeros_like(mixed)
+    dqkv[...] = jnp.zeros_like(dqkv)
+
+    ag_forward(0)
+    ag_finish(0)
+    ag_start(1)
+
+    bias_q, bias_v = bias[0:1, :], bias[1:2, :]
+    hc = heads * HD
+
+    def project(r, carry):
+        rows = rows_at(r * 256, 256, 256)
+        got = mm(normed[rows, :], w[0, :, 0:640])
+        queries = (got[:, 0:hc] + bias_q).astype(BF16) * jnp.asarray(HD**-0.5, BF16)
+        key_rows = got[:, hc : 2 * hc].astype(BF16)
+        value_rows = (got[:, 2 * hc : 3 * hc] + bias_v).astype(BF16)
+        for h in range(heads):
+            q_s[h, rows, :] = queries[:, h * HD : (h + 1) * HD]
+            k_s[h, rows, :] = key_rows[:, h * HD : (h + 1) * HD]
+            v_s[h, rows, :] = value_rows[:, h * HD : (h + 1) * HD]
+        return carry
+
+    lax.fori_loop(0, tokens // 256, project, 0)
+
+    def attend(i):
+        first, last = i * quarter, (i + 1) * quarter
+        rows = slice(first, last)
+        causal = lax.broadcasted_iota(jnp.int32, (quarter, quarter), 0) >= lax.broadcasted_iota(
+            jnp.int32, (quarter, quarter), 1
+        )
+        for h in range(heads):
+            queries = q_s[h, rows, :]
+            diag = jnp.where(causal, mm(queries, k_s[h, rows, :], NT), MASKED)
+            highest = jnp.max(diag, -1, keepdims=True)
+            if i > 0:
+                wide = mm(queries, k_s[h, 0:first, :], NT)
+                highest = jnp.maximum(highest, jnp.max(wide, -1, keepdims=True))
+            e_diag = jnp.exp(diag - highest)
+            summed = jnp.sum(e_diag, -1, keepdims=True)
+            e_diag = e_diag.astype(BF16)
+            e_s[h, rows, first:last] = e_diag
+            total = mm(e_diag, v_s[h, rows, :])
+            if i > 0:
+                e_wide = jnp.exp(wide - highest)
+                summed = summed + jnp.sum(e_wide, -1, keepdims=True)
+                e_wide = e_wide.astype(BF16)
+                e_s[h, rows, 0:first] = e_wide
+                total = total + mm(e_wide, v_s[h, 0:first, :])
+            inverse = 1.0 / summed
+            linv[h, rows, :] = inverse
+            mixed[rows, (h + 1) * HD : (h + 2) * HD] = (total * inverse).astype(BF16)
+
+    def rs_order(s, local_first):
+        half = lax.div(s, 2)
+        odd = lax.rem(s, 2)
+        near = half if not local_first else 1 - half
+        yq = near * y + (1 - near) * (1 - y)
+        cq = odd * c + (1 - odd) * (1 - c)
+        return 2 * yq + cq, half, odd, near
+
+    def rs_core(k, half):
+        return rcopy(ps.at[k % 2, half], crecv.at[k, half], 21 + 2 * k + half, c_dev)
+
+    def rs_y(k):
+        return rcopy(ysend.at[k], yrecv.at[k], 29 + k, y_dev)
+
+    def rs_loop(k, compute, local_first=False, start_y=True, prepare=None):
+        if k >= 2:
+            rs_core_drain(k - 2)
+
+        def step(s, carry):
+            which, half, odd, near = rs_order(s, local_first)
+            if prepare is not None:
+                prepare(s)
+            part = compute(which)
+
+            @pl.when(odd == 0)
+            def _():
+                ps[k % 2, half] = part.astype(BF16)
+                rs_core(k, half).start()
+
+            @pl.when(odd == 1)
+            def _():
+                rs_core(k, half).wait_recv()
+                total = part + crecv[k, half].astype(F32)
+
+                @pl.when(near == 0)
+                def _():
+                    ysend[k] = total.astype(BF16)
+                    if start_y:
+                        rs_y(k).start()
+
+                @pl.when(near == 1)
+                def _():
+                    fin[k] = total
+
+            return carry
+
+        lax.fori_loop(0, 4, step, 0)
+
+    def rs_result(k):
+        rs_y(k).wait_recv()
+        return fin[k] + yrecv[k].astype(F32)
+
+    def rs_core_drain(k):
+        for half in range(2):
+            rs_core(k, half).wait_send()
+
+
+    def attend_proj(which):
+        for i in range(tokens // quarter):
+
+            @pl.when(which == i)
+            def _():
+                attend(i)
+
+        return mm(mixed[rows_at(which * quarter, quarter, quarter), :], w[0, :, 512:768], NT)
+
+    rs_loop(0, attend_proj)
+
+    def q_rows(ref, which):
+        return ref.at[rows_at(which * quarter, quarter, quarter), :]
+
+    def qg_y(g, ref):
+        return rcopy(q_rows(ref, ten), q_rows(ref, ten), 33 + g, y_dev)
+
+    def qg_c(g, ref):
+        return rcopy(q_rows(ref, ten), q_rows(ref, ten), 35 + g, c_dev)
+
+    def qg_f(g, ref):
+        far = ten + 2 - 4 * y
+        return rcopy(q_rows(ref, far), q_rows(ref, far), 37 + g, c_dev)
+
+    def qg_drain(g, ref):
+        qg_y(g, ref).wait_send()
+        qg_c(g, ref).wait_send()
+        qg_f(g, ref).wait_send()
+
+    ag_forward(1)
+    ag_start(2)
+
+    mid[...] = mid[...] + BRANCH_SCALE * (rs_result(0) + vec[4:5, :])
+    center = mid[...] - jnp.mean(mid[...], -1, keepdims=True)
+    inverse = lax.rsqrt(jnp.mean(center * center, -1, keepdims=True) + EPS)
+    scaled = center * inverse
+    xhat2[...] = scaled
+    inv2[...] = inverse
+    hidden[own, :] = (scaled * vec[2:3, :] + vec[3:4, :]).astype(BF16)
+    qg_y(0, hidden).start()
+    qg_c(0, hidden).start()
+
+    ag_finish(1)
+    ag_forward(2)
+    ag_finish(2)
+
+    bias_up = jnp.concatenate([bias[2 + i : 3 + i, :] for i in range(4)], 1)
+
+    def wait_hidden(s):
+        @pl.when(s == 0)
+        def _():
+            qg_c(0, hidden).wait_recv()
+
+        @pl.when(s == 2)
+        def _():
+            qg_y(0, hidden).wait_recv()
+            qg_f(0, hidden).start()
+            qg_f(0, hidden).wait_recv()
+
+    def feed_forward(which):
+        rows = rows_at(which * quarter, quarter, quarter)
+        hq = hidden[rows, :]
+        gq = dmlp[rows, :]
+        for t in range(width // 256):
+            cols = slice(t * 256, (t + 1) * 256)
+            pre = mm(hq, w[1, :, cols]) + bias_up[:, cols]
+            square = pre * pre
+            tanh = jnp.tanh(GELU_A * (pre + GELU_B * (square * pre)))
+            half_up = 0.5 + 0.5 * tanh
+            act_s[rows, cols] = (pre * half_up).astype(BF16)
+            slope = half_up + 0.5 * pre * (1.0 - tanh * tanh) * (
+                GELU_A + (3.0 * GELU_A * GELU_B) * square
+            )
+            d_act = mm(gq, w[2, :, cols]).astype(BF16).astype(F32)
+            d_low = (slope * d_act).astype(BF16)
+            dpre[rows, cols] = d_low
+            sm[6:7, cols] = sm[6:7, cols] + jnp.sum(d_low.astype(F32), 0, keepdims=True)
+        return mm(dpre[rows, :], w[1], NT)
+
+    rs_loop(1, feed_forward, local_first=True, prepare=wait_hidden)
+
+    def branch(which):
+        rows = rows_at(which * quarter, quarter, quarter)
+        return mm(act_s[rows, :], w[2], NT)
+
+    rs_loop(2, branch, start_y=False)
+
+    def grad_block(b, left, right):
+        def tile(t, carry):
+            cols = rows_at(t * 256, 256, 256)
+            gmat[b, cols, :] = mm(left[:, cols], right[...], TN).astype(BF16)
+            return carry
+
+        lax.fori_loop(0, width // 256, tile, 0)
+
+    def g_rows(b, owner):
+        return gmat.at[b, rows_at(owner * shard, shard, shard), :]
+
+    def gx(b, zi):
+        return rcopy(g_rows(b, 2 * zi + 1 - x), xr.at[b, zi], 39 + 4 * b + zi, x_dev)
+
+    def gz(b, j):
+        return rcopy(zs.at[b, j - 1], zr.at[b, j - 1], 51 + 3 * b + j - 1, z_dev(j))
+
+    def g_start(b):
+        for zi in range(4):
+            gx(b, zi).start()
+
+    def g_middle(b):
+        for zi in range(4):
+            gx(b, zi).wait_recv()
+        for j in (1, 2, 3):
+            zo = z_other(j)
+            mine_x = gmat[b, rows_at((2 * zo + x) * shard, shard, shard), :].astype(F32)
+            zs[b, j - 1] = (mine_x + xr[b, zo].astype(F32)).astype(BF16)
+            gz(b, j).start()
+
+    def g_finish(b):
+        total = gmat[b, mine, :].astype(F32) + xr[b, z].astype(F32)
+        for j in (1, 2, 3):
+            gz(b, j).wait_recv()
+            total = total + zr[b, j - 1].astype(F32)
+        gsum_o[b] = total
+
+    def g_drain(b):
+        for zi in range(4):
+            gx(b, zi).wait_send()
+        for j in (1, 2, 3):
+            gz(b, j).wait_send()
+
+    grad_block(1, hidden, dpre)
+    g_start(1)
+    grad_block(2, dmlp, act_s)
+    g_start(2)
+
+    d_hidden = rs_result(1)
+    scaled = xhat2[...]
+    sm[2:3, :] = jnp.sum(d_hidden * scaled, 0, keepdims=True)
+    sm[3:4, :] = jnp.sum(d_hidden, 0, keepdims=True)
+    weighted = d_hidden * vec[2:3, :]
+    d_mid = cot[own, :] + inv2[...] * (
+        weighted
+        - jnp.mean(weighted, -1, keepdims=True)
+        - scaled * jnp.mean(weighted * scaled, -1, keepdims=True)
+    )
+    fin[1] = d_mid
+    d_attn = (BRANCH_SCALE * d_mid).astype(BF16)
+    dattn[own, :] = d_attn
+    sm[4:5, :] = jnp.sum(d_attn.astype(F32), 0, keepdims=True)
+    qg_y(1, dattn).start()
+    qg_c(1, dattn).start()
+
+    dk_s[...] = jnp.zeros_like(dk_s)
+    dv_s[...] = jnp.zeros_like(dv_s)
+
+    def attend_back(i):
+        first, last = i * quarter, (i + 1) * quarter
+        rows = slice(first, last)
+        d_mixed = mm(dattn[rows, :], w[0, :, 512:768]).astype(BF16)
+        for h in range(heads):
+            cols = slice((h + 1) * HD, (h + 2) * HD)
+            d_out = d_mixed[:, cols].astype(F32)
+            inverse = linv[h, rows, :]
+            d_scaled = d_out * inverse
+            inner = jnp.sum(d_scaled * mixed[rows, cols].astype(F32), -1, keepdims=True)
+            d_scaled = d_scaled.astype(BF16)
+            expo = e_s[h, rows, 0:last]
+            d_probs = mm(d_scaled, v_s[h, 0:last, :], NT)
+            d_scores = (expo.astype(F32) * (d_probs - inner)).astype(BF16)
+            d_q = mm(d_scores, k_s[h, 0:last, :]) * HD**-0.5
+            dqkv[rows, h * HD : (h + 1) * HD] = d_q.astype(BF16)
+            dk_s[h, 0:last, :] = dk_s[h, 0:last, :] + mm(d_scores, q_s[h, rows, :], TN)
+            dv_s[h, 0:last, :] = dv_s[h, 0:last, :] + mm(expo, d_scaled, TN)
+
+    def back_step(s, carry):
+        half = lax.div(s, 2)
+        odd = lax.rem(s, 2)
+        yq = (1 - half) * y + half * (1 - y)
+        cq = (1 - odd) * c + odd * (1 - c)
+        which = 2 * yq + cq
+
+        @pl.when(s == 1)
+        def _():
+            qg_c(1, dattn).wait_recv()
+
+        @pl.when(s == 2)
+        def _():
+            g_middle(1)
+            qg_y(1, dattn).wait_recv()
+            qg_f(1, dattn).start()
+            rs_y(2).start()
+
+        @pl.when(s == 3)
+        def _():
+            qg_f(1, dattn).wait_recv()
+
+        for i in range(tokens // quarter):
+
+            @pl.when(which == i)
+            def _():
+                attend_back(i)
+
+        return carry
+
+    lax.fori_loop(0, 4, back_step, 0)
+
+    for h in range(heads):
+        dqkv[:, hc + h * HD : hc + (h + 1) * HD] = dk_s[h].astype(BF16)
+        dqkv[:, 2 * hc + h * HD : 2 * hc + (h + 1) * HD] = dv_s[h].astype(BF16)
+
+    def tile_zero(t, carry):
+        cols = rows_at(t * 256, 256, 256)
+        g_qkv = mm(normed[:, cols], dqkv[...], TN)
+        g_proj = mm(dattn[:, cols], mixed[...], TN)
+        gmat[0, cols, 0:512] = g_qkv[:, 0:512].astype(BF16)
+        gmat[0, cols, 512:640] = (g_qkv[:, 512:640] + g_proj[:, 0:128]).astype(BF16)
+        gmat[0, cols, 640:768] = g_proj[:, 128:256].astype(BF16)
+        return carry
+
+    lax.fori_loop(0, width // 256, tile_zero, 0)
+    g_start(0)
+
+    def first_back(which):
+        rows = rows_at(which * quarter, quarter, quarter)
+        d_low = dqkv[rows, :]
+        part = mm(d_low, w[0, :, 0:640], NT)
+        rounded = part.astype(BF16).astype(F32)
+        sm[0:1, :] = sm[0:1, :] + jnp.sum(rounded * xhat[rows, :], 0, keepdims=True)
+        sm[1:2, :] = sm[1:2, :] + jnp.sum(rounded, 0, keepdims=True)
+        sums = jnp.sum(d_low.astype(F32), 0, keepdims=True)
+        sm[7:8, 0:hc] = sm[7:8, 0:hc] + sums[:, 0:hc]
+        sm[7:8, 256 : 256 + hc] = sm[7:8, 256 : 256 + hc] + sums[:, 2 * hc : 3 * hc]
+        return part
+
+    rs_loop(3, first_back)
+
+    small_x = rcopy(sm, smx, 60, x_dev)
+    small_x.start()
+    g_middle(2)
+    g_finish(1)
+    small_x.wait_recv()
+    smz[z] = sm[...] + smx[...]
+
+    def small_z(j):
+        return rcopy(smz.at[z], smz.at[z], 61 + j - 1, z_dev(j))
+
+    for j in (1, 2, 3):
+        small_z(j).start()
+    g_middle(0)
+    out_o[...] = mid[...] + BRANCH_SCALE * (rs_result(2) + vec[5:6, :])
+    for j in (1, 2, 3):
+        rcopy(smz.at[z_other(j)], smz.at[z_other(j)], 61 + j - 1, z_dev(j)).wait_recv()
+    smy[0] = (smz[0] + smz[1]) + (smz[2] + smz[3])
+    small_y = rcopy(smy.at[0], smy.at[1], 64, y_dev)
+    small_y.start()
+    g_finish(2)
+
+    d_normed = rs_result(3)
+    scaled = xhat[own, :]
+    weighted = d_normed * gain_one
+    grad_o[...] = fin[1] + inv1[own, :] * (
+        weighted
+        - jnp.mean(weighted, -1, keepdims=True)
+        - scaled * jnp.mean(weighted * scaled, -1, keepdims=True)
+    )
+    small_y.wait_recv()
+    smc[0] = smy[0] + smy[1]
+    small_c = rcopy(smc.at[0], smc.at[1], 65, c_dev)
+    small_c.start()
+    g_finish(0)
+    small_c.wait_recv()
+    small_o[0:6, :] = smc[0, 0:6, :] + smc[1, 0:6, :]
+    small_o[6:8, :] = smy[0, 6:8, :]
+
+    for b in range(3):
+        ag_drain(b)
+        g_drain(b)
+    for k in range(4):
+        rs_y(k).wait_send()
+    rs_core_drain(2)
+    rs_core_drain(3)
+    qg_drain(0, hidden)
+    qg_drain(1, dattn)
+    small_x.wait_send()
+    for j in (1, 2, 3):
+        small_z(j).wait_send()
+    small_y.wait_send()
+    small_c.wait_send()
+
+
+def run_block(resid, cotangent, win, wout, bias, vec, rows, n_dp):
+    tokens, width = resid.shape
+    quarter = tokens // 4
+    head_cols = win.shape[2]
+    heads = head_cols // HD
+    sizes = (tokens, width, quarter, heads, rows)
+    vm = pltpu.VMEM
+    scratch = [
+        vm((tokens, width), F32),
+        vm((tokens, width), F32),
+        vm((tokens, 1), F32),
+        vm((tokens, width), BF16),
+        vm((tokens, width), BF16),
+        vm((3, width, width), BF16),
+        vm((heads, tokens, HD), BF16),
+        vm((heads, tokens, HD), BF16),
+        vm((heads, tokens, HD), BF16),
+        vm((heads, tokens, tokens), BF16),
+        vm((heads, tokens, 1), F32),
+        vm((tokens, 256), BF16),
+        vm((2, 2, quarter, width), BF16),
+        vm((4, 2, quarter, width), BF16),
+        vm((4, quarter, width), F32),
+        vm((4, quarter, width), BF16),
+        vm((4, quarter, width), BF16),
+        vm((quarter, width), F32),
+        vm((quarter, width), F32),
+        vm((quarter, 1), F32),
+        vm((tokens, width), BF16),
+        vm((tokens, width), BF16),
+        vm((tokens, width), BF16),
+        vm((tokens, width), BF16),
+        vm((heads, tokens, HD), F32),
+        vm((heads, tokens, HD), F32),
+        vm((tokens, 640), BF16),
+        vm((3, width, width), BF16),
+        vm((3, 4, rows, width), BF16),
+        vm((3, 3, rows, width), BF16),
+        vm((3, 3, rows, width), BF16),
+        vm((8, width), F32),
+        vm((8, width), F32),
+        vm((4, 8, width), F32),
+        vm((2, 8, width), F32),
+        vm((2, 8, width), F32),
+        pltpu.SemaphoreType.DMA((2,)),
+        pltpu.SemaphoreType.DMA((66,)),
+        pltpu.SemaphoreType.DMA((66,)),
+    ]
+    whole = pl.BlockSpec(memory_space=pltpu.VMEM)
+    return pl.pallas_call(
+        functools.partial(block_kernel, sizes),
+        out_shape=(
+            jax.ShapeDtypeStruct((quarter, width), F32),
+            jax.ShapeDtypeStruct((quarter, width), F32),
+            jax.ShapeDtypeStruct((3, rows, width), F32),
+            jax.ShapeDtypeStruct((8, width), F32),
+        ),
+        in_specs=[pl.BlockSpec(memory_space=pl.ANY)] * 2 + [whole] * 4,
+        out_specs=[whole] * 4,
+        scratch_shapes=scratch,
+        compiler_params=pltpu.CompilerParams(
+            collective_id=1, has_side_effects=True, vmem_limit_bytes=62 << 20
+        ),
+        name="block",
+    )(resid, cotangent, win, wout, bias, vec)
+
+
+def fused_shards(
+    resid,
+    cotangent,
+    master_in,
+    moment1_in,
+    moment2_in,
+    master_out,
+    moment1_out,
+    moment2_out,
+    master_bias,
+    moment1_bias,
+    moment2_bias,
+    master_vec,
+    moment1_vec,
+    moment2_vec,
+):
+    rows = master_in.shape[1]
+    hc = master_in.shape[3]
+    out_rows, grad_rows, g_sum, small = run_block(
+        resid,
+        cotangent,
+        jnp.transpose(master_in[0], (1, 0, 2)),
+        master_out[0],
+        master_bias[0],
+        master_vec[0],
+        rows,
+        lax.axis_size("dp"),
+    )
+    kinds = g_sum.reshape(3, rows, 4, hc)
+    g_in = jnp.concatenate([kinds[0, :, 0:3], kinds[1]], 1)[None]
+    g_out = jnp.transpose(
+        jnp.concatenate([kinds[0, :, 3:4], kinds[2]], 1), (1, 2, 0)
+    )[None]
+    g_bias = jnp.concatenate(
+        [small[7:8, 0:hc], small[7:8, 256 : 256 + hc], small[6].reshape(4, hc)], 0
+    )[None]
+    g_vec = small[None, 0:6]
+    first_in, second_in, new_in = adam_step(
+        master_in, moment1_in, moment2_in, g_in, 0.5 * D ** (-0.5), DECAY
+    )
+    first_out, second_out, new_out = adam_step(
+        master_out, moment1_out, moment2_out, g_out, 2.0 * D ** (-0.5), DECAY
+    )
+    first_bias, second_bias, new_bias = adam_step(
+        master_bias, moment1_bias, moment2_bias, g_bias, SMALL_RATE, 0.0
+    )
+    first_vec, second_vec, new_vec = adam_step(
+        master_vec, moment1_vec, moment2_vec, g_vec, SMALL_RATE, 0.0
+    )
+    return (
+        out_rows,
+        grad_rows,
+        first_in,
+        second_in,
+        new_in,
+        first_out,
+        second_out,
+        new_out,
+        first_bias,
+        second_bias,
+        new_bias,
+        first_vec,
+        second_vec,
+        new_vec,
+    )
+
+
 def solution(mesh):
+    fused = mesh.shape["dp"] == 8 and mesh.shape["tensor"] == 4
     return jax.shard_map(
-        shards,
+        fused_shards if fused else shards,
         mesh=mesh,
         in_specs=(
             P("dp", None),

time: 552 us -> 149 us (0.27); the launches traced: 543 us -> 149 us
  waiting for transfers between devices: 310 us -> 0 us
  Pallas kernels: 0 us -> 130 us
  blocking collectives: 60.4 us -> 0 us
  local copies, waits for them, and re-layouts: 58.6 us -> 11.2 us
  matrix products: 46.7 us -> 0 us
  other arithmetic: 50.2 us -> 6.28 us
  between operations: 15.6 us -> 0.84 us
    pallas_call x0 -> x1, Pallas kernels: none -> 130 us  [run_block(): pl.pallas_call(functools.partial(block_kernel, sizes), out_shape=(jax.Sha...]
    all_gather x2 -> x0, waiting for transfers between devices: 114 us -> none  [the longest x1 57.8 us: shards(): lax.all_gather(master_in.astype(jnp.bfloat16), 'dp', axis=1, tiled=True)]
    reduce_scatter x1 -> x0, waiting for transfers between devices: 105 us -> none  [shards(): lax.psum_scatter(summed_in, 'dp', scatter_dimension=1, tiled=True)]
    psum x3 -> x0, waiting for transfers between devices: 65.3 us -> none  [the longest x1 35.9 us: grad_total(): lax.psum(partial_sum.astype(jnp.bfloat16), 'tensor').astype(jnp.float32)]
    psum x2 -> x0, blocking collectives: 60.4 us -> none  [the longest x1 38.8 us: shards(): summed_vector = lax.psum(jnp.stack(list_vector), ('dp', 'tensor'))]
    dot_general x24 -> x0, matrix products: 46.7 us -> none  [the longest x4 14.8 us: left_dot(): lax.dot_general(left, right, (((0,), (0,)), ((), ())), preferred_element_...]
    unnamed x8 -> x0, waiting for transfers between devices: 26.2 us -> none
    unnamed x166 -> x35, local copies, waits for them, and re-layouts: 31.2 us -> 6.48 us
  transfers between devices with their start and end apart: 7 -> 0, of which waited for: 6 -> 0; matrix products, arithmetic and copies ran while one was open for 17% -> 0% of each run, Pallas kernels for 0% -> 0%
where the time goes in v1:
time: 149 us
  Pallas kernels  130 us (87%)
  local copies, waits for them, and re-layouts  11.2 us (8%)
  other arithmetic  6.28 us (4%)
    pallas_call x1, Pallas kernels, run_block(): pl.pallas_call(functools.partial(block_kernel, sizes), out_shape=(jax.Sha...  130 us
    unnamed x35, local copies, waits for them, and re-layouts  6.48 us
    sub x4, other arithmetic, adam_step(): return (first_new, second_new, master - rate * (direction + decay * master))  6.28 us

profile of v1, /device:TPU:0, one launch (start us, length us, event | category | flops | bytes accessed | tf_op | source)
XLA Modules:
  0.0 148.5 jit_solution(2754686234004302800)
XLA Ops:
  0.6 1.3 copy.66
  1.9 1.3 copy.65
  3.3 130.2 %block.1 = (f32[256,768]{1,0:T(8,128)}, f32[256,768]{1,0:T(8,128)}, f32[3,96,768]{2,1,0:T(8,128)}, f32[8,768]{1,0:T(8,128)}) custom-call(f32[1024,768]{1,0:T(8,128)} %resid_h.1, f32[1024,768]{1,0:T(8,128)} %cot_h.1, f32[7,96,192]{2,1,0:T(8,128)} %bitcast.40, f32[5,192,96]{2,1,0:T(8,128)} %bitcast.41, f32[6,192]{1,0:T(8,128)} %bitcast.45, f32[6,768]{1,0:T(8,128)} %bitcast.44), custom_call_target="tpu_custom_call" | custom-call | tf_op jit(solution)/shard_map/block/pallas_call | solution.py:971
  133.5 0.0 copy-start.1
  133.5 0.0 copy-start
  133.5 2.1 %reshape.252 = f32[3,96,4,192]{3,2,1,0:T(4,128)S(1)} reshape(f32[3,96,768]{2,1,0:T(8,128)} %get-tuple-element.20) | data formatting | bytes 1769472 | tf_op jit(solution)/shard_map/reshape | solution.py:1017
  135.6 0.1 copy_dynamic-update-slice_fusion.1
  135.7 0.0 copy-done.1
  135.7 0.8 fusion.12
  136.6 1.3 concatenate.57
  137.9 0.1 copy_dynamic-update-slice_fusion
  138.0 0.0 copy-start.2
  138.0 3.0 %multiply_subtract_fusion = (f32[1,96,7,192]{3,1,2,0:T(8,128)}, f32[1,96,7,192]{3,1,2,0:T(8,128)}, f32[1,96,7,192]{3,1,2,0:T(8,128)}) fusion(f32[1,96,7,192]{3,1,2,0:T(8,128)S(1)} %copy-done, f32[1,96,7,192]{3,1,2,0:T(8,128)S(1)} %copy_dynamic-update-slice_fusion, f32[1,96,7,192]{3,1,2,0:T(8,128)} %param.18, f32[1,96,7,192]{3,1,2,0:T(8,128)} %param.17), kind=kLoop, calls=%fused_computation.3 | loop fusion | flops 1935360 | bytes 3612672 | tf_op jit(solution)/shard_map/sub | solution.py:258
  141.0 0.0 copy-start.6
  141.0 0.0 copy-start.9
  141.0 0.0 copy-start.10
  141.0 0.0 copy-done.3
  141.0 0.0 copy-start.4
  141.0 0.2 copy.40
  141.2 0.1 slice.35
  141.3 0.0 copy-start.5
  141.3 0.1 copy.44
  141.4 0.0 copy-done.2
  141.4 2.6 %multiply_subtract_fusion.1 = (f32[1,5,192,96]{3,2,1,0:T(8,128)}, f32[1,5,192,96]{3,2,1,0:T(8,128)}, f32[1,5,192,96]{3,2,1,0:T(8,128)}) fusion(f32[1,5,192,96]{3,2,1,0:T(8,128)S(1)} %copy-done.2, f32[96,4,192]{0,2,1:T(8,128)S(1)} %bitcast.42, f32[96,1,192]{0,2,1:T(8,128)S(1)} %bitcast.43, f32[1,5,192,96]{3,2,1,0:T(8,128)} %param.21, f32[1,5,192,96]{3,2,1,0:T(8,128)} %param.20), kind=kLoop, calls=%fused_computation.9 | loop fusion | flops 1474560 | bytes 2580480 | tf_op jit(solution)/shard_map/sub | solution.py:258
  144.0 0.1 concatenate.64
  144.1 0.0 copy-done.8
  144.2 0.7 multiply_subtract_fusion.2
  144.9 0.6 copy.37
  145.5 0.6 copy.38
  146.1 0.6 copy.39
  146.7 0.9 copy.70
  147.6 0.9 copy.71
  (18 shorter events, 0.1 us)
Async XLA Ops:
  133.5 2.2 %copy-start.1 = (f32[3,96,768]{2,1,0:T(8,128)S(1)}, f32[3,96,768]{2,1,0:T(8,128)}, u32[]{:S(2)}) copy-start(f32[3,96,768]{2,1,0:T(8,128)} %get-tuple-element.20) | copy-start | bytes 2654212
  133.5 4.5 %copy-start = (f32[1,96,7,192]{3,1,2,0:T(8,128)S(1)}, f32[1,96,7,192]{3,1,2,0:T(8,128)}, u32[]{:S(2)}) copy-start(f32[1,96,7,192]{3,1,2,0:T(8,128)} %param.16) | copy-start | bytes 1548292
  136.6 4.4 %copy-start.3 = (f32[1,96,768]{2,1,0:T(8,128)S(1)}, f32[1,96,768]{2,1,0:T(8,128)}, u32[]{:S(2)}) copy-start(f32[1,96,768]{2,1,0:T(8,128)} %get-tuple-element.48) | copy-start | bytes 884740
  138.0 3.5 %copy-start.2 = (f32[1,5,192,96]{3,2,1,0:T(8,128)S(1)}, f32[1,5,192,96]{3,2,1,0:T(8,128)}, u32[]{:S(2)}) copy-start(f32[1,5,192,96]{3,2,1,0:T(8,128)} %param.19) | copy-start | bytes 1105924
  141.0 3.1 %copy-start.7 = (f32[8,768]{1,0:T(8,128)S(1)}, f32[8,768]{1,0:T(8,128)}, u32[]{:S(2)}) copy-start(f32[8,768]{1,0:T(8,128)} %get-tuple-element.21) | copy-start | bytes 73732
  141.0 3.2 %copy-start.8 = (f32[1,6,192]{2,0,1:T(1,128)S(1)}, f32[1,6,192]{2,0,1:T(1,128)}, u32[]{:S(2)}) copy-start(f32[1,6,192]{2,0,1:T(1,128)} %param.22) | copy-start | bytes 13828
  141.0 3.2 %copy-start.11 = (f32[1,6,192]{2,0,1:T(1,128)S(1)}, f32[1,6,192]{2,0,1:T(1,128)}, u32[]{:S(2)}) copy-start(f32[1,6,192]{2,0,1:T(1,128)} %param.24) | copy-start | bytes 13828
  141.0 3.2 %copy-start.12 = (f32[1,6,192]{2,0,1:T(1,128)S(1)}, f32[1,6,192]{2,0,1:T(1,128)}, u32[]{:S(2)}) copy-start(f32[1,6,192]{2,0,1:T(1,128)} %param.23) | copy-start | bytes 13828
  141.0 3.8 %copy-start.6 = (f32[1,6,768]{2,0,1:T(1,128)S(1)}, f32[1,6,768]{2,0,1:T(1,128)}, u32[]{:S(2)}) copy-start(f32[1,6,768]{2,0,1:T(1,128)} %param.25) | copy-start | bytes 55300
  141.0 3.8 %copy-start.9 = (f32[1,6,768]{2,0,1:T(1,128)S(1)}, f32[1,6,768]{2,0,1:T(1,128)}, u32[]{:S(2)}) copy-start(f32[1,6,768]{2,0,1:T(1,128)} %param.27) | copy-start | bytes 55300
  141.0 3.8 %copy-start.10 = (f32[1,6,768]{2,0,1:T(1,128)S(1)}, f32[1,6,768]{2,0,1:T(1,128)}, u32[]{:S(2)}) copy-start(f32[1,6,768]{2,0,1:T(1,128)} %param.26) | copy-start | bytes 55300
  141.0 6.6 %copy-start.4 = (f32[256,768]{1,0:T(8,128)S(1)}, f32[256,768]{1,0:T(8,128)}, u32[]{:S(2)}) copy-start(f32[256,768]{1,0:T(8,128)} %get-tuple-element.67) | copy-start | bytes 2359300
  141.3 5.4 %copy-start.5 = (f32[256,768]{1,0:T(8,128)S(1)}, f32[256,768]{1,0:T(8,128)}, u32[]{:S(2)}) copy-start(f32[256,768]{1,0:T(8,128)} %get-tuple-element.66) | copy-start | bytes 2359300

commit v2 on v1

--- a/solution.py
+++ b/solution.py
@@ -434,12 +434,12 @@
     def z_dev(j):
         return (2 * z_other(j) + x, ten)
 
-    def rcopy(src, dst, idx, dev):
+    def rcopy(src, dst, idx, dev, recv_idx=None):
         return pltpu.make_async_remote_copy(
             src_ref=src,
             dst_ref=dst,
             send_sem=ssem.at[idx],
-            recv_sem=rsem.at[idx],
+            recv_sem=rsem.at[idx if recv_idx is None else recv_idx],
             device_id=dev,
             device_id_type=MESH_IDS,
         )
@@ -454,52 +454,86 @@
     load_cot.start()
 
     mine = rows_at(dp * shard, shard, shard)
-    wout_t = [jnp.transpose(wout[i]) for i in range(5)]
-    w[0, mine, :] = jnp.concatenate([win[0], win[1], win[2], wout_t[0]], 1).astype(BF16)
+    out_t = [jnp.transpose(wout[i]) for i in range(5)]
+    w[0, mine, :] = jnp.concatenate([win[0], win[1], win[2], out_t[0]], 1).astype(BF16)
+
+    pl.semaphore_wait(barrier, len(peers))
+
+    is_end = 1 - lax.rem(lax.div(z + 1, 2), 2)
+    is_mid = 1 - is_end
+    upper = lax.div(z, 2)
+    pair_dev = (2 * z_other(1) + x, ten)
+    mid_dev = (2 * (2 - upper) + x, ten)
+    owner_z = (z_other(1), 2 - upper, 3 - 3 * upper)
+    ag_parts = (2, 1, 1)
+    ag_base = (0, 18, 27)
+
+    def piece(b, zi, p):
+        size = shard // ag_parts[b]
+        return w.at[b, rows_at((2 * zi + x) * shard + p * size, size, size), :]
+
+    def ag_copy(b, zi, p, send, recv, dev):
+        src = piece(b, zi, p)
+        n = ag_parts[b]
+        return rcopy(src, src, ag_base[b] + n * send + p, dev, ag_base[b] + n * recv + p)
+
+    def ag_pair(b, p):
+        return ag_copy(b, z, p, 0, 0, pair_dev)
+
+    def ag_mid(b, p):
+        return ag_copy(b, z, p, 1, 1, mid_dev)
+
+    def ag_onward(b, i, p):
+        if i == 0:
+            return ag_copy(b, owner_z[0], p, 2, 2, mid_dev)
+        return ag_copy(b, owner_z[i], p, 2 + i, i, pair_dev)
+
+    def ag_x(b, i, p):
+        return ag_copy(b, z if i == 0 else owner_z[i - 1], p, 5 + i, 4 + i, x_dev)
+
+    def ag_start(b):
+        for p in range(ag_parts[b]):
+            ag_x(b, 0, p).start()
+            ag_pair(b, p).start()
+
+            @pl.when(is_mid == 1)
+            def _():
+                ag_mid(b, p).start()
+
+    def ag_pump(b, i):
+        for p in range(ag_parts[b]):
+            ag_copy(b, owner_z[i], p, i, i, x_dev).wait_recv()
+
+            @pl.when(is_mid == 1)
+            def _():
+                ag_onward(b, i, p).start()
+
+            ag_x(b, 1 + i, p).start()
+
+    def ag_finish(b):
+        for p in range(ag_parts[b]):
+            for i in range(4):
+                ag_x(b, i, p).wait_recv()
+
+    def ag_drain(b):
+        for p in range(ag_parts[b]):
+            ag_pair(b, p).wait_send()
+            for i in range(4):
+                ag_x(b, i, p).wait_send()
+
+            @pl.when(is_mid == 1)
+            def _():
+                ag_mid(b, p).wait_send()
+                for i in range(3):
+                    ag_onward(b, i, p).wait_send()
+
+    ag_start(0)
     w[1, mine, :] = jnp.concatenate([win[3 + i] for i in range(4)], 1).astype(BF16)
-    w[2, mine, :] = jnp.concatenate(wout_t[1:], 1).astype(BF16)
-
-    pl.semaphore_wait(barrier, len(peers))
-
-    def piece(b, owner):
-        return w.at[b, rows_at(owner * shard, shard, shard), :]
-
-    def ag_x(b):
-        return rcopy(piece(b, dp), piece(b, dp), b, x_dev)
-
-    def ag_z(b, j):
-        return rcopy(piece(b, dp), piece(b, dp), 3 + 3 * b + j - 1, z_dev(j))
-
-    def ag_f(b, j):
-        owner = 2 * z_other(j) + x
-        return rcopy(piece(b, owner), piece(b, owner), 12 + 3 * b + j - 1, x_dev)
-
-    def ag_start(b):
-        for j in (1, 2, 3):
-            ag_z(b, j).start()
-        ag_x(b).start()
-
-    def ag_forward(b):
-        for j in (1, 2, 3):
-            ag_z(b, j).wait_recv()
-            ag_f(b, j).start()
-
-    def ag_finish(b):
-        ag_x(b).wait_recv()
-        for j in (1, 2, 3):
-            ag_f(b, j).wait_recv()
-
-    def ag_drain(b):
-        ag_x(b).wait_send()
-        for j in (1, 2, 3):
-            ag_z(b, j).wait_send()
-            ag_f(b, j).wait_send()
-
-    ag_start(0)
+    w[2, mine, :] = jnp.concatenate(out_t[1:], 1).astype(BF16)
 
     load_resid.wait()
     load_cot.wait()
-    gain_one, shift_one = vec[0:1, :], vec[1:2, :]
+    gain_one, shift_one = vec[0], vec[1]
 
     own = rows_at(ten * quarter, quarter, quarter)
     mid[...] = resid[own, :]
@@ -518,16 +552,18 @@
         return carry
 
     lax.fori_loop(0, tokens // 128, first_norm, 0)
+    ag_pump(0, 0)
     sm[...] = jnp.zeros_like(sm)
     sm[5:6, :] = jnp.sum(dmlp[own, :].astype(F32), 0, keepdims=True)
     mixed[...] = jnp.zeros_like(mixed)
     dqkv[...] = jnp.zeros_like(dqkv)
 
-    ag_forward(0)
+    ag_pump(0, 1)
+    ag_pump(0, 2)
+    ag_start(1)
     ag_finish(0)
-    ag_start(1)
-
-    bias_q, bias_v = bias[0:1, :], bias[1:2, :]
+
+    bias_q, bias_v = bias[0], bias[1]
     hc = heads * HD
 
     def project(r, carry):
@@ -572,26 +608,26 @@
             linv[h, rows, :] = inverse
             mixed[rows, (h + 1) * HD : (h + 2) * HD] = (total * inverse).astype(BF16)
 
-    def rs_order(s, local_first):
+    def rs_order(s):
         half = lax.div(s, 2)
         odd = lax.rem(s, 2)
-        near = half if not local_first else 1 - half
+        near = half
         yq = near * y + (1 - near) * (1 - y)
         cq = odd * c + (1 - odd) * (1 - c)
         return 2 * yq + cq, half, odd, near
 
     def rs_core(k, half):
-        return rcopy(ps.at[k % 2, half], crecv.at[k, half], 21 + 2 * k + half, c_dev)
+        return rcopy(ps.at[k % 2, half], crecv.at[k, half], 36 + 2 * k + half, c_dev)
 
     def rs_y(k):
-        return rcopy(ysend.at[k], yrecv.at[k], 29 + k, y_dev)
-
-    def rs_loop(k, compute, local_first=False, start_y=True, prepare=None):
+        return rcopy(ysend.at[k], yrecv.at[k], 44 + k, y_dev)
+
+    def rs_loop(k, compute, start_y=True, prepare=None):
         if k >= 2:
             rs_core_drain(k - 2)
 
         def step(s, carry):
-            which, half, odd, near = rs_order(s, local_first)
+            which, half, odd, near = rs_order(s)
             if prepare is not None:
                 prepare(s)
             part = compute(which)
@@ -629,6 +665,13 @@
             rs_core(k, half).wait_send()
 
 
+    def pump_up(s):
+        for i in range(3):
+
+            @pl.when(s == 1 + i)
+            def _():
+                ag_pump(1, i)
+
     def attend_proj(which):
         for i in range(tokens // quarter):
 
@@ -638,60 +681,46 @@
 
         return mm(mixed[rows_at(which * quarter, quarter, quarter), :], w[0, :, 512:768], NT)
 
-    rs_loop(0, attend_proj)
+    rs_loop(0, attend_proj, prepare=pump_up)
 
     def q_rows(ref, which):
         return ref.at[rows_at(which * quarter, quarter, quarter), :]
 
     def qg_y(g, ref):
-        return rcopy(q_rows(ref, ten), q_rows(ref, ten), 33 + g, y_dev)
+        return rcopy(q_rows(ref, ten), q_rows(ref, ten), 48 + g, y_dev)
 
     def qg_c(g, ref):
-        return rcopy(q_rows(ref, ten), q_rows(ref, ten), 35 + g, c_dev)
+        return rcopy(q_rows(ref, ten), q_rows(ref, ten), 50 + g, c_dev)
 
     def qg_f(g, ref):
         far = ten + 2 - 4 * y
-        return rcopy(q_rows(ref, far), q_rows(ref, far), 37 + g, c_dev)
+        return rcopy(q_rows(ref, far), q_rows(ref, far), 52 + g, c_dev)
 
     def qg_drain(g, ref):
         qg_y(g, ref).wait_send()
         qg_c(g, ref).wait_send()
         qg_f(g, ref).wait_send()
 
-    ag_forward(1)
     ag_start(2)
 
-    mid[...] = mid[...] + BRANCH_SCALE * (rs_result(0) + vec[4:5, :])
+    mid[...] = mid[...] + BRANCH_SCALE * (rs_result(0) + vec[4])
     center = mid[...] - jnp.mean(mid[...], -1, keepdims=True)
     inverse = lax.rsqrt(jnp.mean(center * center, -1, keepdims=True) + EPS)
     scaled = center * inverse
     xhat2[...] = scaled
     inv2[...] = inverse
-    hidden[own, :] = (scaled * vec[2:3, :] + vec[3:4, :]).astype(BF16)
+    hidden[own, :] = (scaled * vec[2] + vec[3]).astype(BF16)
     qg_y(0, hidden).start()
     qg_c(0, hidden).start()
 
+    ag_pump(2, 0)
     ag_finish(1)
-    ag_forward(2)
-    ag_finish(2)
-
-    bias_up = jnp.concatenate([bias[2 + i : 3 + i, :] for i in range(4)], 1)
-
-    def wait_hidden(s):
-        @pl.when(s == 0)
-        def _():
-            qg_c(0, hidden).wait_recv()
-
-        @pl.when(s == 2)
-        def _():
-            qg_y(0, hidden).wait_recv()
-            qg_f(0, hidden).start()
-            qg_f(0, hidden).wait_recv()
-
-    def feed_forward(which):
+
+    bias_up = jnp.concatenate([bias[2 + i] for i in range(4)], 1)
+
+    def forward_units(which):
         rows = rows_at(which * quarter, quarter, quarter)
         hq = hidden[rows, :]
-        gq = dmlp[rows, :]
         for t in range(width // 256):
             cols = slice(t * 256, (t + 1) * 256)
             pre = mm(hq, w[1, :, cols]) + bias_up[:, cols]
@@ -702,19 +731,31 @@
             slope = half_up + 0.5 * pre * (1.0 - tanh * tanh) * (
                 GELU_A + (3.0 * GELU_A * GELU_B) * square
             )
-            d_act = mm(gq, w[2, :, cols]).astype(BF16).astype(F32)
-            d_low = (slope * d_act).astype(BF16)
-            dpre[rows, cols] = d_low
-            sm[6:7, cols] = sm[6:7, cols] + jnp.sum(d_low.astype(F32), 0, keepdims=True)
-        return mm(dpre[rows, :], w[1], NT)
-
-    rs_loop(1, feed_forward, local_first=True, prepare=wait_hidden)
-
-    def branch(which):
-        rows = rows_at(which * quarter, quarter, quarter)
-        return mm(act_s[rows, :], w[2], NT)
-
-    rs_loop(2, branch, start_y=False)
+            dpre[rows, cols] = slope.astype(BF16)
+
+    def near_units(s, carry):
+        @pl.when(s == 1)
+        def _():
+            qg_c(0, hidden).wait_recv()
+            ag_pump(2, 1)
+
+        forward_units(2 * y + lax.rem(s + c, 2))
+        return carry
+
+    lax.fori_loop(0, 2, near_units, 0)
+    qg_y(0, hidden).wait_recv()
+    qg_f(0, hidden).start()
+    ag_pump(2, 2)
+
+    def far_units(s, carry):
+        @pl.when(s == 1)
+        def _():
+            qg_f(0, hidden).wait_recv()
+
+        forward_units(2 * (1 - y) + lax.rem(s + c, 2))
+        return carry
+
+    lax.fori_loop(0, 2, far_units, 0)
 
     def grad_block(b, left, right):
         def tile(t, carry):
@@ -728,25 +769,24 @@
         return gmat.at[b, rows_at(owner * shard, shard, shard), :]
 
     def gx(b, zi):
-        return rcopy(g_rows(b, 2 * zi + 1 - x), xr.at[b, zi], 39 + 4 * b + zi, x_dev)
+        return rcopy(g_rows(b, 2 * zi + 1 - x), xr.at[b, zi], 54 + 4 * b + zi, x_dev)
 
     def gz(b, j):
-        return rcopy(zs.at[b, j - 1], zr.at[b, j - 1], 51 + 3 * b + j - 1, z_dev(j))
+        return rcopy(zs.at[b, j - 1], zr.at[b, j - 1], 66 + 3 * b + j - 1, z_dev(j))
 
     def g_start(b):
-        for zi in range(4):
-            gx(b, zi).start()
-
-    def g_middle(b):
-        for zi in range(4):
-            gx(b, zi).wait_recv()
-        for j in (1, 2, 3):
-            zo = z_other(j)
-            mine_x = gmat[b, rows_at((2 * zo + x) * shard, shard, shard), :].astype(F32)
-            zs[b, j - 1] = (mine_x + xr[b, zo].astype(F32)).astype(BF16)
-            gz(b, j).start()
+        for j in (3, 2, 1, 0):
+            gx(b, z_other(j) if j else z).start()
+
+    def g_pump(b, j):
+        zo = z_other(j)
+        gx(b, zo).wait_recv()
+        mine_x = gmat[b, rows_at((2 * zo + x) * shard, shard, shard), :].astype(F32)
+        zs[b, j - 1] = (mine_x + xr[b, zo].astype(F32)).astype(BF16)
+        gz(b, j).start()
 
     def g_finish(b):
+        gx(b, z).wait_recv()
         total = gmat[b, mine, :].astype(F32) + xr[b, z].astype(F32)
         for j in (1, 2, 3):
             gz(b, j).wait_recv()
@@ -759,16 +799,40 @@
         for j in (1, 2, 3):
             gz(b, j).wait_send()
 
+    grad_block(2, dmlp, act_s)
+    g_start(2)
+    ag_finish(2)
+
+    def backward_units(which):
+        rows = rows_at(which * quarter, quarter, quarter)
+        gq = dmlp[rows, :]
+        for t in range(width // 256):
+            cols = slice(t * 256, (t + 1) * 256)
+            d_act = mm(gq, w[2, :, cols]).astype(BF16).astype(F32)
+            d_low = (dpre[rows, cols].astype(F32) * d_act).astype(BF16)
+            dpre[rows, cols] = d_low
+            sm[6:7, cols] = sm[6:7, cols] + jnp.sum(d_low.astype(F32), 0, keepdims=True)
+        return mm(dpre[rows, :], w[1], NT)
+
+    rs_loop(1, backward_units)
+    g_pump(2, 3)
     grad_block(1, hidden, dpre)
     g_start(1)
-    grad_block(2, dmlp, act_s)
-    g_start(2)
+    g_pump(2, 2)
+
+    def branch(which):
+        rows = rows_at(which * quarter, quarter, quarter)
+        return mm(act_s[rows, :], w[2], NT)
+
+    rs_loop(2, branch, start_y=False)
+
+    g_pump(2, 1)
 
     d_hidden = rs_result(1)
     scaled = xhat2[...]
     sm[2:3, :] = jnp.sum(d_hidden * scaled, 0, keepdims=True)
     sm[3:4, :] = jnp.sum(d_hidden, 0, keepdims=True)
-    weighted = d_hidden * vec[2:3, :]
+    weighted = d_hidden * vec[2]
     d_mid = cot[own, :] + inv2[...] * (
         weighted
         - jnp.mean(weighted, -1, keepdims=True)
@@ -816,7 +880,8 @@
 
         @pl.when(s == 2)
         def _():
-            g_middle(1)
+            g_pump(1, 3)
+            g_pump(1, 2)
             qg_y(1, dattn).wait_recv()
             qg_f(1, dattn).start()
             rs_y(2).start()
@@ -824,6 +889,7 @@
         @pl.when(s == 3)
         def _():
             qg_f(1, dattn).wait_recv()
+            g_pump(1, 1)
 
         for i in range(tokens // quarter):
 
@@ -839,17 +905,31 @@
         dqkv[:, hc + h * HD : hc + (h + 1) * HD] = dk_s[h].astype(BF16)
         dqkv[:, 2 * hc + h * HD : 2 * hc + (h + 1) * HD] = dv_s[h].astype(BF16)
 
-    def tile_zero(t, carry):
-        cols = rows_at(t * 256, 256, 256)
-        g_qkv = mm(normed[:, cols], dqkv[...], TN)
-        g_proj = mm(dattn[:, cols], mixed[...], TN)
-        gmat[0, cols, 0:512] = g_qkv[:, 0:512].astype(BF16)
-        gmat[0, cols, 512:640] = (g_qkv[:, 512:640] + g_proj[:, 0:128]).astype(BF16)
-        gmat[0, cols, 640:768] = g_proj[:, 128:256].astype(BF16)
-        return carry
-
-    lax.fori_loop(0, width // 256, tile_zero, 0)
-    g_start(0)
+    def zero_rows(zo):
+        def tile(zi):
+            cols = slice(zi * 2 * shard, (zi + 1) * 2 * shard)
+            g_qkv = mm(normed[:, cols], dqkv[...], TN)
+            g_proj = mm(dattn[:, cols], mixed[...], TN)
+            gmat[0, cols, 0:512] = g_qkv[:, 0:512].astype(BF16)
+            gmat[0, cols, 512:640] = (g_qkv[:, 512:640] + g_proj[:, 0:128]).astype(BF16)
+            gmat[0, cols, 640:768] = g_proj[:, 128:256].astype(BF16)
+
+        for zi in range(4):
+
+            @pl.when(zo == zi)
+            def _():
+                tile(zi)
+
+        gx(0, zo).start()
+
+    def zero_pair(first, second):
+        def step(s, carry):
+            zero_rows((1 - s) * first + s * second)
+            return carry
+
+        lax.fori_loop(0, 2, step, 0)
+
+    zero_pair(z_other(3), z_other(2))
 
     def first_back(which):
         rows = rows_at(which * quarter, quarter, quarter)
@@ -865,26 +945,28 @@
 
     rs_loop(3, first_back)
 
-    small_x = rcopy(sm, smx, 60, x_dev)
+    small_x = rcopy(sm, smx, 75, x_dev)
     small_x.start()
-    g_middle(2)
-    g_finish(1)
+    zero_pair(z_other(1), z)
+    g_pump(0, 3)
     small_x.wait_recv()
     smz[z] = sm[...] + smx[...]
 
     def small_z(j):
-        return rcopy(smz.at[z], smz.at[z], 61 + j - 1, z_dev(j))
-
+        return rcopy(smz.at[z], smz.at[z], 76 + j - 1, z_dev(j))
+
+    for j in (3, 2, 1):
+        small_z(j).start()
+    g_pump(0, 2)
+    g_finish(2)
+    g_finish(1)
+    out_o[...] = mid[...] + BRANCH_SCALE * (rs_result(2) + vec[5])
+    g_pump(0, 1)
     for j in (1, 2, 3):
-        small_z(j).start()
-    g_middle(0)
-    out_o[...] = mid[...] + BRANCH_SCALE * (rs_result(2) + vec[5:6, :])
-    for j in (1, 2, 3):
-        rcopy(smz.at[z_other(j)], smz.at[z_other(j)], 61 + j - 1, z_dev(j)).wait_recv()
+        rcopy(smz.at[z_other(j)], smz.at[z_other(j)], 76 + j - 1, z_dev(j)).wait_recv()
     smy[0] = (smz[0] + smz[1]) + (smz[2] + smz[3])
-    small_y = rcopy(smy.at[0], smy.at[1], 64, y_dev)
+    small_y = rcopy(smy.at[0], smy.at[1], 79, y_dev)
     small_y.start()
-    g_finish(2)
 
     d_normed = rs_result(3)
     scaled = xhat[own, :]
@@ -896,7 +978,7 @@
     )
     small_y.wait_recv()
     smc[0] = smy[0] + smy[1]
-    small_c = rcopy(smc.at[0], smc.at[1], 65, c_dev)
+    small_c = rcopy(smc.at[0], smc.at[1], 80, c_dev)
     small_c.start()
     g_finish(0)
     small_c.wait_recv()
@@ -964,8 +1046,8 @@
         vm((2, 8, width), F32),
         vm((2, 8, width), F32),
         pltpu.SemaphoreType.DMA((2,)),
-        pltpu.SemaphoreType.DMA((66,)),
-        pltpu.SemaphoreType.DMA((66,)),
+        pltpu.SemaphoreType.DMA((81,)),
+        pltpu.SemaphoreType.DMA((81,)),
     ]
     whole = pl.BlockSpec(memory_space=pltpu.VMEM)
     return pl.pallas_call(
@@ -986,6 +1068,99 @@
     )(resid, cotangent, win, wout, bias, vec)
 
 
+def adam_kernel(
+    sizes,
+    out_h,
+    grad_h,
+    gsum,
+    small,
+    win,
+    m1_in,
+    m2_in,
+    wout,
+    m1_out,
+    m2_out,
+    wb,
+    m1_b,
+    m2_b,
+    wv,
+    m1_v,
+    m2_v,
+    *refs,
+):
+    out_o, grad_o = refs[0:2]
+    outs = refs[2:14]
+    vin = refs[14:17]
+    vout = refs[17:20]
+    rin = refs[20:23]
+    rout = refs[23:26]
+    sems = refs[26]
+    hc = sizes
+    count = [0]
+
+    def copy(src, dst):
+        made = pltpu.make_async_copy(src, dst, sems.at[count[0]])
+        count[0] += 1
+        made.start()
+        return made
+
+    loads_in = [copy(src, dst) for src, dst in zip((m1_in, m2_in, win), vin)]
+    loads_out = [copy(src, dst) for src, dst in zip((m1_out, m2_out, wout), vout)]
+    done = [copy(out_h, out_o), copy(grad_h, grad_o)]
+    rate_in, rate_out = 0.5 * D ** (-0.5), 2.0 * D ** (-0.5)
+
+    for i in range(6):
+        new = adam_step(wv[i], m1_v[i], m2_v[i], small[i : i + 1, :], SMALL_RATE, 0.0)
+        for ref, value in zip(outs[9:12], new):
+            ref[i] = value
+        at = (7, 0) if i == 0 else (7, 256) if i == 1 else (6, (i - 2) * hc)
+        part = small[at[0] : at[0] + 1, at[1] : at[1] + hc]
+        new = adam_step(wb[i], m1_b[i], m2_b[i], part, SMALL_RATE, 0.0)
+        for ref, value in zip(outs[6:9], new):
+            ref[i] = value
+
+    for load in loads_in:
+        load.wait()
+    for i in range(7):
+        b, at = (0, i * hc) if i < 3 else (1, (i - 3) * hc)
+        new = adam_step(vin[2][i], vin[0][i], vin[1][i], gsum[b, :, at : at + hc], rate_in, DECAY)
+        for ref, value in zip(rin, new):
+            ref[i] = value
+    done += [copy(src, dst) for src, dst in zip(rin, outs[0:3])]
+    for load in loads_out:
+        load.wait()
+    for i in range(5):
+        b, at = (0, 3 * hc) if i < 1 else (2, (i - 1) * hc)
+        part = jnp.transpose(gsum[b, :, at : at + hc])
+        new = adam_step(vout[2][i], vout[0][i], vout[1][i], part, rate_out, DECAY)
+        for ref, value in zip(rout, new):
+            ref[i] = value
+    done += [copy(src, dst) for src, dst in zip(rout, outs[3:6])]
+    for made in done:
+        made.wait()
+
+
+def run_adam(*operands):
+    hc = operands[4].shape[2]
+    shapes = [operands[0], operands[1], *operands[4:16]]
+    hbm = pl.BlockSpec(memory_space=pl.ANY)
+    whole = pl.BlockSpec(memory_space=pltpu.VMEM)
+    big_in, big_out = operands[4].shape, operands[7].shape
+    return pl.pallas_call(
+        functools.partial(adam_kernel, hc),
+        out_shape=[jax.ShapeDtypeStruct(a.shape, F32) for a in shapes],
+        in_specs=[hbm] * 2 + [whole] * 2 + [hbm] * 6 + [whole] * 6,
+        out_specs=[hbm] * 8 + [whole] * 6,
+        scratch_shapes=[pltpu.VMEM(big_in, F32)] * 3
+        + [pltpu.VMEM(big_out, F32)] * 3
+        + [pltpu.VMEM(big_in, F32)] * 3
+        + [pltpu.VMEM(big_out, F32)] * 3
+        + [pltpu.SemaphoreType.DMA((14,))],
+        compiler_params=pltpu.CompilerParams(vmem_limit_bytes=62 << 20),
+        name="adam",
+    )(*operands)
+
+
 def fused_shards(
     resid,
     cotangent,
@@ -1004,52 +1179,21 @@
 ):
     rows = master_in.shape[1]
     hc = master_in.shape[3]
-    out_rows, grad_rows, g_sum, small = run_block(
-        resid,
-        cotangent,
-        jnp.transpose(master_in[0], (1, 0, 2)),
-        master_out[0],
-        master_bias[0],
-        master_vec[0],
-        rows,
-        lax.axis_size("dp"),
-    )
-    kinds = g_sum.reshape(3, rows, 4, hc)
-    g_in = jnp.concatenate([kinds[0, :, 0:3], kinds[1]], 1)[None]
-    g_out = jnp.transpose(
-        jnp.concatenate([kinds[0, :, 3:4], kinds[2]], 1), (1, 2, 0)
-    )[None]
-    g_bias = jnp.concatenate(
-        [small[7:8, 0:hc], small[7:8, 256 : 256 + hc], small[6].reshape(4, hc)], 0
-    )[None]
-    g_vec = small[None, 0:6]
-    first_in, second_in, new_in = adam_step(
-        master_in, moment1_in, moment2_in, g_in, 0.5 * D ** (-0.5), DECAY
-    )
-    first_out, second_out, new_out = adam_step(
-        master_out, moment1_out, moment2_out, g_out, 2.0 * D ** (-0.5), DECAY
-    )
-    first_bias, second_bias, new_bias = adam_step(
-        master_bias, moment1_bias, moment2_bias, g_bias, SMALL_RATE, 0.0
-    )
-    first_vec, second_vec, new_vec = adam_step(
-        master_vec, moment1_vec, moment2_vec, g_vec, SMALL_RATE, 0.0
-    )
+    turned = [jnp.transpose(a[0], (1, 0, 2)) for a in (master_in, moment1_in, moment2_in)]
+    plain = [a[0] for a in (master_out, moment1_out, moment2_out)]
+    biases = [a.reshape(6, 1, hc) for a in (master_bias, moment1_bias, moment2_bias)]
+    vectors = [a.reshape(6, 1, D) for a in (master_vec, moment1_vec, moment2_vec)]
+    sums = run_block(
+        resid, cotangent, turned[0], plain[0], biases[0], vectors[0], rows, lax.axis_size("dp")
+    )
+    new = run_adam(*sums, *turned, *plain, *biases, *vectors)
     return (
-        out_rows,
-        grad_rows,
-        first_in,
-        second_in,
-        new_in,
-        first_out,
-        second_out,
-        new_out,
-        first_bias,
-        second_bias,
-        new_bias,
-        first_vec,
-        second_vec,
-        new_vec,
+        new[0],
+        new[1],
+        *[jnp.transpose(a, (1, 0, 2))[None] for a in new[2:5]],
+        *[a[None] for a in new[5:8]],
+        *[a.reshape(1, 6, hc) for a in new[8:11]],
+        *[a.reshape(1, 6, D) for a in new[11:14]],
     )
 
 

time: 149 us -> 162 us (1.087)
  Pallas kernels: 130 us -> 161 us
  local copies, waits for them, and re-layouts: 11.2 us -> 0 us
  other arithmetic: 6.28 us -> 0 us
    pallas_call x0 -> x1, Pallas kernels: none -> 50.8 us  [run_adam(): pl.pallas_call(functools.partial(adam_kernel, hc), out_shape=[jax.ShapeDt...]
    pallas_call x1, Pallas kernels: 130 us -> 111 us  [run_block(): pl.pallas_call(functools.partial(block_kernel, sizes), out_shape=(jax.Sha...]
    unnamed x35 -> x0, local copies, waits for them, and re-layouts: 6.48 us -> none
    sub x4 -> x0, other arithmetic: 6.28 us -> none  [adam_step(): return (first_new, second_new, master - rate * (direction + decay * master))]
    reshape x1 -> x0, local copies, waits for them, and re-layouts: 2.12 us -> none  [fused_shards(): kinds = g_sum.reshape(3, rows, 4, hc)]
where the time goes in v2:
time: 162 us
  Pallas kernels  161 us (99%)
    pallas_call x1, Pallas kernels, run_block(): pl.pallas_call(functools.partial(block_kernel, sizes), out_shape=(jax.Sha...  111 us
    pallas_call x1, Pallas kernels, run_adam(): pl.pallas_call(functools.partial(adam_kernel, hc), out_shape=[jax.ShapeDt...  50.8 us

profile of v2, /device:TPU:0, one launch (start us, length us, event | category | flops | bytes accessed | tf_op | source)
XLA Modules:
  0.0 162.3 jit_solution(15202813350812932833)
XLA Ops:
  0.6 110.7 %block.1 = (f32[256,768]{1,0:T(8,128)}, f32[256,768]{1,0:T(8,128)}, f32[3,96,768]{2,1,0:T(8,128)}, f32[8,768]{1,0:T(8,128)}) custom-call(f32[1024,768]{1,0:T(8,128)} %resid_h.1, f32[1024,768]{1,0:T(8,128)} %cot_h.1, f32[7,96,192]{2,1,0:T(8,128)} %bitcast.36, f32[5,192,96]{2,1,0:T(8,128)} %bitcast.38, f32[6,1,192]{2,1,0:T(1,128)} %bitcast.46, ...), custom_call_target="tpu_custom_call" | custom-call | tf_op jit(solution)/shard_map/block/pallas_call | solution.py:1053
  111.3 50.8 %adam.1 = (f32[256,768]{1,0:T(8,128)}, f32[256,768]{1,0:T(8,128)}, f32[7,96,192]{2,1,0:T(8,128)}, f32[7,96,192]{2,1,0:T(8,128)}, f32[7,96,192]{2,1,0:T(8,128)}, ...) custom-call(f32[256,768]{1,0:T(8,128)} %get-tuple-element.32.out_h, ...), custom_call_target="tpu_custom_call" | custom-call | tf_op jit(solution)/shard_map/adam/pallas_call | solution.py:1149

commit v3 on v2

--- a/solution.py
+++ b/solution.py
@@ -365,14 +365,16 @@
     sizes,
     resid_h,
     cot_h,
-    win,
-    wout,
+    win_h,
+    wout_h,
     bias,
     vec,
     out_o,
     grad_o,
     gsum_o,
     small_o,
+    win,
+    wout,
     resid,
     cot,
     inv1,
@@ -393,13 +395,16 @@
     mid,
     xhat2,
     inv2,
+    normed_t,
     hidden,
     act_s,
     dpre,
     dattn,
+    dmix,
     dk_s,
     dv_s,
     dqkv,
+    gproj,
     gmat,
     xr,
     zs,
@@ -448,15 +453,24 @@
     peers = [x_dev, c_dev, y_dev, z_dev(1), z_dev(2), z_dev(3)]
     for dev in peers:
         pl.semaphore_signal(barrier, inc=1, device_id=dev, device_id_type=MESH_IDS)
+    load_win = pltpu.make_async_copy(win_h, win, lsem.at[2])
+    load_wout = pltpu.make_async_copy(wout_h, wout, lsem.at[3])
+    load_win.start()
+    load_wout.start()
     load_resid = pltpu.make_async_copy(resid_h, resid, lsem.at[0])
     load_cot = pltpu.make_async_copy(cot_h, cot, lsem.at[1])
     load_resid.start()
     load_cot.start()
 
     mine = rows_at(dp * shard, shard, shard)
+    load_win.wait()
+    load_wout.wait()
     out_t = [jnp.transpose(wout[i]) for i in range(5)]
-    w[0, mine, :] = jnp.concatenate([win[0], win[1], win[2], out_t[0]], 1).astype(BF16)
-
+    by_head = [win[i, :, h * HD : (h + 1) * HD] for h in range(heads) for i in range(3)]
+    w[0, mine, :] = jnp.concatenate([*by_head, out_t[0]], 1).astype(BF16)
+
+    w[1, mine, :] = jnp.concatenate([win[3 + i] for i in range(4)], 1).astype(BF16)
+    w[2, mine, :] = jnp.concatenate(out_t[1:], 1).astype(BF16)
     pl.semaphore_wait(barrier, len(peers))
 
     is_end = 1 - lax.rem(lax.div(z + 1, 2), 2)
@@ -491,23 +505,32 @@
     def ag_x(b, i, p):
         return ag_copy(b, z if i == 0 else owner_z[i - 1], p, 5 + i, 4 + i, x_dev)
 
-    def ag_start(b):
+    def ag_start_x(b):
         for p in range(ag_parts[b]):
             ag_x(b, 0, p).start()
+
+    def ag_start_z(b):
+        for p in range(ag_parts[b]):
             ag_pair(b, p).start()
 
             @pl.when(is_mid == 1)
             def _():
                 ag_mid(b, p).start()
 
-    def ag_pump(b, i):
-        for p in range(ag_parts[b]):
-            ag_copy(b, owner_z[i], p, i, i, x_dev).wait_recv()
-
-            @pl.when(is_mid == 1)
-            def _():
-                ag_onward(b, i, p).start()
-
+    def ag_arrive(b, i, p):
+        ag_copy(b, owner_z[i], p, i, i, x_dev).wait_recv()
+
+    def pump_end(b, i, p=0):
+        @pl.when(is_end == 1)
+        def _():
+            ag_arrive(b, i, p)
+            ag_x(b, 1 + i, p).start()
+
+    def pump_mid(b, i, p=0):
+        @pl.when(is_mid == 1)
+        def _():
+            ag_arrive(b, i, p)
+            ag_onward(b, i, p).start()
             ag_x(b, 1 + i, p).start()
 
     def ag_finish(b):
@@ -527,9 +550,13 @@
                 for i in range(3):
                     ag_onward(b, i, p).wait_send()
 
-    ag_start(0)
-    w[1, mine, :] = jnp.concatenate([win[3 + i] for i in range(4)], 1).astype(BF16)
-    w[2, mine, :] = jnp.concatenate(out_t[1:], 1).astype(BF16)
+    ag_start_x(0)
+    ag_start_z(0)
+
+    @pl.when(is_end == 1)
+    def _():
+        for b in (1, 2):
+            ag_pair(b, 0).start()
 
     load_resid.wait()
     load_cot.wait()
@@ -552,33 +579,53 @@
         return carry
 
     lax.fori_loop(0, tokens // 128, first_norm, 0)
-    ag_pump(0, 0)
+    for i, p in ((0, 0), (1, 0), (0, 1), (1, 1), (2, 0), (2, 1)):
+        pump_mid(0, i, p)
+    for i, p in ((0, 0), (0, 1), (1, 0), (1, 1), (2, 0), (2, 1)):
+        pump_end(0, i, p)
     sm[...] = jnp.zeros_like(sm)
     sm[5:6, :] = jnp.sum(dmlp[own, :].astype(F32), 0, keepdims=True)
     mixed[...] = jnp.zeros_like(mixed)
     dqkv[...] = jnp.zeros_like(dqkv)
 
-    ag_pump(0, 1)
-    ag_pump(0, 2)
-    ag_start(1)
+    ag_start_x(1)
+    ag_start_x(2)
+
+    @pl.when(is_mid == 1)
+    def _():
+        ag_start_z(1)
+
+    for i in range(3):
+        pump_mid(1, i)
+
+    @pl.when(is_mid == 1)
+    def _():
+        ag_start_z(2)
+
+    pump_mid(2, 0)
     ag_finish(0)
-
-    bias_q, bias_v = bias[0], bias[1]
+    pump_end(1, 0)
+
     hc = heads * HD
+    no_bias = jnp.zeros((1, HD), F32)
+    bias_qkv = []
+    for h in range(heads):
+        at = slice(h * HD, (h + 1) * HD)
+        bias_qkv += [bias[0, :, at], no_bias, bias[1, :, at]]
+    bias_qkv = jnp.concatenate([*bias_qkv, no_bias], 1)
 
     def project(r, carry):
         rows = rows_at(r * 256, 256, 256)
-        got = mm(normed[rows, :], w[0, :, 0:640])
-        queries = (got[:, 0:hc] + bias_q).astype(BF16) * jnp.asarray(HD**-0.5, BF16)
-        key_rows = got[:, hc : 2 * hc].astype(BF16)
-        value_rows = (got[:, 2 * hc : 3 * hc] + bias_v).astype(BF16)
+        got = (mm(normed[rows, :], w[0, :, 0:640]) + bias_qkv).astype(BF16)
         for h in range(heads):
-            q_s[h, rows, :] = queries[:, h * HD : (h + 1) * HD]
-            k_s[h, rows, :] = key_rows[:, h * HD : (h + 1) * HD]
-            v_s[h, rows, :] = value_rows[:, h * HD : (h + 1) * HD]
+            at = 3 * h * HD
+            q_s[h, rows, :] = got[:, at : at + HD] * jnp.asarray(HD**-0.5, BF16)
+            k_s[h, rows, :] = got[:, at + HD : at + 2 * HD]
+            v_s[h, rows, :] = got[:, at + 2 * HD : at + 3 * HD]
         return carry
 
     lax.fori_loop(0, tokens // 256, project, 0)
+    pump_end(1, 1)
 
     def attend(i):
         first, last = i * quarter, (i + 1) * quarter
@@ -608,69 +655,67 @@
             linv[h, rows, :] = inverse
             mixed[rows, (h + 1) * HD : (h + 2) * HD] = (total * inverse).astype(BF16)
 
-    def rs_order(s):
-        half = lax.div(s, 2)
-        odd = lax.rem(s, 2)
-        near = half
-        yq = near * y + (1 - near) * (1 - y)
-        cq = odd * c + (1 - odd) * (1 - c)
-        return 2 * yq + cq, half, odd, near
-
     def rs_core(k, half):
         return rcopy(ps.at[k % 2, half], crecv.at[k, half], 36 + 2 * k + half, c_dev)
 
     def rs_y(k):
         return rcopy(ysend.at[k], yrecv.at[k], 44 + k, y_dev)
 
-    def rs_loop(k, compute, start_y=True, prepare=None):
+    def rs_pair(k, near, compute, start_y=True, prepare=None, filler=None):
+        half = 1 if near else 0
         if k >= 2:
-            rs_core_drain(k - 2)
+            rs_core(k - 2, half).wait_send()
 
         def step(s, carry):
-            which, half, odd, near = rs_order(s)
+            yq = y if near else 1 - y
             if prepare is not None:
                 prepare(s)
-            part = compute(which)
-
-            @pl.when(odd == 0)
+            part = compute(2 * yq + lax.rem(1 - s + c, 2))
+
+            @pl.when(s == 0)
             def _():
                 ps[k % 2, half] = part.astype(BF16)
                 rs_core(k, half).start()
 
-            @pl.when(odd == 1)
+            @pl.when(s == 1)
             def _():
+                if filler is not None:
+                    fin[(k + 1) % 3] = part
+                    filler()
+                    kept = fin[(k + 1) % 3]
+                else:
+                    kept = part
                 rs_core(k, half).wait_recv()
-                total = part + crecv[k, half].astype(F32)
-
-                @pl.when(near == 0)
-                def _():
+                total = kept + crecv[k, half].astype(F32)
+                if near:
+                    fin[k % 3] = total
+                else:
                     ysend[k] = total.astype(BF16)
                     if start_y:
                         rs_y(k).start()
 
-                @pl.when(near == 1)
-                def _():
-                    fin[k] = total
-
             return carry
 
-        lax.fori_loop(0, 4, step, 0)
+        lax.fori_loop(0, 2, step, 0)
 
     def rs_result(k):
         rs_y(k).wait_recv()
-        return fin[k] + yrecv[k].astype(F32)
-
-    def rs_core_drain(k):
-        for half in range(2):
-            rs_core(k, half).wait_send()
-
-
-    def pump_up(s):
-        for i in range(3):
-
-            @pl.when(s == 1 + i)
-            def _():
-                ag_pump(1, i)
+        return fin[k % 3] + yrecv[k].astype(F32)
+
+    def pump_far(s):
+        @pl.when(s == 1)
+        def _():
+            pump_end(1, 2)
+            pump_mid(2, 1)
+
+    def pump_near(s):
+        @pl.when(s == 0)
+        def _():
+            pump_mid(2, 2)
+
+        @pl.when(s == 1)
+        def _():
+            pump_end(2, 0)
 
     def attend_proj(which):
         for i in range(tokens // quarter):
@@ -681,7 +726,8 @@
 
         return mm(mixed[rows_at(which * quarter, quarter, quarter), :], w[0, :, 512:768], NT)
 
-    rs_loop(0, attend_proj, prepare=pump_up)
+    rs_pair(0, False, attend_proj, prepare=pump_far)
+    rs_pair(0, True, attend_proj, prepare=pump_near)
 
     def q_rows(ref, which):
         return ref.at[rows_at(which * quarter, quarter, quarter), :]
@@ -701,7 +747,7 @@
         qg_c(g, ref).wait_send()
         qg_f(g, ref).wait_send()
 
-    ag_start(2)
+    pump_end(2, 1)
 
     mid[...] = mid[...] + BRANCH_SCALE * (rs_result(0) + vec[4])
     center = mid[...] - jnp.mean(mid[...], -1, keepdims=True)
@@ -713,7 +759,6 @@
     qg_y(0, hidden).start()
     qg_c(0, hidden).start()
 
-    ag_pump(2, 0)
     ag_finish(1)
 
     bias_up = jnp.concatenate([bias[2 + i] for i in range(4)], 1)
@@ -733,75 +778,66 @@
             )
             dpre[rows, cols] = slope.astype(BF16)
 
-    def near_units(s, carry):
-        @pl.when(s == 1)
-        def _():
-            qg_c(0, hidden).wait_recv()
-            ag_pump(2, 1)
-
-        forward_units(2 * y + lax.rem(s + c, 2))
-        return carry
-
-    lax.fori_loop(0, 2, near_units, 0)
-    qg_y(0, hidden).wait_recv()
-    qg_f(0, hidden).start()
-    ag_pump(2, 2)
-
-    def far_units(s, carry):
-        @pl.when(s == 1)
-        def _():
-            qg_f(0, hidden).wait_recv()
-
-        forward_units(2 * (1 - y) + lax.rem(s + c, 2))
-        return carry
-
-    lax.fori_loop(0, 2, far_units, 0)
-
-    def grad_block(b, left, right):
+    units = (
+        (0, slice(0, 384)),
+        (0, slice(384, 768)),
+        (1, slice(0, 768)),
+        (2, slice(0, 768)),
+    )
+
+    def grad_block(b, left, right, near):
+        rows = rows_at((y if near else 1 - y) * 2 * quarter, 2 * quarter, 2 * quarter)
+
         def tile(t, carry):
             cols = rows_at(t * 256, 256, 256)
-            gmat[b, cols, :] = mm(left[:, cols], right[...], TN).astype(BF16)
+            part = mm(left[rows, cols], right[rows, :], TN)
+            if not near:
+                part = part + gmat[b, cols, :].astype(F32)
+            gmat[b, cols, :] = part.astype(BF16)
             return carry
 
         lax.fori_loop(0, width // 256, tile, 0)
 
-    def g_rows(b, owner):
-        return gmat.at[b, rows_at(owner * shard, shard, shard), :]
-
-    def gx(b, zi):
-        return rcopy(g_rows(b, 2 * zi + 1 - x), xr.at[b, zi], 54 + 4 * b + zi, x_dev)
-
-    def gz(b, j):
-        return rcopy(zs.at[b, j - 1], zr.at[b, j - 1], 66 + 3 * b + j - 1, z_dev(j))
-
-    def g_start(b):
+    def g_rows(u, owner):
+        b, cols = units[u]
+        return gmat.at[b, rows_at(owner * shard, shard, shard), cols]
+
+    def gx(u, zi):
+        b, cols = units[u]
+        return rcopy(g_rows(u, 2 * zi + 1 - x), xr.at[b, zi, :, cols], 54 + 4 * u + zi, x_dev)
+
+    def gz(u, j):
+        b, cols = units[u]
+        return rcopy(
+            zs.at[b, j - 1, :, cols], zr.at[b, j - 1, :, cols], 70 + 3 * u + j - 1, z_dev(j)
+        )
+
+    def g_start(u):
         for j in (3, 2, 1, 0):
-            gx(b, z_other(j) if j else z).start()
-
-    def g_pump(b, j):
+            gx(u, z_other(j) if j else z).start()
+
+    def g_pump(u, j):
+        b, cols = units[u]
         zo = z_other(j)
-        gx(b, zo).wait_recv()
-        mine_x = gmat[b, rows_at((2 * zo + x) * shard, shard, shard), :].astype(F32)
-        zs[b, j - 1] = (mine_x + xr[b, zo].astype(F32)).astype(BF16)
-        gz(b, j).start()
-
-    def g_finish(b):
-        gx(b, z).wait_recv()
-        total = gmat[b, mine, :].astype(F32) + xr[b, z].astype(F32)
+        gx(u, zo).wait_recv()
+        mine_x = gmat[b, rows_at((2 * zo + x) * shard, shard, shard), cols].astype(F32)
+        zs[b, j - 1, :, cols] = (mine_x + xr[b, zo, :, cols].astype(F32)).astype(BF16)
+        gz(u, j).start()
+
+    def g_finish(u):
+        b, cols = units[u]
+        gx(u, z).wait_recv()
+        total = gmat[b, mine, cols].astype(F32) + xr[b, z, :, cols].astype(F32)
         for j in (1, 2, 3):
-            gz(b, j).wait_recv()
-            total = total + zr[b, j - 1].astype(F32)
-        gsum_o[b] = total
-
-    def g_drain(b):
+            gz(u, j).wait_recv()
+            total = total + zr[b, j - 1, :, cols].astype(F32)
+        gsum_o[b, :, cols] = total
+
+    def g_drain(u):
         for zi in range(4):
-            gx(b, zi).wait_send()
+            gx(u, zi).wait_send()
         for j in (1, 2, 3):
-            gz(b, j).wait_send()
-
-    grad_block(2, dmlp, act_s)
-    g_start(2)
-    ag_finish(2)
+            gz(u, j).wait_send()
 
     def backward_units(which):
         rows = rows_at(which * quarter, quarter, quarter)
@@ -814,19 +850,51 @@
             sm[6:7, cols] = sm[6:7, cols] + jnp.sum(d_low.astype(F32), 0, keepdims=True)
         return mm(dpre[rows, :], w[1], NT)
 
-    rs_loop(1, backward_units)
-    g_pump(2, 3)
-    grad_block(1, hidden, dpre)
-    g_start(1)
-    g_pump(2, 2)
-
     def branch(which):
         rows = rows_at(which * quarter, quarter, quarter)
         return mm(act_s[rows, :], w[2], NT)
 
-    rs_loop(2, branch, start_y=False)
-
-    g_pump(2, 1)
+    def near_units(s, carry):
+        @pl.when(s == 1)
+        def _():
+            qg_c(0, hidden).wait_recv()
+
+        forward_units(2 * y + lax.rem(s + c, 2))
+        return carry
+
+    lax.fori_loop(0, 2, near_units, 0)
+    pump_end(2, 2)
+    grad_block(2, dmlp, act_s, True)
+    for t in range(width // 256):
+        cols = slice(t * 256, (t + 1) * 256)
+        normed_t[cols, :] = jnp.transpose(normed[:, cols])
+    ag_finish(2)
+    rs_pair(1, True, backward_units)
+    grad_block(1, hidden, dpre, True)
+    qg_y(0, hidden).wait_recv()
+    qg_f(0, hidden).start()
+
+    def far_units(s, carry):
+        @pl.when(s == 1)
+        def _():
+            qg_f(0, hidden).wait_recv()
+
+        forward_units(2 * (1 - y) + lax.rem(s + c, 2))
+        return carry
+
+    def down_gradient():
+        grad_block(2, dmlp, act_s, False)
+        g_start(3)
+
+    lax.fori_loop(0, 2, far_units, 0)
+    rs_pair(1, False, backward_units, filler=down_gradient)
+    grad_block(1, hidden, dpre, False)
+    g_start(2)
+    rs_pair(2, False, branch, start_y=False)
+    g_pump(3, 3)
+    rs_pair(2, True, branch)
+    g_pump(3, 2)
+    g_pump(3, 1)
 
     d_hidden = rs_result(1)
     scaled = xhat2[...]
@@ -848,13 +916,12 @@
     dk_s[...] = jnp.zeros_like(dk_s)
     dv_s[...] = jnp.zeros_like(dv_s)
 
-    def attend_back(i):
+    def attend_back(i, which_heads):
         first, last = i * quarter, (i + 1) * quarter
         rows = slice(first, last)
-        d_mixed = mm(dattn[rows, :], w[0, :, 512:768]).astype(BF16)
-        for h in range(heads):
+        for h in which_heads:
             cols = slice((h + 1) * HD, (h + 2) * HD)
-            d_out = d_mixed[:, cols].astype(F32)
+            d_out = dmix[rows, cols].astype(F32)
             inverse = linv[h, rows, :]
             d_scaled = d_out * inverse
             inner = jnp.sum(d_scaled * mixed[rows, cols].astype(F32), -1, keepdims=True)
@@ -863,73 +930,83 @@
             d_probs = mm(d_scaled, v_s[h, 0:last, :], NT)
             d_scores = (expo.astype(F32) * (d_probs - inner)).astype(BF16)
             d_q = mm(d_scores, k_s[h, 0:last, :]) * HD**-0.5
-            dqkv[rows, h * HD : (h + 1) * HD] = d_q.astype(BF16)
-            dk_s[h, 0:last, :] = dk_s[h, 0:last, :] + mm(d_scores, q_s[h, rows, :], TN)
-            dv_s[h, 0:last, :] = dv_s[h, 0:last, :] + mm(expo, d_scaled, TN)
-
-    def back_step(s, carry):
-        half = lax.div(s, 2)
-        odd = lax.rem(s, 2)
-        yq = (1 - half) * y + half * (1 - y)
-        cq = (1 - odd) * c + odd * (1 - c)
-        which = 2 * yq + cq
-
+            dqkv[rows, 3 * h * HD : (3 * h + 1) * HD] = d_q.astype(BF16)
+            dk_s[h, :, 0:last] = dk_s[h, :, 0:last] + mm(q_s[h, rows, :], d_scores, TN)
+            dv_s[h, :, 0:last] = dv_s[h, :, 0:last] + mm(d_scaled, expo, TN)
+
+    def back_quarters(near, which_heads, fresh, prepare=None):
+        def step(s, carry):
+            if prepare is not None:
+                prepare(s)
+            yq = y if near else 1 - y
+            which = 2 * yq + lax.rem(s + c, 2)
+            if fresh:
+                rows = rows_at(which * quarter, quarter, quarter)
+                dmix[rows, :] = mm(dattn[rows, :], w[0, :, 512:768]).astype(BF16)
+            for i in range(tokens // quarter):
+
+                @pl.when(which == i)
+                def _():
+                    attend_back(i, which_heads)
+
+            return carry
+
+        lax.fori_loop(0, 2, step, 0)
+
+    def near_ready(s):
         @pl.when(s == 1)
         def _():
             qg_c(1, dattn).wait_recv()
 
-        @pl.when(s == 2)
-        def _():
-            g_pump(1, 3)
-            g_pump(1, 2)
-            qg_y(1, dattn).wait_recv()
-            qg_f(1, dattn).start()
-            rs_y(2).start()
-
-        @pl.when(s == 3)
+    def far_ready(s):
+        @pl.when(s == 1)
         def _():
             qg_f(1, dattn).wait_recv()
-            g_pump(1, 1)
-
-        for i in range(tokens // quarter):
-
-            @pl.when(which == i)
-            def _():
-                attend_back(i)
-
-        return carry
-
-    lax.fori_loop(0, 4, back_step, 0)
-
-    for h in range(heads):
-        dqkv[:, hc + h * HD : hc + (h + 1) * HD] = dk_s[h].astype(BF16)
-        dqkv[:, 2 * hc + h * HD : 2 * hc + (h + 1) * HD] = dv_s[h].astype(BF16)
-
-    def zero_rows(zo):
-        def tile(zi):
-            cols = slice(zi * 2 * shard, (zi + 1) * 2 * shard)
-            g_qkv = mm(normed[:, cols], dqkv[...], TN)
-            g_proj = mm(dattn[:, cols], mixed[...], TN)
-            gmat[0, cols, 0:512] = g_qkv[:, 0:512].astype(BF16)
-            gmat[0, cols, 512:640] = (g_qkv[:, 512:640] + g_proj[:, 0:128]).astype(BF16)
+
+    def keys_values(which_heads):
+        for h in which_heads:
+            at = 3 * h * HD
+            dqkv[:, at + HD : at + 2 * HD] = jnp.transpose(dk_s[h]).astype(BF16)
+            dqkv[:, at + 2 * HD : at + 3 * HD] = jnp.transpose(dv_s[h]).astype(BF16)
+
+    def zero_rows(u, zo):
+        cols = rows_at(zo * 2 * shard, 2 * shard, 2 * shard)
+        left = normed_t[cols, :]
+        if u == 0:
+            gmat[0, cols, 0:384] = mm(left, dqkv[:, 0:384]).astype(BF16)
+        else:
+            g_qkv = mm(left, dqkv[:, 384:640])
+            g_proj = gproj[cols, :]
+            gmat[0, cols, 384:512] = g_qkv[:, 0:128].astype(BF16)
+            gmat[0, cols, 512:640] = (g_qkv[:, 128:256] + g_proj[:, 0:128]).astype(BF16)
             gmat[0, cols, 640:768] = g_proj[:, 128:256].astype(BF16)
-
-        for zi in range(4):
-
-            @pl.when(zo == zi)
-            def _():
-                tile(zi)
-
-        gx(0, zo).start()
-
-    def zero_pair(first, second):
+        gx(u, zo).start()
+
+    def zero_unit(u):
         def step(s, carry):
-            zero_rows((1 - s) * first + s * second)
+            odd, half = lax.rem(s, 2), lax.div(s, 2)
+            early = (1 - odd) * z_other(3) + odd * z_other(2)
+            late = (1 - odd) * z_other(1) + odd * z
+            zero_rows(u, (1 - half) * early + half * late)
             return carry
 
-        lax.fori_loop(0, 2, step, 0)
-
-    zero_pair(z_other(3), z_other(2))
+        lax.fori_loop(0, 4, step, 0)
+
+    back_quarters(True, (0, 1, 2), True, near_ready)
+    g_pump(2, 3)
+    g_pump(2, 2)
+    qg_y(1, dattn).wait_recv()
+    qg_f(1, dattn).start()
+    rs_y(2).start()
+    back_quarters(False, (0, 1), True, far_ready)
+    keys_values((0, 1))
+    zero_unit(0)
+    gproj[...] = jnp.transpose(mm(mixed[...], dattn[...], TN))
+
+    g_pump(2, 1)
+    back_quarters(False, (2,), False)
+    keys_values((2,))
+    g_pump(0, 3)
 
     def first_back(which):
         rows = rows_at(which * quarter, quarter, quarter)
@@ -938,36 +1015,30 @@
         rounded = part.astype(BF16).astype(F32)
         sm[0:1, :] = sm[0:1, :] + jnp.sum(rounded * xhat[rows, :], 0, keepdims=True)
         sm[1:2, :] = sm[1:2, :] + jnp.sum(rounded, 0, keepdims=True)
-        sums = jnp.sum(d_low.astype(F32), 0, keepdims=True)
-        sm[7:8, 0:hc] = sm[7:8, 0:hc] + sums[:, 0:hc]
-        sm[7:8, 256 : 256 + hc] = sm[7:8, 256 : 256 + hc] + sums[:, 2 * hc : 3 * hc]
+        sm[7:8, 0:640] = sm[7:8, 0:640] + jnp.sum(d_low.astype(F32), 0, keepdims=True)
         return part
 
-    rs_loop(3, first_back)
-
-    small_x = rcopy(sm, smx, 75, x_dev)
+    rs_pair(3, False, first_back)
+    rs_pair(3, True, first_back)
+
+    small_x = rcopy(sm, smx, 82, x_dev)
     small_x.start()
-    zero_pair(z_other(1), z)
-    g_pump(0, 3)
+    g_pump(0, 2)
+    zero_unit(1)
+    g_pump(0, 1)
     small_x.wait_recv()
     smz[z] = sm[...] + smx[...]
 
     def small_z(j):
-        return rcopy(smz.at[z], smz.at[z], 76 + j - 1, z_dev(j))
+        return rcopy(smz.at[z], smz.at[z], 83 + j - 1, z_dev(j))
 
     for j in (3, 2, 1):
         small_z(j).start()
-    g_pump(0, 2)
+    g_finish(3)
     g_finish(2)
-    g_finish(1)
     out_o[...] = mid[...] + BRANCH_SCALE * (rs_result(2) + vec[5])
-    g_pump(0, 1)
-    for j in (1, 2, 3):
-        rcopy(smz.at[z_other(j)], smz.at[z_other(j)], 76 + j - 1, z_dev(j)).wait_recv()
-    smy[0] = (smz[0] + smz[1]) + (smz[2] + smz[3])
-    small_y = rcopy(smy.at[0], smy.at[1], 79, y_dev)
-    small_y.start()
-
+    g_pump(1, 3)
+    g_pump(1, 2)
     d_normed = rs_result(3)
     scaled = xhat[own, :]
     weighted = d_normed * gain_one
@@ -976,22 +1047,31 @@
         - jnp.mean(weighted, -1, keepdims=True)
         - scaled * jnp.mean(weighted * scaled, -1, keepdims=True)
     )
+    g_pump(1, 1)
+    for j in (1, 2, 3):
+        rcopy(smz.at[z_other(j)], smz.at[z_other(j)], 83 + j - 1, z_dev(j)).wait_recv()
+    smy[0] = (smz[0] + smz[1]) + (smz[2] + smz[3])
+    small_y = rcopy(smy.at[0], smy.at[1], 86, y_dev)
+    small_y.start()
+    g_finish(0)
     small_y.wait_recv()
     smc[0] = smy[0] + smy[1]
-    small_c = rcopy(smc.at[0], smc.at[1], 80, c_dev)
+    small_c = rcopy(smc.at[0], smc.at[1], 87, c_dev)
     small_c.start()
-    g_finish(0)
+    g_finish(1)
     small_c.wait_recv()
     small_o[0:6, :] = smc[0, 0:6, :] + smc[1, 0:6, :]
     small_o[6:8, :] = smy[0, 6:8, :]
 
     for b in range(3):
         ag_drain(b)
-        g_drain(b)
+    for u in range(4):
+        g_drain(u)
     for k in range(4):
         rs_y(k).wait_send()
-    rs_core_drain(2)
-    rs_core_drain(3)
+    for k in (2, 3):
+        for half in range(2):
+            rs_core(k, half).wait_send()
     qg_drain(0, hidden)
     qg_drain(1, dattn)
     small_x.wait_send()
@@ -1009,6 +1089,8 @@
     sizes = (tokens, width, quarter, heads, rows)
     vm = pltpu.VMEM
     scratch = [
+        vm(win.shape, F32),
+        vm(wout.shape, F32),
         vm((tokens, width), F32),
         vm((tokens, width), F32),
         vm((tokens, 1), F32),
@@ -1023,19 +1105,22 @@
         vm((tokens, 256), BF16),
         vm((2, 2, quarter, width), BF16),
         vm((4, 2, quarter, width), BF16),
-        vm((4, quarter, width), F32),
+        vm((3, quarter, width), F32),
         vm((4, quarter, width), BF16),
         vm((4, quarter, width), BF16),
         vm((quarter, width), F32),
         vm((quarter, width), F32),
         vm((quarter, 1), F32),
+        vm((width, tokens), BF16),
         vm((tokens, width), BF16),
         vm((tokens, width), BF16),
         vm((tokens, width), BF16),
         vm((tokens, width), BF16),
-        vm((heads, tokens, HD), F32),
-        vm((heads, tokens, HD), F32),
+        vm((tokens, 256), BF16),
+        vm((heads, HD, tokens), F32),
+        vm((heads, HD, tokens), F32),
         vm((tokens, 640), BF16),
+        vm((width, 256), F32),
         vm((3, width, width), BF16),
         vm((3, 4, rows, width), BF16),
         vm((3, 3, rows, width), BF16),
@@ -1045,9 +1130,9 @@
         vm((4, 8, width), F32),
         vm((2, 8, width), F32),
         vm((2, 8, width), F32),
-        pltpu.SemaphoreType.DMA((2,)),
-        pltpu.SemaphoreType.DMA((81,)),
-        pltpu.SemaphoreType.DMA((81,)),
+        pltpu.SemaphoreType.DMA((4,)),
+        pltpu.SemaphoreType.DMA((90,)),
+        pltpu.SemaphoreType.DMA((90,)),
     ]
     whole = pl.BlockSpec(memory_space=pltpu.VMEM)
     return pl.pallas_call(
@@ -1058,7 +1143,7 @@
             jax.ShapeDtypeStruct((3, rows, width), F32),
             jax.ShapeDtypeStruct((8, width), F32),
         ),
-        in_specs=[pl.BlockSpec(memory_space=pl.ANY)] * 2 + [whole] * 4,
+        in_specs=[pl.BlockSpec(memory_space=pl.ANY)] * 4 + [whole] * 2,
         out_specs=[whole] * 4,
         scratch_shapes=scratch,
         compiler_params=pltpu.CompilerParams(
@@ -1068,34 +1153,13 @@
     )(resid, cotangent, win, wout, bias, vec)
 
 
-def adam_kernel(
-    sizes,
-    out_h,
-    grad_h,
-    gsum,
-    small,
-    win,
-    m1_in,
-    m2_in,
-    wout,
-    m1_out,
-    m2_out,
-    wb,
-    m1_b,
-    m2_b,
-    wv,
-    m1_v,
-    m2_v,
-    *refs,
-):
-    out_o, grad_o = refs[0:2]
-    outs = refs[2:14]
-    vin = refs[14:17]
-    vout = refs[17:20]
-    rin = refs[20:23]
-    rout = refs[23:26]
-    sems = refs[26]
-    hc = sizes
+def adam_kernel(hc, out_h, grad_h, gsum_h, small, *refs):
+    in_h, out_h_mat = refs[0:3], refs[3:6]
+    wb, m1_b, m2_b, wv, m1_v, m2_v = refs[6:12]
+    out_o, grad_o = refs[12:14]
+    outs = refs[14:26]
+    vin, vout, rin, rout = refs[26:29], refs[29:32], refs[32:35], refs[35:38]
+    gsum, pass_out, pass_grad, sems = refs[38:42]
     count = [0]
 
     def copy(src, dst):
@@ -1104,38 +1168,51 @@
         made.start()
         return made
 
-    loads_in = [copy(src, dst) for src, dst in zip((m1_in, m2_in, win), vin)]
-    loads_out = [copy(src, dst) for src, dst in zip((m1_out, m2_out, wout), vout)]
-    done = [copy(out_h, out_o), copy(grad_h, grad_o)]
-    rate_in, rate_out = 0.5 * D ** (-0.5), 2.0 * D ** (-0.5)
+    loads_g = [copy(gsum_h.at[i], gsum.at[i]) for i in range(3)]
+    loads_in = [[copy(a.at[i], v.at[i]) for a, v in zip(in_h, vin)] for i in range(7)]
+    loads_out = [[copy(a.at[i], v.at[i]) for a, v in zip(out_h_mat, vout)] for i in range(5)]
+    passing = [copy(out_h, pass_out), copy(grad_h, pass_grad)]
+    done = []
 
     for i in range(6):
         new = adam_step(wv[i], m1_v[i], m2_v[i], small[i : i + 1, :], SMALL_RATE, 0.0)
         for ref, value in zip(outs[9:12], new):
             ref[i] = value
-        at = (7, 0) if i == 0 else (7, 256) if i == 1 else (6, (i - 2) * hc)
-        part = small[at[0] : at[0] + 1, at[1] : at[1] + hc]
+        if i < 2:
+            heads = [(3 * h + 2 * i) * HD for h in range(hc // HD)]
+            part = jnp.concatenate([small[7:8, at : at + HD] for at in heads], 1)
+        else:
+            part = small[6:7, (i - 2) * hc : (i - 1) * hc]
         new = adam_step(wb[i], m1_b[i], m2_b[i], part, SMALL_RATE, 0.0)
         for ref, value in zip(outs[6:9], new):
             ref[i] = value
 
-    for load in loads_in:
+    for load in loads_g:
         load.wait()
     for i in range(7):
-        b, at = (0, i * hc) if i < 3 else (1, (i - 3) * hc)
-        new = adam_step(vin[2][i], vin[0][i], vin[1][i], gsum[b, :, at : at + hc], rate_in, DECAY)
-        for ref, value in zip(rin, new):
-            ref[i] = value
-    done += [copy(src, dst) for src, dst in zip(rin, outs[0:3])]
-    for load in loads_out:
-        load.wait()
+        for load in loads_in[i]:
+            load.wait()
+        if i < 3:
+            heads = [(3 * h + i) * HD for h in range(hc // HD)]
+            part = jnp.concatenate([gsum[0, :, at : at + HD] for at in heads], 1)
+        else:
+            part = gsum[1, :, (i - 3) * hc : (i - 2) * hc]
+        new = adam_step(vin[0][i], vin[1][i], vin[2][i], part, 0.5 * D ** (-0.5), DECAY)
+        for v, value, o in zip(rin, new, outs[0:3]):
+            v[i] = value
+            done.append(copy(v.at[i], o.at[i]))
     for i in range(5):
+        for load in loads_out[i]:
+            load.wait()
         b, at = (0, 3 * hc) if i < 1 else (2, (i - 1) * hc)
         part = jnp.transpose(gsum[b, :, at : at + hc])
-        new = adam_step(vout[2][i], vout[0][i], vout[1][i], part, rate_out, DECAY)
-        for ref, value in zip(rout, new):
-            ref[i] = value
-    done += [copy(src, dst) for src, dst in zip(rout, outs[3:6])]
+        new = adam_step(vout[0][i], vout[1][i], vout[2][i], part, 2.0 * D ** (-0.5), DECAY)
+        for v, value, o in zip(rout, new, outs[3:6]):
+            v[i] = value
+            done.append(copy(v.at[i], o.at[i]))
+    for load in passing:
+        load.wait()
+    done += [copy(pass_out, out_o), copy(pass_grad, grad_o)]
     for made in done:
         made.wait()
 
@@ -1149,13 +1226,15 @@
     return pl.pallas_call(
         functools.partial(adam_kernel, hc),
         out_shape=[jax.ShapeDtypeStruct(a.shape, F32) for a in shapes],
-        in_specs=[hbm] * 2 + [whole] * 2 + [hbm] * 6 + [whole] * 6,
+        in_specs=[hbm] * 3 + [whole] + [hbm] * 6 + [whole] * 6,
         out_specs=[hbm] * 8 + [whole] * 6,
         scratch_shapes=[pltpu.VMEM(big_in, F32)] * 3
         + [pltpu.VMEM(big_out, F32)] * 3
         + [pltpu.VMEM(big_in, F32)] * 3
         + [pltpu.VMEM(big_out, F32)] * 3
-        + [pltpu.SemaphoreType.DMA((14,))],
+        + [pltpu.VMEM(operands[2].shape, F32)]
+        + [pltpu.VMEM(operands[0].shape, F32)] * 2
+        + [pltpu.SemaphoreType.DMA((79,))],
         compiler_params=pltpu.CompilerParams(vmem_limit_bytes=62 << 20),
         name="adam",
     )(*operands)

time: 162 us -> 115 us (0.71)
  Pallas kernels: 161 us -> 114 us
    pallas_call x1, Pallas kernels: 50.8 us -> 7.07 us  [run_adam(): pl.pallas_call(functools.partial(adam_kernel, hc), out_shape=[jax.ShapeDt...]
    pallas_call x1, Pallas kernels: 111 us -> 107 us  [run_block(): pl.pallas_call(functools.partial(block_kernel, sizes), out_shape=(jax.Sha...]
where the time goes in v3:
time: 115 us
  Pallas kernels  114 us (99%)
    pallas_call x1, Pallas kernels, run_block(): pl.pallas_call(functools.partial(block_kernel, sizes), out_shape=(jax.Sha...  107 us
    pallas_call x1, Pallas kernels, run_adam(): pl.pallas_call(functools.partial(adam_kernel, hc), out_shape=[jax.ShapeDt...  7.07 us

profile of v3, /device:TPU:0, one launch (start us, length us, event | category | flops | bytes accessed | tf_op | source)
XLA Modules:
  0.0 115.2 jit_solution(9033529922126791053)
XLA Ops:
  0.6 107.3 %block.1 = (f32[256,768]{1,0:T(8,128)}, f32[256,768]{1,0:T(8,128)}, f32[3,96,768]{2,1,0:T(8,128)}, f32[8,768]{1,0:T(8,128)}) custom-call(f32[1024,768]{1,0:T(8,128)} %resid_h.1, f32[1024,768]{1,0:T(8,128)} %cot_h.1, f32[7,96,192]{2,1,0:T(8,128)} %bitcast.36, f32[5,192,96]{2,1,0:T(8,128)} %bitcast.38, f32[6,1,192]{2,1,0:T(1,128)} %bitcast.46, ...), custom_call_target="tpu_custom_call" | custom-call | tf_op jit(solution)/shard_map/block/pallas_call | solution.py:1138
  108.0 7.1 %adam.1 = (f32[256,768]{1,0:T(8,128)}, f32[256,768]{1,0:T(8,128)}, f32[7,96,192]{2,1,0:T(8,128)}, f32[7,96,192]{2,1,0:T(8,128)}, f32[7,96,192]{2,1,0:T(8,128)}, ...) custom-call(f32[256,768]{1,0:T(8,128)} %get-tuple-element.32.out_h, ...), custom_call_target="tpu_custom_call" | custom-call | tf_op jit(solution)/shard_map/adam/pallas_call | solution.py:1226

commit v4 on v3

--- a/solution.py
+++ b/solution.py
@@ -409,6 +409,7 @@
     xr,
     zs,
     zr,
+    gsum,
     sm,
     smx,
     smz,
@@ -439,12 +440,12 @@
     def z_dev(j):
         return (2 * z_other(j) + x, ten)
 
-    def rcopy(src, dst, idx, dev, recv_idx=None):
+    def rcopy(src, dst, send_idx, recv_idx, dev):
         return pltpu.make_async_remote_copy(
             src_ref=src,
             dst_ref=dst,
-            send_sem=ssem.at[idx],
-            recv_sem=rsem.at[idx if recv_idx is None else recv_idx],
+            send_sem=ssem.at[send_idx],
+            recv_sem=rsem.at[recv_idx],
             device_id=dev,
             device_id_type=MESH_IDS,
         )
@@ -466,97 +467,109 @@
     load_win.wait()
     load_wout.wait()
     out_t = [jnp.transpose(wout[i]) for i in range(5)]
-    by_head = [win[i, :, h * HD : (h + 1) * HD] for h in range(heads) for i in range(3)]
-    w[0, mine, :] = jnp.concatenate([*by_head, out_t[0]], 1).astype(BF16)
+    pairs, last = slice(0, 2 * HD), slice(2 * HD, 3 * HD)
+    tiles = [win[0, :, pairs], win[1, :, pairs], win[2, :, pairs], win[0, :, last], win[2, :, last]]
+    tiles += [out_t[0][:, pairs], win[1, :, last], out_t[0][:, last]]
+    w[0, mine, :] = jnp.concatenate(tiles, 1).astype(BF16)
 
     w[1, mine, :] = jnp.concatenate([win[3 + i] for i in range(4)], 1).astype(BF16)
     w[2, mine, :] = jnp.concatenate(out_t[1:], 1).astype(BF16)
     pl.semaphore_wait(barrier, len(peers))
 
+    half_cols = width // 2
+    units = (
+        (0, slice(0, half_cols)),
+        (0, slice(half_cols, width)),
+        (1, slice(0, width)),
+        (2, slice(0, width)),
+    )
+
     is_end = 1 - lax.rem(lax.div(z + 1, 2), 2)
     is_mid = 1 - is_end
     upper = lax.div(z, 2)
-    pair_dev = (2 * z_other(1) + x, ten)
-    mid_dev = (2 * (2 - upper) + x, ten)
     owner_z = (z_other(1), 2 - upper, 3 - 3 * upper)
-    ag_parts = (2, 1, 1)
-    ag_base = (0, 18, 27)
-
-    def piece(b, zi, p):
-        size = shard // ag_parts[b]
-        return w.at[b, rows_at((2 * zi + x) * shard + p * size, size, size), :]
-
-    def ag_copy(b, zi, p, send, recv, dev):
-        src = piece(b, zi, p)
-        n = ag_parts[b]
-        return rcopy(src, src, ag_base[b] + n * send + p, dev, ag_base[b] + n * recv + p)
-
-    def ag_pair(b, p):
-        return ag_copy(b, z, p, 0, 0, pair_dev)
-
-    def ag_mid(b, p):
-        return ag_copy(b, z, p, 1, 1, mid_dev)
-
-    def ag_onward(b, i, p):
+    pair_dev, mid_dev = (2 * owner_z[0] + x, ten), (2 * owner_z[1] + x, ten)
+
+    def ag_copy(u, zi, send, recv, dev):
+        b, cols = units[u]
+        src = w.at[b, rows_at((2 * zi + x) * shard, shard, shard), cols]
+        return rcopy(src, src, send + u, recv, dev)
+
+    def ag_pair(u):
+        return ag_copy(u, z, 4, 3 * u, pair_dev)
+
+    def ag_mid(u):
+        return ag_copy(u, z, 4, 3 * u + 1, mid_dev)
+
+    def ag_onward(u, i):
         if i == 0:
-            return ag_copy(b, owner_z[0], p, 2, 2, mid_dev)
-        return ag_copy(b, owner_z[i], p, 2 + i, i, pair_dev)
-
-    def ag_x(b, i, p):
-        return ag_copy(b, z if i == 0 else owner_z[i - 1], p, 5 + i, 4 + i, x_dev)
-
-    def ag_start_x(b):
-        for p in range(ag_parts[b]):
-            ag_x(b, 0, p).start()
-
-    def ag_start_z(b):
-        for p in range(ag_parts[b]):
-            ag_pair(b, p).start()
-
-            @pl.when(is_mid == 1)
-            def _():
-                ag_mid(b, p).start()
-
-    def ag_arrive(b, i, p):
-        ag_copy(b, owner_z[i], p, i, i, x_dev).wait_recv()
-
-    def pump_end(b, i, p=0):
+            return ag_copy(u, owner_z[0], 4, 3 * u + 2, mid_dev)
+        return ag_copy(u, owner_z[i], 4, 3 * u + i, pair_dev)
+
+    def ag_x(u, i):
+        return ag_copy(u, z if i == 0 else owner_z[i - 1], 0, 12 + u, x_dev)
+
+    def ag_bytes(u, pieces, send, recv):
+        b, cols = units[u]
+        ref = w.at[b, 0 : pieces * shard, cols]
+        return rcopy(ref, ref, send, recv, x_dev)
+
+    def mid_start(u):
+        @pl.when(is_mid == 1)
+        def _():
+            ag_pair(u).start()
+            ag_mid(u).start()
+
+    def ag_arrive(u, i):
+        ag_copy(u, owner_z[i], 0, 3 * u + i, x_dev).wait_recv()
+
+    def pump_end(u, i):
         @pl.when(is_end == 1)
         def _():
-            ag_arrive(b, i, p)
-            ag_x(b, 1 + i, p).start()
-
-    def pump_mid(b, i, p=0):
+            ag_arrive(u, i)
+            ag_x(u, 1 + i).start()
+
+    def pump_mid(u, i):
         @pl.when(is_mid == 1)
         def _():
-            ag_arrive(b, i, p)
-            ag_onward(b, i, p).start()
-            ag_x(b, 1 + i, p).start()
-
-    def ag_finish(b):
-        for p in range(ag_parts[b]):
-            for i in range(4):
-                ag_x(b, i, p).wait_recv()
-
-    def ag_drain(b):
-        for p in range(ag_parts[b]):
-            ag_pair(b, p).wait_send()
-            for i in range(4):
-                ag_x(b, i, p).wait_send()
-
-            @pl.when(is_mid == 1)
-            def _():
-                ag_mid(b, p).wait_send()
-                for i in range(3):
-                    ag_onward(b, i, p).wait_send()
-
-    ag_start_x(0)
-    ag_start_z(0)
+            ag_arrive(u, i)
+            ag_onward(u, i).start()
+            ag_x(u, 1 + i).start()
+
+    def mid_onward(u, i):
+        @pl.when(is_mid == 1)
+        def _():
+            ag_arrive(u, i)
+            ag_onward(u, i).start()
+
+    def mid_x(u, i):
+        @pl.when(is_mid == 1)
+        def _():
+            ag_x(u, i).start()
+
+    def ag_finish(u):
+        ag_bytes(u, 4, u, 12 + u).wait_recv()
+
+    def ag_drain(u):
+        ag_bytes(u, 4, u, 12 + u).wait_send()
+
+        @pl.when(is_end == 1)
+        def _():
+            ag_bytes(u, 1, 4 + u, 12 + u).wait_send()
+
+        @pl.when(is_mid == 1)
+        def _():
+            ag_bytes(u, 5, 4 + u, 12 + u).wait_send()
+
+    ag_x(0, 0).start()
+    ag_x(1, 0).start()
+    mid_start(0)
+    mid_start(1)
 
     @pl.when(is_end == 1)
     def _():
-        for b in (1, 2):
-            ag_pair(b, 0).start()
+        for u in range(4):
+            ag_pair(u).start()
 
     load_resid.wait()
     load_cot.wait()
@@ -579,93 +592,102 @@
         return carry
 
     lax.fori_loop(0, tokens // 128, first_norm, 0)
-    for i, p in ((0, 0), (1, 0), (0, 1), (1, 1), (2, 0), (2, 1)):
-        pump_mid(0, i, p)
-    for i, p in ((0, 0), (0, 1), (1, 0), (1, 1), (2, 0), (2, 1)):
-        pump_end(0, i, p)
+    for u, i in ((0, 0), (0, 1), (1, 0), (1, 1), (0, 2), (1, 2)):
+        pump_mid(u, i)
+    for u, i in ((0, 0), (1, 0), (0, 1), (1, 1), (0, 2), (1, 2)):
+        pump_end(u, i)
+    ag_x(2, 0).start()
+    mid_start(2)
+    pump_mid(2, 0)
+    ag_x(3, 0).start()
+    mid_start(3)
+    mid_onward(3, 0)
+
     sm[...] = jnp.zeros_like(sm)
     sm[5:6, :] = jnp.sum(dmlp[own, :].astype(F32), 0, keepdims=True)
     mixed[...] = jnp.zeros_like(mixed)
     dqkv[...] = jnp.zeros_like(dqkv)
-
-    ag_start_x(1)
-    ag_start_x(2)
-
-    @pl.when(is_mid == 1)
-    def _():
-        ag_start_z(1)
-
-    for i in range(3):
-        pump_mid(1, i)
-
-    @pl.when(is_mid == 1)
-    def _():
-        ag_start_z(2)
-
-    pump_mid(2, 0)
+    dk_s[...] = jnp.zeros_like(dk_s)
+    dv_s[...] = jnp.zeros_like(dv_s)
+
+    hc = heads * HD
+    low_half = lax.broadcasted_iota(jnp.int32, (1, 2 * HD), 1) < HD
+    bias_v01, bias_q01 = bias[1, :, pairs], bias[0, :, pairs]
+    bias_q2v2 = jnp.concatenate([bias[0, :, last], bias[1, :, last]], 1)
+    eighth = HD**-0.5
+
+    def project_pair(r):
+        rows = slice(r * 256, (r + 1) * 256)
+        got = mm(normed[rows, :], w[0, :, 0:384])
+        queries = (got[:, 0:128] + bias_q01).astype(BF16).astype(F32) * eighth
+        q_s[0, rows, :] = jnp.where(low_half, queries, 0.0).astype(BF16)
+        q_s[1, rows, :] = jnp.where(low_half, 0.0, queries).astype(BF16)
+        k_s[0, rows, :] = got[:, 128:256].astype(BF16)
+        v_s[0, rows, :] = (got[:, 256:384] + bias_v01).astype(BF16)
+
+    def project_last(r):
+        rows = slice(r * 256, (r + 1) * 256)
+        got = mm(normed[rows, :], w[0, :, 384:768])
+        both = (got[:, 0:128] + bias_q2v2).astype(BF16)
+        q_s[2, rows, :] = jnp.where(low_half, both.astype(F32) * eighth, 0.0).astype(BF16)
+        v_s[1, rows, :] = both
+        k_s[1, rows, :] = got[:, 256:384].astype(BF16)
+
     ag_finish(0)
-    pump_end(1, 0)
-
-    hc = heads * HD
-    no_bias = jnp.zeros((1, HD), F32)
-    bias_qkv = []
-    for h in range(heads):
-        at = slice(h * HD, (h + 1) * HD)
-        bias_qkv += [bias[0, :, at], no_bias, bias[1, :, at]]
-    bias_qkv = jnp.concatenate([*bias_qkv, no_bias], 1)
-
-    def project(r, carry):
-        rows = rows_at(r * 256, 256, 256)
-        got = (mm(normed[rows, :], w[0, :, 0:640]) + bias_qkv).astype(BF16)
-        for h in range(heads):
-            at = 3 * h * HD
-            q_s[h, rows, :] = got[:, at : at + HD] * jnp.asarray(HD**-0.5, BF16)
-            k_s[h, rows, :] = got[:, at + HD : at + 2 * HD]
-            v_s[h, rows, :] = got[:, at + 2 * HD : at + 3 * HD]
-        return carry
-
-    lax.fori_loop(0, tokens // 256, project, 0)
-    pump_end(1, 1)
-
-    def attend(i):
-        first, last = i * quarter, (i + 1) * quarter
-        rows = slice(first, last)
+    for r in range(tokens // 256):
+        project_pair(r)
+    pump_end(2, 0)
+    pump_mid(2, 1)
+
+    def attend(i, which_heads):
+        first, last_row = i * quarter, (i + 1) * quarter
+        rows = slice(first, last_row)
         causal = lax.broadcasted_iota(jnp.int32, (quarter, quarter), 0) >= lax.broadcasted_iota(
             jnp.int32, (quarter, quarter), 1
         )
-        for h in range(heads):
+        got = {}
+        for h in which_heads:
+            at = h // 2
             queries = q_s[h, rows, :]
-            diag = jnp.where(causal, mm(queries, k_s[h, rows, :], NT), MASKED)
+            diag = jnp.where(causal, mm(queries, k_s[at, rows, :], NT), MASKED)
             highest = jnp.max(diag, -1, keepdims=True)
             if i > 0:
-                wide = mm(queries, k_s[h, 0:first, :], NT)
+                wide = mm(queries, k_s[at, 0:first, :], NT)
                 highest = jnp.maximum(highest, jnp.max(wide, -1, keepdims=True))
             e_diag = jnp.exp(diag - highest)
             summed = jnp.sum(e_diag, -1, keepdims=True)
             e_diag = e_diag.astype(BF16)
-            e_s[h, rows, first:last] = e_diag
-            total = mm(e_diag, v_s[h, rows, :])
+            e_s[h, rows, first:last_row] = e_diag
+            total = mm(e_diag, v_s[at, rows, :])
             if i > 0:
                 e_wide = jnp.exp(wide - highest)
                 summed = summed + jnp.sum(e_wide, -1, keepdims=True)
                 e_wide = e_wide.astype(BF16)
                 e_s[h, rows, 0:first] = e_wide
-                total = total + mm(e_wide, v_s[h, 0:first, :])
+                total = total + mm(e_wide, v_s[at, 0:first, :])
             inverse = 1.0 / summed
             linv[h, rows, :] = inverse
-            mixed[rows, (h + 1) * HD : (h + 2) * HD] = (total * inverse).astype(BF16)
+            got[h] = total * inverse
+        if 0 in got:
+            mixed[rows, 0:128] = jnp.where(low_half, got[0], got[1]).astype(BF16)
+        if 2 in got:
+            mixed[rows, 128:256] = jnp.where(low_half, 0.0, got[2]).astype(BF16)
 
     def rs_core(k, half):
-        return rcopy(ps.at[k % 2, half], crecv.at[k, half], 36 + 2 * k + half, c_dev)
-
-    def rs_y(k):
-        return rcopy(ysend.at[k], yrecv.at[k], 44 + k, y_dev)
-
-    def rs_pair(k, near, compute, start_y=True, prepare=None, filler=None):
+        return rcopy(ps.at[k % 2, half], crecv.at[k, half], 16 + 2 * (k % 2) + half, 16 + 2 * k + half, c_dev)
+
+    halves = [slice(0, quarter // 2), slice(quarter // 2, quarter)]
+
+    def rs_y(k, hh):
+        src, dst = ysend.at[k, halves[hh], :], yrecv.at[k, halves[hh], :]
+        return rcopy(src, dst, 20, 24 + 2 * k + hh, y_dev)
+
+    def rs_y_start(k):
+        for hh in range(2):
+            rs_y(k, hh).start()
+
+    def rs_pair(k, near, compute, prepare=None, filler=None):
         half = 1 if near else 0
-        if k >= 2:
-            rs_core(k - 2, half).wait_send()
-
         def step(s, carry):
             yq = y if near else 1 - y
             if prepare is not None:
@@ -691,75 +713,141 @@
                     fin[k % 3] = total
                 else:
                     ysend[k] = total.astype(BF16)
-                    if start_y:
-                        rs_y(k).start()
+                    rs_y_start(k)
 
             return carry
 
         lax.fori_loop(0, 2, step, 0)
 
-    def rs_result(k):
-        rs_y(k).wait_recv()
-        return fin[k % 3] + yrecv[k].astype(F32)
-
-    def pump_far(s):
-        @pl.when(s == 1)
-        def _():
-            pump_end(1, 2)
-            pump_mid(2, 1)
-
-    def pump_near(s):
-        @pl.when(s == 0)
-        def _():
-            pump_mid(2, 2)
-
-        @pl.when(s == 1)
-        def _():
-            pump_end(2, 0)
-
-    def attend_proj(which):
+    def rs_quad(k, compute, held):
+        for half in range(2):
+            rs_core(k - 2, half).wait_send()
+
+        def step(s, carry):
+            half, odd = lax.div(s, 2), lax.rem(s, 2)
+            yq = half * y + (1 - half) * (1 - y)
+            part = compute(2 * yq + lax.rem(1 - odd + c, 2))
+
+            @pl.when(odd == 0)
+            def _():
+                ps[k % 2, half] = part.astype(BF16)
+                rs_core(k, half).start()
+
+            @pl.when(s == 1)
+            def _():
+                held[...] = part
+
+            @pl.when(s == 3)
+            def _():
+                fin[k % 3] = part
+
+            return carry
+
+        lax.fori_loop(0, 4, step, 0)
+
+    def quad_far(k, held):
+        rs_core(k, 0).wait_recv()
+        ysend[k] = (held[...] + crecv[k, 0].astype(F32)).astype(BF16)
+
+    def quad_near(k):
+        rs_core(k, 1).wait_recv()
+        fin[k % 3] = fin[k % 3] + crecv[k, 1].astype(F32)
+
+    def rs_result(k, hh):
+        rs_y(k, hh).wait_recv()
+        return fin[k % 3, halves[hh], :] + yrecv[k, halves[hh], :].astype(F32)
+
+    def attend_quarter(which, which_heads):
         for i in range(tokens // quarter):
 
             @pl.when(which == i)
             def _():
-                attend(i)
-
+                attend(i, which_heads)
+
+    def proj(which):
         return mm(mixed[rows_at(which * quarter, quarter, quarter), :], w[0, :, 512:768], NT)
 
-    rs_pair(0, False, attend_proj, prepare=pump_far)
-    rs_pair(0, True, attend_proj, prepare=pump_near)
-
-    def q_rows(ref, which):
-        return ref.at[rows_at(which * quarter, quarter, quarter), :]
-
-    def qg_y(g, ref):
-        return rcopy(q_rows(ref, ten), q_rows(ref, ten), 48 + g, y_dev)
-
-    def qg_c(g, ref):
-        return rcopy(q_rows(ref, ten), q_rows(ref, ten), 50 + g, c_dev)
-
-    def qg_f(g, ref):
-        far = ten + 2 - 4 * y
-        return rcopy(q_rows(ref, far), q_rows(ref, far), 52 + g, c_dev)
-
-    def qg_drain(g, ref):
-        qg_y(g, ref).wait_send()
-        qg_c(g, ref).wait_send()
-        qg_f(g, ref).wait_send()
-
+    def far_early(s, carry):
+        attend_quarter(2 * (1 - y) + lax.rem(s + c, 2), (0, 1))
+        return carry
+
+    def far_proj(which):
+        attend_quarter(which, (2,))
+        return proj(which)
+
+    def near_proj(which):
+        attend_quarter(which, (0, 1, 2))
+        return proj(which)
+
+    def near_pumps(s):
+        @pl.when(s == 1)
+        def _():
+            pump_end(2, 2)
+            pump_end(3, 0)
+            pump_mid(3, 2)
+
+    lax.fori_loop(0, 2, far_early, 0)
+    pump_mid(2, 2)
+    mid_x(3, 1)
+    ag_finish(1)
+    for r in range(tokens // 256):
+        project_last(r)
+    rs_pair(0, False, far_proj)
     pump_end(2, 1)
-
-    mid[...] = mid[...] + BRANCH_SCALE * (rs_result(0) + vec[4])
-    center = mid[...] - jnp.mean(mid[...], -1, keepdims=True)
-    inverse = lax.rsqrt(jnp.mean(center * center, -1, keepdims=True) + EPS)
-    scaled = center * inverse
-    xhat2[...] = scaled
-    inv2[...] = inverse
-    hidden[own, :] = (scaled * vec[2] + vec[3]).astype(BF16)
-    qg_y(0, hidden).start()
-    qg_c(0, hidden).start()
-
-    ag_finish(1)
+    pump_mid(3, 1)
+    rs_pair(0, True, near_proj, prepare=near_pumps)
+
+    def q_rows(ref, which, hh):
+        return ref.at[rows_at(which * quarter + hh * (quarter // 2), quarter // 2, quarter // 2), :]
+
+    def qg_y(g, ref, hh):
+        src = q_rows(ref, ten, hh)
+        return rcopy(src, src, 21, 32 + 2 * g + hh, y_dev)
+
+    def qg_c(g, ref, hh):
+        src = q_rows(ref, ten, hh)
+        return rcopy(src, src, 22, 36 + g, c_dev)
+
+    def qg_f(g, ref, hh):
+        src = q_rows(ref, ten + 2 - 4 * y, hh)
+        return rcopy(src, src, 23, 38 + g, c_dev)
+
+    def qg_start(g, ref, hh):
+        qg_y(g, ref, hh).start()
+        qg_c(g, ref, hh).start()
+
+    def qg_rows(ref, count, send, recv):
+        rows = ref.at[0:count, :]
+        return rcopy(rows, rows, send, recv, c_dev)
+
+    def qg_near(g, ref):
+        qg_rows(ref, quarter, 22, 36 + g).wait_recv()
+
+    def qg_far(g, ref):
+        for hh in range(2):
+            qg_y(g, ref, hh).wait_recv()
+            qg_f(g, ref, hh).start()
+
+    def qg_last(g, ref):
+        qg_rows(ref, quarter, 23, 38 + g).wait_recv()
+
+    pump_end(3, 1)
+
+    for hh in range(2):
+        half = halves[hh]
+        middle = mid[half, :] + BRANCH_SCALE * (rs_result(0, hh) + vec[4])
+        mid[half, :] = middle
+        center = middle - jnp.mean(middle, -1, keepdims=True)
+        inverse = lax.rsqrt(jnp.mean(center * center, -1, keepdims=True) + EPS)
+        scaled = center * inverse
+        xhat2[half, :] = scaled
+        inv2[half, :] = inverse
+        mine_h = rows_at(ten * quarter + hh * (quarter // 2), quarter // 2, quarter // 2)
+        hidden[mine_h, :] = (scaled * vec[2] + vec[3]).astype(BF16)
+        qg_start(0, hidden, hh)
+
+    pump_end(3, 2)
+    ag_finish(2)
 
     bias_up = jnp.concatenate([bias[2 + i] for i in range(4)], 1)
 
@@ -778,66 +866,115 @@
             )
             dpre[rows, cols] = slope.astype(BF16)
 
-    units = (
-        (0, slice(0, 384)),
-        (0, slice(384, 768)),
-        (1, slice(0, 768)),
-        (2, slice(0, 768)),
-    )
-
     def grad_block(b, left, right, near):
-        rows = rows_at((y if near else 1 - y) * 2 * quarter, 2 * quarter, 2 * quarter)
+        rows = slice(0, tokens)
+        if near is not None:
+            rows = rows_at((y if near else 1 - y) * 2 * quarter, 2 * quarter, 2 * quarter)
 
         def tile(t, carry):
             cols = rows_at(t * 256, 256, 256)
             part = mm(left[rows, cols], right[rows, :], TN)
-            if not near:
+            if near is False:
                 part = part + gmat[b, cols, :].astype(F32)
             gmat[b, cols, :] = part.astype(BF16)
             return carry
 
         lax.fori_loop(0, width // 256, tile, 0)
 
-    def g_rows(u, owner):
-        b, cols = units[u]
-        return gmat.at[b, rows_at(owner * shard, shard, shard), cols]
 
     def gx(u, zi):
         b, cols = units[u]
-        return rcopy(g_rows(u, 2 * zi + 1 - x), xr.at[b, zi, :, cols], 54 + 4 * u + zi, x_dev)
-
-    def gz(u, j):
+        src = gmat.at[b, rows_at((2 * zi + 1 - x) * shard, shard, shard), cols]
+        return rcopy(src, xr.at[b, zi, :, cols], 8 + u, 40 + 4 * u + zi, x_dev)
+
+    def line_to(i):
+        if i == 0:
+            return pair_dev, 0
+        return (2 * (is_end * owner_z[0] + is_mid * owner_z[i]) + x, ten), is_end * i + is_mid * 3
+
+    def gz(u, i):
         b, cols = units[u]
+        if u < 2:
+            src, dst = zs.at[b, i - 1, :, cols], zr.at[b, i - 1, :, cols]
+            return rcopy(src, dst, 12 + u, 56 + u, z_dev(i))
+        dev, slot = line_to(i)
         return rcopy(
-            zs.at[b, j - 1, :, cols], zr.at[b, j - 1, :, cols], 70 + 3 * u + j - 1, z_dev(j)
+            zs.at[b, i, :, cols], zr.at[b, slot, :, cols], 12 + u, 58 + 4 * (u - 2) + slot, dev
         )
 
+    def gz_arrive(u, slot):
+        b, cols = units[u]
+        ref = zr.at[b, slot, :, cols]
+        rcopy(ref, ref, 12 + u, 58 + 4 * (u - 2) + slot, x_dev).wait_recv()
+
     def g_start(u):
-        for j in (3, 2, 1, 0):
-            gx(u, z_other(j) if j else z).start()
+        @pl.when(is_end == 1)
+        def _():
+            for i in (2, 1, 0):
+                gx(u, owner_z[i]).start()
+
+        @pl.when(is_mid == 1)
+        def _():
+            for i in (0, 2, 1):
+                gx(u, owner_z[i]).start()
+
+        gx(u, z).start()
+
+    def x_sum(u, zo):
+        b, cols = units[u]
+        gx(u, zo).wait_recv()
+        mine_x = gmat[b, rows_at((2 * zo + x) * shard, shard, shard), cols].astype(F32)
+        return mine_x + xr[b, zo, :, cols].astype(F32)
 
     def g_pump(u, j):
         b, cols = units[u]
-        zo = z_other(j)
-        gx(u, zo).wait_recv()
-        mine_x = gmat[b, rows_at((2 * zo + x) * shard, shard, shard), cols].astype(F32)
-        zs[b, j - 1, :, cols] = (mine_x + xr[b, zo, :, cols].astype(F32)).astype(BF16)
+        zs[b, j - 1, :, cols] = x_sum(u, z_other(j)).astype(BF16)
         gz(u, j).start()
+
+    def end_pump(u, i):
+        b, cols = units[u]
+
+        @pl.when(is_end == 1)
+        def _():
+            zs[b, i, :, cols] = x_sum(u, owner_z[i]).astype(BF16)
+            gz(u, i).start()
+
+    def mid_pump(u, i):
+        b, cols = units[u]
+
+        @pl.when(is_mid == 1)
+        def _():
+            total = x_sum(u, owner_z[i])
+            if i > 0:
+                gz_arrive(u, i)
+                total = total + zr[b, i, :, cols].astype(F32)
+            zs[b, i, :, cols] = total.astype(BF16)
+            gz(u, i).start()
 
     def g_finish(u):
         b, cols = units[u]
-        gx(u, z).wait_recv()
-        total = gmat[b, mine, cols].astype(F32) + xr[b, z, :, cols].astype(F32)
-        for j in (1, 2, 3):
-            gz(u, j).wait_recv()
-            total = total + zr[b, j - 1, :, cols].astype(F32)
-        gsum_o[b, :, cols] = total
+        total = x_sum(u, z)
+        if u < 2:
+            three = zr.at[b, 0:3, :, cols]
+            rcopy(three, three, 12 + u, 56 + u, x_dev).wait_recv()
+            for j in range(3):
+                total = total + zr[b, j, :, cols].astype(F32)
+        else:
+            for slot in (0, 3):
+                gz_arrive(u, slot)
+                total = total + zr[b, slot, :, cols].astype(F32)
+        gsum[b, :, cols] = total
+        g_out(u).start()
+
+    def g_out(u):
+        b, cols = units[u]
+        return pltpu.make_async_copy(gsum.at[b, :, cols], gsum_o.at[b, :, cols], lsem.at[4 + u])
 
     def g_drain(u):
-        for zi in range(4):
-            gx(u, zi).wait_send()
-        for j in (1, 2, 3):
-            gz(u, j).wait_send()
+        b, cols = units[u]
+        rcopy(xr.at[b, :, :, cols], xr.at[b, :, :, cols], 8 + u, 56, x_dev).wait_send()
+        rcopy(zs.at[b, :, :, cols], zs.at[b, :, :, cols], 12 + u, 56, x_dev).wait_send()
+        g_out(u).wait()
 
     def backward_units(which):
         rows = rows_at(which * quarter, quarter, quarter)
@@ -857,27 +994,22 @@
     def near_units(s, carry):
         @pl.when(s == 1)
         def _():
-            qg_c(0, hidden).wait_recv()
+            qg_near(0, hidden)
 
         forward_units(2 * y + lax.rem(s + c, 2))
         return carry
 
     lax.fori_loop(0, 2, near_units, 0)
-    pump_end(2, 2)
     grad_block(2, dmlp, act_s, True)
     for t in range(width // 256):
         cols = slice(t * 256, (t + 1) * 256)
         normed_t[cols, :] = jnp.transpose(normed[:, cols])
-    ag_finish(2)
-    rs_pair(1, True, backward_units)
-    grad_block(1, hidden, dpre, True)
-    qg_y(0, hidden).wait_recv()
-    qg_f(0, hidden).start()
+    qg_far(0, hidden)
 
     def far_units(s, carry):
         @pl.when(s == 1)
         def _():
-            qg_f(0, hidden).wait_recv()
+            qg_last(0, hidden)
 
         forward_units(2 * (1 - y) + lax.rem(s + c, 2))
         return carry
@@ -887,52 +1019,58 @@
         g_start(3)
 
     lax.fori_loop(0, 2, far_units, 0)
+    ag_finish(3)
     rs_pair(1, False, backward_units, filler=down_gradient)
-    grad_block(1, hidden, dpre, False)
+    rs_pair(1, True, backward_units)
+    grad_block(1, hidden, dpre, None)
     g_start(2)
-    rs_pair(2, False, branch, start_y=False)
-    g_pump(3, 3)
-    rs_pair(2, True, branch)
-    g_pump(3, 2)
-    g_pump(3, 1)
-
-    d_hidden = rs_result(1)
-    scaled = xhat2[...]
-    sm[2:3, :] = jnp.sum(d_hidden * scaled, 0, keepdims=True)
-    sm[3:4, :] = jnp.sum(d_hidden, 0, keepdims=True)
-    weighted = d_hidden * vec[2]
-    d_mid = cot[own, :] + inv2[...] * (
-        weighted
-        - jnp.mean(weighted, -1, keepdims=True)
-        - scaled * jnp.mean(weighted * scaled, -1, keepdims=True)
-    )
-    fin[1] = d_mid
-    d_attn = (BRANCH_SCALE * d_mid).astype(BF16)
-    dattn[own, :] = d_attn
-    sm[4:5, :] = jnp.sum(d_attn.astype(F32), 0, keepdims=True)
-    qg_y(1, dattn).start()
-    qg_c(1, dattn).start()
-
-    dk_s[...] = jnp.zeros_like(dk_s)
-    dv_s[...] = jnp.zeros_like(dv_s)
+    end_pump(3, 2)
+    mid_pump(3, 0)
+    rs_quad(2, branch, fin.at[0])
+    end_pump(3, 1)
+    quad_far(2, fin.at[0])
+    quad_near(2)
+
+    for hh in range(2):
+        half = halves[hh]
+        mine_h = rows_at(ten * quarter + hh * (quarter // 2), quarter // 2, quarter // 2)
+        d_hidden = rs_result(1, hh)
+        scaled = xhat2[half, :]
+        sm[2:3, :] = sm[2:3, :] + jnp.sum(d_hidden * scaled, 0, keepdims=True)
+        sm[3:4, :] = sm[3:4, :] + jnp.sum(d_hidden, 0, keepdims=True)
+        weighted = d_hidden * vec[2]
+        d_mid = cot[mine_h, :] + inv2[half, :] * (
+            weighted
+            - jnp.mean(weighted, -1, keepdims=True)
+            - scaled * jnp.mean(weighted * scaled, -1, keepdims=True)
+        )
+        fin[1, half, :] = d_mid
+        d_attn = (BRANCH_SCALE * d_mid).astype(BF16)
+        dattn[mine_h, :] = d_attn
+        sm[4:5, :] = sm[4:5, :] + jnp.sum(d_attn.astype(F32), 0, keepdims=True)
+        qg_start(1, dattn, hh)
 
     def attend_back(i, which_heads):
-        first, last = i * quarter, (i + 1) * quarter
-        rows = slice(first, last)
+        first, last_row = i * quarter, (i + 1) * quarter
+        rows = slice(first, last_row)
+        got = {}
         for h in which_heads:
-            cols = slice((h + 1) * HD, (h + 2) * HD)
-            d_out = dmix[rows, cols].astype(F32)
-            inverse = linv[h, rows, :]
-            d_scaled = d_out * inverse
-            inner = jnp.sum(d_scaled * mixed[rows, cols].astype(F32), -1, keepdims=True)
-            d_scaled = d_scaled.astype(BF16)
-            expo = e_s[h, rows, 0:last]
-            d_probs = mm(d_scaled, v_s[h, 0:last, :], NT)
+            at = h // 2
+            tile = slice(at * 128, (at + 1) * 128)
+            d_out = dmix[rows, tile].astype(F32) * linv[h, rows, :]
+            d_out = jnp.where(low_half, d_out, 0.0) if h == 0 else jnp.where(low_half, 0.0, d_out)
+            inner = jnp.sum(d_out * mixed[rows, tile].astype(F32), -1, keepdims=True)
+            d_scaled = d_out.astype(BF16)
+            expo = e_s[h, rows, 0:last_row]
+            d_probs = mm(d_scaled, v_s[at, 0:last_row, :], NT)
             d_scores = (expo.astype(F32) * (d_probs - inner)).astype(BF16)
-            d_q = mm(d_scores, k_s[h, 0:last, :]) * HD**-0.5
-            dqkv[rows, 3 * h * HD : (3 * h + 1) * HD] = d_q.astype(BF16)
-            dk_s[h, :, 0:last] = dk_s[h, :, 0:last] + mm(q_s[h, rows, :], d_scores, TN)
-            dv_s[h, :, 0:last] = dv_s[h, :, 0:last] + mm(d_scaled, expo, TN)
+            got[h] = mm(d_scores, k_s[at, 0:last_row, :]) * eighth
+            dk_s[at, :, 0:last_row] = dk_s[at, :, 0:last_row] + mm(q_s[h, rows, :], d_scores, TN)
+            dv_s[at, :, 0:last_row] = dv_s[at, :, 0:last_row] + mm(d_scaled, expo, TN)
+        if 0 in got:
+            dqkv[rows, 0:128] = jnp.where(low_half, got[0], got[1]).astype(BF16)
+        if 2 in got:
+            dqkv[rows, 384:512] = jnp.where(low_half, got[2], 0.0).astype(BF16)
 
     def back_quarters(near, which_heads, fresh, prepare=None):
         def step(s, carry):
@@ -956,18 +1094,22 @@
     def near_ready(s):
         @pl.when(s == 1)
         def _():
-            qg_c(1, dattn).wait_recv()
+            qg_near(1, dattn)
 
     def far_ready(s):
         @pl.when(s == 1)
         def _():
-            qg_f(1, dattn).wait_recv()
-
-    def keys_values(which_heads):
-        for h in which_heads:
-            at = 3 * h * HD
-            dqkv[:, at + HD : at + 2 * HD] = jnp.transpose(dk_s[h]).astype(BF16)
-            dqkv[:, at + 2 * HD : at + 3 * HD] = jnp.transpose(dv_s[h]).astype(BF16)
+            qg_last(1, dattn)
+            end_pump(2, 1)
+
+    def keys_values(at):
+        if at == 0:
+            dqkv[:, 128:256] = jnp.transpose(dk_s[0]).astype(BF16)
+            dqkv[:, 256:384] = jnp.transpose(dv_s[0]).astype(BF16)
+        else:
+            d_v = jnp.transpose(dv_s[1]).astype(BF16)
+            dqkv[:, 384:512] = jnp.where(low_half, dqkv[:, 384:512], d_v)
+            dqkv[:, 640:768] = jnp.transpose(dk_s[1]).astype(BF16)
 
     def zero_rows(u, zo):
         cols = rows_at(zo * 2 * shard, 2 * shard, 2 * shard)
@@ -975,11 +1117,9 @@
         if u == 0:
             gmat[0, cols, 0:384] = mm(left, dqkv[:, 0:384]).astype(BF16)
         else:
-            g_qkv = mm(left, dqkv[:, 384:640])
-            g_proj = gproj[cols, :]
+            g_qkv = mm(left, dqkv[:, 384:768])
             gmat[0, cols, 384:512] = g_qkv[:, 0:128].astype(BF16)
-            gmat[0, cols, 512:640] = (g_qkv[:, 128:256] + g_proj[:, 0:128]).astype(BF16)
-            gmat[0, cols, 640:768] = g_proj[:, 128:256].astype(BF16)
+            gmat[0, cols, 512:768] = (g_qkv[:, 128:384] + gproj[cols, :]).astype(BF16)
         gx(u, zo).start()
 
     def zero_unit(u):
@@ -992,93 +1132,110 @@
 
         lax.fori_loop(0, 4, step, 0)
 
+    end_pump(3, 0)
+    mid_pump(3, 2)
     back_quarters(True, (0, 1, 2), True, near_ready)
-    g_pump(2, 3)
-    g_pump(2, 2)
-    qg_y(1, dattn).wait_recv()
-    qg_f(1, dattn).start()
-    rs_y(2).start()
+    mid_pump(3, 1)
+    end_pump(2, 2)
+    mid_pump(2, 0)
+    qg_far(1, dattn)
+    rs_y_start(2)
     back_quarters(False, (0, 1), True, far_ready)
-    keys_values((0, 1))
+    keys_values(0)
     zero_unit(0)
     gproj[...] = jnp.transpose(mm(mixed[...], dattn[...], TN))
-
-    g_pump(2, 1)
+    end_pump(2, 0)
+    mid_pump(2, 2)
     back_quarters(False, (2,), False)
-    keys_values((2,))
-    g_pump(0, 3)
+    keys_values(1)
+    mid_pump(2, 1)
 
     def first_back(which):
         rows = rows_at(which * quarter, quarter, quarter)
         d_low = dqkv[rows, :]
-        part = mm(d_low, w[0, :, 0:640], NT)
+        part = mm(d_low, w[0], NT)
         rounded = part.astype(BF16).astype(F32)
         sm[0:1, :] = sm[0:1, :] + jnp.sum(rounded * xhat[rows, :], 0, keepdims=True)
         sm[1:2, :] = sm[1:2, :] + jnp.sum(rounded, 0, keepdims=True)
-        sm[7:8, 0:640] = sm[7:8, 0:640] + jnp.sum(d_low.astype(F32), 0, keepdims=True)
+        sm[7:8, :] = sm[7:8, :] + jnp.sum(d_low.astype(F32), 0, keepdims=True)
         return part
 
-    rs_pair(3, False, first_back)
-    rs_pair(3, True, first_back)
-
-    small_x = rcopy(sm, smx, 82, x_dev)
+    rs_quad(3, first_back, xhat2)
+
+    small_x = rcopy(sm, smx, 24, 66, x_dev)
     small_x.start()
+    quad_far(3, xhat2)
+    rs_y_start(3)
+    g_pump(0, 3)
+    zero_unit(1)
+    quad_near(3)
     g_pump(0, 2)
-    zero_unit(1)
-    g_pump(0, 1)
     small_x.wait_recv()
     smz[z] = sm[...] + smx[...]
 
     def small_z(j):
-        return rcopy(smz.at[z], smz.at[z], 83 + j - 1, z_dev(j))
+        return rcopy(smz.at[z], smz.at[z], 25, 67, z_dev(j))
 
     for j in (3, 2, 1):
         small_z(j).start()
+    g_pump(0, 1)
     g_finish(3)
     g_finish(2)
-    out_o[...] = mid[...] + BRANCH_SCALE * (rs_result(2) + vec[5])
+    for hh in range(2):
+        half = halves[hh]
+        mid[half, :] = mid[half, :] + BRANCH_SCALE * (rs_result(2, hh) + vec[5])
+    put_out = pltpu.make_async_copy(mid, out_o, lsem.at[8])
+    put_out.start()
     g_pump(1, 3)
     g_pump(1, 2)
-    d_normed = rs_result(3)
-    scaled = xhat[own, :]
-    weighted = d_normed * gain_one
-    grad_o[...] = fin[1] + inv1[own, :] * (
-        weighted
-        - jnp.mean(weighted, -1, keepdims=True)
-        - scaled * jnp.mean(weighted * scaled, -1, keepdims=True)
-    )
+
+    def first_norm_back(hh):
+        half = halves[hh]
+        mine_h = rows_at(ten * quarter + hh * (quarter // 2), quarter // 2, quarter // 2)
+        d_normed = rs_result(3, hh)
+        scaled = xhat[mine_h, :]
+        weighted = d_normed * gain_one
+        xhat2[half, :] = fin[1, half, :] + inv1[mine_h, :] * (
+            weighted
+            - jnp.mean(weighted, -1, keepdims=True)
+            - scaled * jnp.mean(weighted * scaled, -1, keepdims=True)
+        )
+
+    first_norm_back(0)
     g_pump(1, 1)
-    for j in (1, 2, 3):
-        rcopy(smz.at[z_other(j)], smz.at[z_other(j)], 83 + j - 1, z_dev(j)).wait_recv()
+    first_norm_back(1)
+    put_grad = pltpu.make_async_copy(xhat2, grad_o, lsem.at[9])
+    put_grad.start()
+    three = rcopy(smz.at[0:3], smz.at[0:3], 25, 67, x_dev)
+    three.wait_recv()
     smy[0] = (smz[0] + smz[1]) + (smz[2] + smz[3])
-    small_y = rcopy(smy.at[0], smy.at[1], 86, y_dev)
+    small_y = rcopy(smy.at[0], smy.at[1], 26, 68, y_dev)
     small_y.start()
     g_finish(0)
     small_y.wait_recv()
     smc[0] = smy[0] + smy[1]
-    small_c = rcopy(smc.at[0], smc.at[1], 87, c_dev)
+    small_c = rcopy(smc.at[0], smc.at[1], 27, 69, c_dev)
     small_c.start()
     g_finish(1)
     small_c.wait_recv()
     small_o[0:6, :] = smc[0, 0:6, :] + smc[1, 0:6, :]
     small_o[6:8, :] = smy[0, 6:8, :]
 
-    for b in range(3):
-        ag_drain(b)
     for u in range(4):
+        ag_drain(u)
         g_drain(u)
-    for k in range(4):
-        rs_y(k).wait_send()
+    rcopy(ysend, yrecv, 20, 24, y_dev).wait_send()
     for k in (2, 3):
         for half in range(2):
             rs_core(k, half).wait_send()
-    qg_drain(0, hidden)
-    qg_drain(1, dattn)
+    for send in (21, 22, 23):
+        qg_rows(hidden, 2 * quarter, send, 36).wait_send()
     small_x.wait_send()
-    for j in (1, 2, 3):
-        small_z(j).wait_send()
+    three.wait_send()
     small_y.wait_send()
     small_c.wait_send()
+    put_out.wait()
+    put_grad.wait()
 
 
 def run_block(resid, cotangent, win, wout, bias, vec, rows, n_dp):
@@ -1097,9 +1254,9 @@
         vm((tokens, width), BF16),
         vm((tokens, width), BF16),
         vm((3, width, width), BF16),
-        vm((heads, tokens, HD), BF16),
-        vm((heads, tokens, HD), BF16),
-        vm((heads, tokens, HD), BF16),
+        vm((heads, tokens, 2 * HD), BF16),
+        vm((2, tokens, 2 * HD), BF16),
+        vm((2, tokens, 2 * HD), BF16),
         vm((heads, tokens, tokens), BF16),
         vm((heads, tokens, 1), F32),
         vm((tokens, 256), BF16),
@@ -1117,22 +1274,23 @@
         vm((tokens, width), BF16),
         vm((tokens, width), BF16),
         vm((tokens, 256), BF16),
-        vm((heads, HD, tokens), F32),
-        vm((heads, HD, tokens), F32),
-        vm((tokens, 640), BF16),
+        vm((2, 2 * HD, tokens), F32),
+        vm((2, 2 * HD, tokens), F32),
+        vm((tokens, width), BF16),
         vm((width, 256), F32),
         vm((3, width, width), BF16),
         vm((3, 4, rows, width), BF16),
         vm((3, 3, rows, width), BF16),
-        vm((3, 3, rows, width), BF16),
+        vm((3, 4, rows, width), BF16),
+        vm((3, rows, width), F32),
         vm((8, width), F32),
         vm((8, width), F32),
         vm((4, 8, width), F32),
         vm((2, 8, width), F32),
         vm((2, 8, width), F32),
-        pltpu.SemaphoreType.DMA((4,)),
-        pltpu.SemaphoreType.DMA((90,)),
-        pltpu.SemaphoreType.DMA((90,)),
+        pltpu.SemaphoreType.DMA((10,)),
+        pltpu.SemaphoreType.DMA((28,)),
+        pltpu.SemaphoreType.DMA((70,)),
     ]
     whole = pl.BlockSpec(memory_space=pltpu.VMEM)
     return pl.pallas_call(
@@ -1144,7 +1302,7 @@
             jax.ShapeDtypeStruct((8, width), F32),
         ),
         in_specs=[pl.BlockSpec(memory_space=pl.ANY)] * 4 + [whole] * 2,
-        out_specs=[whole] * 4,
+        out_specs=[pl.BlockSpec(memory_space=pl.ANY)] * 3 + [whole],
         scratch_shapes=scratch,
         compiler_params=pltpu.CompilerParams(
             collective_id=1, has_side_effects=True, vmem_limit_bytes=62 << 20
@@ -1153,88 +1311,107 @@
     )(resid, cotangent, win, wout, bias, vec)
 
 
-def adam_kernel(hc, out_h, grad_h, gsum_h, small, *refs):
-    in_h, out_h_mat = refs[0:3], refs[3:6]
-    wb, m1_b, m2_b, wv, m1_v, m2_v = refs[6:12]
-    out_o, grad_o = refs[12:14]
-    outs = refs[14:26]
-    vin, vout, rin, rout = refs[26:29], refs[29:32], refs[32:35], refs[35:38]
-    gsum, pass_out, pass_grad, sems = refs[38:42]
-    count = [0]
-
-    def copy(src, dst):
-        made = pltpu.make_async_copy(src, dst, sems.at[count[0]])
-        count[0] += 1
-        made.start()
-        return made
-
-    loads_g = [copy(gsum_h.at[i], gsum.at[i]) for i in range(3)]
-    loads_in = [[copy(a.at[i], v.at[i]) for a, v in zip(in_h, vin)] for i in range(7)]
-    loads_out = [[copy(a.at[i], v.at[i]) for a, v in zip(out_h_mat, vout)] for i in range(5)]
-    passing = [copy(out_h, pass_out), copy(grad_h, pass_grad)]
-    done = []
-
+BLOCK_ZERO = (((0, 128), (384, 448)), ((128, 256), (640, 704)), ((256, 384), (448, 512)), ((512, 640), (704, 768)))
+
+
+def adam_kernel(hc, *refs):
+    passed_h, gsum_h, small_h = refs[0:2], refs[2], refs[3]
+    in_h, out_h, bias_h, vec_h = refs[4:7], refs[7:10], refs[10:13], refs[13:16]
+    passed_o, in_o, out_o, bias_o, vec_o = refs[16:18], refs[18:21], refs[21:24], refs[24:27], refs[27:30]
+    vin, vout, vbias, vvec, rin, rout, rbias, rvec, gsum, small, passed, sems = refs[30:42]
+
+    def copy(src, dst, sem):
+        pltpu.make_async_copy(src, dst, sems.at[sem]).start()
+
+    def wait(ref, sem):
+        pltpu.make_async_copy(ref, ref, sems.at[sem]).wait()
+
+    def columns(ref, rows, kind):
+        return jnp.concatenate([ref[rows + (slice(a, b),)] for a, b in BLOCK_ZERO[kind]], 1)
+
+    every = slice(None)
+    kinds_in = (3, 4, 5, 6, 0, 1, 2)
+    copy(gsum_h.at[1], gsum.at[1], 0)
+    for i in kinds_in:
+        for a in range(3):
+            copy(in_h[a].at[i], vin.at[i, a], 3 + i)
+        if i == 6:
+            copy(gsum_h.at[0], gsum.at[0], 1)
+    copy(small_h, small, 15)
+    for a in range(3):
+        copy(bias_h[a], vbias.at[a], 16)
+        copy(vec_h[a], vvec.at[a], 17)
+    copy(gsum_h.at[2], gsum.at[2], 2)
+    for i in range(5):
+        for a in range(3):
+            copy(out_h[a].at[i], vout.at[i, a], 10 + i)
+    for a in range(2):
+        copy(passed_h[a], passed.at[a], 18)
+
+    wait(gsum.at[1], 0)
+    for i in kinds_in:
+        wait(vin.at[i], 3 + i)
+        if i == 0:
+            wait(gsum.at[0], 1)
+        part = columns(gsum, (0, every), i) if i < 3 else gsum[1, :, (i - 3) * hc : (i - 2) * hc]
+        new = adam_step(vin[i, 0], vin[i, 1], vin[i, 2], part, 0.5 * D ** (-0.5), DECAY)
+        for a in range(3):
+            rin[i, a] = new[a]
+            copy(rin.at[i, a], in_o[a].at[i], 19)
+    wait(small, 15)
+    wait(vbias, 16)
+    wait(vvec, 17)
     for i in range(6):
-        new = adam_step(wv[i], m1_v[i], m2_v[i], small[i : i + 1, :], SMALL_RATE, 0.0)
-        for ref, value in zip(outs[9:12], new):
-            ref[i] = value
+        new = adam_step(vvec[0, i], vvec[1, i], vvec[2, i], small[i : i + 1, :], SMALL_RATE, 0.0)
+        for a in range(3):
+            rvec[a, i] = new[a]
         if i < 2:
-            heads = [(3 * h + 2 * i) * HD for h in range(hc // HD)]
-            part = jnp.concatenate([small[7:8, at : at + HD] for at in heads], 1)
+            part = columns(small, (slice(7, 8),), 2 * i)
         else:
             part = small[6:7, (i - 2) * hc : (i - 1) * hc]
-        new = adam_step(wb[i], m1_b[i], m2_b[i], part, SMALL_RATE, 0.0)
-        for ref, value in zip(outs[6:9], new):
-            ref[i] = value
-
-    for load in loads_g:
-        load.wait()
-    for i in range(7):
-        for load in loads_in[i]:
-            load.wait()
-        if i < 3:
-            heads = [(3 * h + i) * HD for h in range(hc // HD)]
-            part = jnp.concatenate([gsum[0, :, at : at + HD] for at in heads], 1)
-        else:
-            part = gsum[1, :, (i - 3) * hc : (i - 2) * hc]
-        new = adam_step(vin[0][i], vin[1][i], vin[2][i], part, 0.5 * D ** (-0.5), DECAY)
-        for v, value, o in zip(rin, new, outs[0:3]):
-            v[i] = value
-            done.append(copy(v.at[i], o.at[i]))
+        new = adam_step(vbias[0, i], vbias[1, i], vbias[2, i], part, SMALL_RATE, 0.0)
+        for a in range(3):
+            rbias[a, i] = new[a]
+    for a in range(3):
+        copy(rbias.at[a], bias_o[a], 20)
+        copy(rvec.at[a], vec_o[a], 21)
+    wait(gsum.at[2], 2)
     for i in range(5):
-        for load in loads_out[i]:
-            load.wait()
-        b, at = (0, 3 * hc) if i < 1 else (2, (i - 1) * hc)
-        part = jnp.transpose(gsum[b, :, at : at + hc])
-        new = adam_step(vout[0][i], vout[1][i], vout[2][i], part, 2.0 * D ** (-0.5), DECAY)
-        for v, value, o in zip(rout, new, outs[3:6]):
-            v[i] = value
-            done.append(copy(v.at[i], o.at[i]))
-    for load in passing:
-        load.wait()
-    done += [copy(pass_out, out_o), copy(pass_grad, grad_o)]
-    for made in done:
-        made.wait()
+        wait(vout.at[i], 10 + i)
+        part = columns(gsum, (0, every), 3) if i == 0 else gsum[2, :, (i - 1) * hc : i * hc]
+        part = jnp.transpose(part)
+        new = adam_step(vout[i, 0], vout[i, 1], vout[i, 2], part, 2.0 * D ** (-0.5), DECAY)
+        for a in range(3):
+            rout[i, a] = new[a]
+            copy(rout.at[i, a], out_o[a].at[i], 22)
+    wait(passed, 18)
+    for a in range(2):
+        copy(passed.at[a], passed_o[a], 23)
+    for ref, sem in ((rin, 19), (rbias, 20), (rvec, 21), (rout, 22), (passed, 23)):
+        wait(ref, sem)
 
 
 def run_adam(*operands):
     hc = operands[4].shape[2]
-    shapes = [operands[0], operands[1], *operands[4:16]]
+    out_rows, _, g_sum, small = operands[0:4]
+    shapes = [out_rows, out_rows, *operands[4:16]]
     hbm = pl.BlockSpec(memory_space=pl.ANY)
-    whole = pl.BlockSpec(memory_space=pltpu.VMEM)
-    big_in, big_out = operands[4].shape, operands[7].shape
+    kinds_in, kinds_out = operands[4].shape, operands[7].shape
+    small_bias, small_vec = operands[10].shape, operands[13].shape
+    big = [
+        pltpu.VMEM((kinds_in[0], 3, *kinds_in[1:]), F32),
+        pltpu.VMEM((kinds_out[0], 3, *kinds_out[1:]), F32),
+        pltpu.VMEM((3, *small_bias), F32),
+        pltpu.VMEM((3, *small_vec), F32),
+    ]
     return pl.pallas_call(
         functools.partial(adam_kernel, hc),
         out_shape=[jax.ShapeDtypeStruct(a.shape, F32) for a in shapes],
-        in_specs=[hbm] * 3 + [whole] + [hbm] * 6 + [whole] * 6,
-        out_specs=[hbm] * 8 + [whole] * 6,
-        scratch_shapes=[pltpu.VMEM(big_in, F32)] * 3
-        + [pltpu.VMEM(big_out, F32)] * 3
-        + [pltpu.VMEM(big_in, F32)] * 3
-        + [pltpu.VMEM(big_out, F32)] * 3
-        + [pltpu.VMEM(operands[2].shape, F32)]
-        + [pltpu.VMEM(operands[0].shape, F32)] * 2
-        + [pltpu.SemaphoreType.DMA((79,))],
+        in_specs=[hbm] * 16,
+        out_specs=[hbm] * 14,
+        scratch_shapes=big * 2
+        + [pltpu.VMEM(g_sum.shape, F32), pltpu.VMEM(small.shape, F32)]
+        + [pltpu.VMEM((2, *out_rows.shape), F32), pltpu.SemaphoreType.DMA((24,))],
         compiler_params=pltpu.CompilerParams(vmem_limit_bytes=62 << 20),
         name="adam",
     )(*operands)

time: 115 us -> 109 us (0.948)
  Pallas kernels: 114 us -> 107 us
    pallas_call x1, Pallas kernels: 107 us -> 102 us  [run_block(): pl.pallas_call(functools.partial(block_kernel, sizes), out_shape=(jax.Sha...]
    pallas_call x1, Pallas kernels: 7.07 us -> 5.41 us  [run_adam(): pl.pallas_call(functools.partial(adam_kernel, hc), out_shape=[jax.ShapeDt...]
where the time goes in v4:
time: 109 us; the launch traced here: 108 us
  Pallas kernels  107 us (98%)
    pallas_call x1, Pallas kernels, run_block(): pl.pallas_call(functools.partial(block_kernel, sizes), out_shape=(jax.Sha...  102 us
    pallas_call x1, Pallas kernels, run_adam(): pl.pallas_call(functools.partial(adam_kernel, hc), out_shape=[jax.ShapeDt...  5.41 us

profile of v4, /device:TPU:0, one launch (start us, length us, event | category | flops | bytes accessed | tf_op | source)
XLA Modules:
  0.0 108.3 jit_solution(1181714597939838263)
XLA Ops:
  0.6 102.0 %block.1 = (f32[256,768]{1,0:T(8,128)}, f32[256,768]{1,0:T(8,128)}, f32[3,96,768]{2,1,0:T(8,128)}, f32[8,768]{1,0:T(8,128)}) custom-call(f32[1024,768]{1,0:T(8,128)} %resid_h.1, f32[1024,768]{1,0:T(8,128)} %cot_h.1, f32[7,96,192]{2,1,0:T(8,128)} %bitcast.36, f32[5,192,96]{2,1,0:T(8,128)} %bitcast.38, f32[6,1,192]{2,1,0:T(1,128)} %bitcast.46, ...), custom_call_target="tpu_custom_call" | custom-call | tf_op jit(solution)/shard_map/block/pallas_call | solution.py:1296
  102.7 5.4 %adam.1 = (f32[256,768]{1,0:T(8,128)}, f32[256,768]{1,0:T(8,128)}, f32[7,96,192]{2,1,0:T(8,128)}, f32[7,96,192]{2,1,0:T(8,128)}, f32[7,96,192]{2,1,0:T(8,128)}, ...) custom-call(f32[256,768]{1,0:T(8,128)} %get-tuple-element.32.refs_0_, ...), custom_call_target="tpu_custom_call" | custom-call | tf_op jit(solution)/shard_map/adam/pallas_call | solution.py:1407

commit v5 on v4

--- a/solution.py
+++ b/solution.py
@@ -409,12 +409,16 @@
     xr,
     zs,
     zr,
+    side_r,
+    side_s,
+    side_xs,
+    side_xr,
     gsum,
     sm,
+    smp,
     smx,
     smz,
     smy,
-    smc,
     lsem,
     ssem,
     rsem,
@@ -451,7 +455,8 @@
         )
 
     barrier = pltpu.get_barrier_semaphore()
-    peers = [x_dev, c_dev, y_dev, z_dev(1), z_dev(2), z_dev(3)]
+    cross_dev = (dp + 1 - 2 * x, ten + 1 - 2 * c)
+    peers = [x_dev, c_dev, y_dev, cross_dev, z_dev(1), z_dev(2), z_dev(3)]
     for dev in peers:
         pl.semaphore_signal(barrier, inc=1, device_id=dev, device_id_type=MESH_IDS)
     load_win = pltpu.make_async_copy(win_h, win, lsem.at[2])
@@ -501,6 +506,10 @@
     def ag_mid(u):
         return ag_copy(u, z, 4, 3 * u + 1, mid_dev)
 
+    def ag_end_far(u, i):
+        dev = (2 * owner_z[i] + x, ten)
+        return ag_copy(u, z, 4, 3 * u + 2, dev)
+
     def ag_onward(u, i):
         if i == 0:
             return ag_copy(u, owner_z[0], 4, 3 * u + 2, mid_dev)
@@ -533,7 +542,8 @@
         @pl.when(is_mid == 1)
         def _():
             ag_arrive(u, i)
-            ag_onward(u, i).start()
+            if u > 1 or i == 1:
+                ag_onward(u, i).start()
             ag_x(u, 1 + i).start()
 
     def mid_onward(u, i):
@@ -553,6 +563,10 @@
     def ag_drain(u):
         ag_bytes(u, 4, u, 12 + u).wait_send()
 
+        if u < 2:
+            ag_bytes(u, 3, 4 + u, 12 + u).wait_send()
+            return
+
         @pl.when(is_end == 1)
         def _():
             ag_bytes(u, 1, 4 + u, 12 + u).wait_send()
@@ -568,8 +582,10 @@
 
     @pl.when(is_end == 1)
     def _():
-        for u in range(4):
+        for u in range(2):
             ag_pair(u).start()
+            ag_end_far(u, 2).start()
+            ag_end_far(u, 1).start()
 
     load_resid.wait()
     load_cot.wait()
@@ -592,16 +608,26 @@
         return carry
 
     lax.fori_loop(0, tokens // 128, first_norm, 0)
-    for u, i in ((0, 0), (0, 1), (1, 0), (1, 1), (0, 2), (1, 2)):
+    for u, i in ((0, 0), (0, 1), (1, 0), (1, 1)):
         pump_mid(u, i)
-    for u, i in ((0, 0), (1, 0), (0, 1), (1, 1), (0, 2), (1, 2)):
+    mid_start(2)
+    pump_mid(0, 2)
+    pump_mid(1, 2)
+    pump_end(0, 0)
+    pump_end(1, 0)
+
+    @pl.when(is_end == 1)
+    def _():
+        ag_pair(2).start()
+
+    for u, i in ((0, 2), (0, 1), (1, 2), (1, 1)):
         pump_end(u, i)
+
+    @pl.when(is_end == 1)
+    def _():
+        ag_pair(3).start()
+
     ag_x(2, 0).start()
-    mid_start(2)
-    pump_mid(2, 0)
-    ag_x(3, 0).start()
-    mid_start(3)
-    mid_onward(3, 0)
 
     sm[...] = jnp.zeros_like(sm)
     sm[5:6, :] = jnp.sum(dmlp[own, :].astype(F32), 0, keepdims=True)
@@ -637,7 +663,10 @@
     for r in range(tokens // 256):
         project_pair(r)
     pump_end(2, 0)
+    pump_mid(2, 0)
     pump_mid(2, 1)
+    ag_x(3, 0).start()
+    mid_start(3)
 
     def attend(i, which_heads):
         first, last_row = i * quarter, (i + 1) * quarter
@@ -719,13 +748,19 @@
 
         lax.fori_loop(0, 2, step, 0)
 
-    def rs_quad(k, compute, held):
+    def rs_quad(k, compute, held, prepare=None):
         for half in range(2):
             rs_core(k - 2, half).wait_send()
 
         def step(s, carry):
             half, odd = lax.div(s, 2), lax.rem(s, 2)
             yq = half * y + (1 - half) * (1 - y)
+            if prepare is not None:
+
+                @pl.when(s == 3)
+                def _():
+                    prepare()
+
             part = compute(2 * yq + lax.rem(1 - odd + c, 2))
 
             @pl.when(odd == 0)
@@ -779,23 +814,19 @@
         attend_quarter(which, (0, 1, 2))
         return proj(which)
 
-    def near_pumps(s):
-        @pl.when(s == 1)
-        def _():
-            pump_end(2, 2)
-            pump_end(3, 0)
-            pump_mid(3, 2)
-
     lax.fori_loop(0, 2, far_early, 0)
-    pump_mid(2, 2)
-    mid_x(3, 1)
+    mid_onward(3, 0)
     ag_finish(1)
     for r in range(tokens // 256):
         project_last(r)
     rs_pair(0, False, far_proj)
     pump_end(2, 1)
+    pump_mid(2, 2)
+    mid_x(3, 1)
+    rs_pair(0, True, near_proj)
+    pump_end(2, 2)
+    pump_end(3, 0)
     pump_mid(3, 1)
-    rs_pair(0, True, near_proj, prepare=near_pumps)
 
     def q_rows(ref, which, hh):
         return ref.at[rows_at(which * quarter + hh * (quarter // 2), quarter // 2, quarter // 2), :]
@@ -810,7 +841,7 @@
 
     def qg_f(g, ref, hh):
         src = q_rows(ref, ten + 2 - 4 * y, hh)
-        return rcopy(src, src, 23, 38 + g, c_dev)
+        return rcopy(src, src, 23, 38 + 2 * g + hh, c_dev)
 
     def qg_start(g, ref, hh):
         qg_y(g, ref, hh).start()
@@ -823,17 +854,33 @@
     def qg_near(g, ref):
         qg_rows(ref, quarter, 22, 36 + g).wait_recv()
 
-    def qg_far(g, ref):
-        for hh in range(2):
-            qg_y(g, ref, hh).wait_recv()
-            qg_f(g, ref, hh).start()
-
-    def qg_last(g, ref):
-        qg_rows(ref, quarter, 23, 38 + g).wait_recv()
-
-    pump_end(3, 1)
+    def qg_far(g, ref, hh):
+        qg_y(g, ref, hh).wait_recv()
+        qg_f(g, ref, hh).start()
+
+    def qg_last(g, ref, hh):
+        qg_f(g, ref, hh).wait_recv()
+
+    def far_rows(g, ref, compute, between=None):
+        def step(hh, carry):
+            if between is not None:
+
+                @pl.when(hh == 1)
+                def _():
+                    between()
+
+            qg_far(g, ref, hh)
+            compute(2 * (1 - y) + c, hh)
+            qg_last(g, ref, hh)
+            compute(2 * (1 - y) + 1 - c, hh)
+            return carry
+
+        lax.fori_loop(0, 2, step, 0)
 
     for hh in range(2):
+        if hh == 1:
+            pump_end(3, 1)
+            pump_mid(3, 2)
         half = halves[hh]
         middle = mid[half, :] + BRANCH_SCALE * (rs_result(0, hh) + vec[4])
         mid[half, :] = middle
@@ -851,8 +898,10 @@
 
     bias_up = jnp.concatenate([bias[2 + i] for i in range(4)], 1)
 
-    def forward_units(which):
+    def forward_units(which, hh=None):
         rows = rows_at(which * quarter, quarter, quarter)
+        if hh is not None:
+            rows = rows_at(which * quarter + hh * (quarter // 2), quarter // 2, quarter // 2)
         hq = hidden[rows, :]
         for t in range(width // 256):
             cols = slice(t * 256, (t + 1) * 256)
@@ -881,11 +930,13 @@
 
         lax.fori_loop(0, width // 256, tile, 0)
 
+    g_units = (*units[0:3], (2, slice(0, half_cols)))
+    right_half = slice(half_cols, width)
 
     def gx(u, zi):
-        b, cols = units[u]
+        b, cols = g_units[u]
         src = gmat.at[b, rows_at((2 * zi + 1 - x) * shard, shard, shard), cols]
-        return rcopy(src, xr.at[b, zi, :, cols], 8 + u, 40 + 4 * u + zi, x_dev)
+        return rcopy(src, xr.at[b, zi, :, cols], 8 + u, 42 + 4 * u + zi, x_dev)
 
     def line_to(i):
         if i == 0:
@@ -893,19 +944,14 @@
         return (2 * (is_end * owner_z[0] + is_mid * owner_z[i]) + x, ten), is_end * i + is_mid * 3
 
     def gz(u, i):
-        b, cols = units[u]
-        if u < 2:
-            src, dst = zs.at[b, i - 1, :, cols], zr.at[b, i - 1, :, cols]
-            return rcopy(src, dst, 12 + u, 56 + u, z_dev(i))
+        b, cols = g_units[u]
         dev, slot = line_to(i)
-        return rcopy(
-            zs.at[b, i, :, cols], zr.at[b, slot, :, cols], 12 + u, 58 + 4 * (u - 2) + slot, dev
-        )
+        return rcopy(zs.at[b, i, :, cols], zr.at[b, slot, :, cols], 12 + u, 58 + 4 * u + slot, dev)
 
     def gz_arrive(u, slot):
-        b, cols = units[u]
+        b, cols = g_units[u]
         ref = zr.at[b, slot, :, cols]
-        rcopy(ref, ref, 12 + u, 58 + 4 * (u - 2) + slot, x_dev).wait_recv()
+        rcopy(ref, ref, 12 + u, 58 + 4 * u + slot, x_dev).wait_recv()
 
     def g_start(u):
         @pl.when(is_end == 1)
@@ -921,18 +967,13 @@
         gx(u, z).start()
 
     def x_sum(u, zo):
-        b, cols = units[u]
+        b, cols = g_units[u]
         gx(u, zo).wait_recv()
         mine_x = gmat[b, rows_at((2 * zo + x) * shard, shard, shard), cols].astype(F32)
         return mine_x + xr[b, zo, :, cols].astype(F32)
 
-    def g_pump(u, j):
-        b, cols = units[u]
-        zs[b, j - 1, :, cols] = x_sum(u, z_other(j)).astype(BF16)
-        gz(u, j).start()
-
     def end_pump(u, i):
-        b, cols = units[u]
+        b, cols = g_units[u]
 
         @pl.when(is_end == 1)
         def _():
@@ -940,7 +981,7 @@
             gz(u, i).start()
 
     def mid_pump(u, i):
-        b, cols = units[u]
+        b, cols = g_units[u]
 
         @pl.when(is_mid == 1)
         def _():
@@ -952,29 +993,72 @@
             gz(u, i).start()
 
     def g_finish(u):
-        b, cols = units[u]
+        b, cols = g_units[u]
         total = x_sum(u, z)
-        if u < 2:
-            three = zr.at[b, 0:3, :, cols]
-            rcopy(three, three, 12 + u, 56 + u, x_dev).wait_recv()
-            for j in range(3):
-                total = total + zr[b, j, :, cols].astype(F32)
-        else:
-            for slot in (0, 3):
-                gz_arrive(u, slot)
-                total = total + zr[b, slot, :, cols].astype(F32)
+        for slot in (0, 3):
+            gz_arrive(u, slot)
+            total = total + zr[b, slot, :, cols].astype(F32)
         gsum[b, :, cols] = total
-        g_out(u).start()
+        if u < 3:
+            g_out(u).start()
 
     def g_out(u):
         b, cols = units[u]
         return pltpu.make_async_copy(gsum.at[b, :, cols], gsum_o.at[b, :, cols], lsem.at[4 + u])
 
     def g_drain(u):
-        b, cols = units[u]
+        b, cols = g_units[u]
         rcopy(xr.at[b, :, :, cols], xr.at[b, :, :, cols], 8 + u, 56, x_dev).wait_send()
         rcopy(zs.at[b, :, :, cols], zs.at[b, :, :, cols], 12 + u, 56, x_dev).wait_send()
         g_out(u).wait()
+
+    def side_rows(zo):
+        return gmat.at[2, rows_at(zo * 2 * shard, 2 * shard, 2 * shard), right_half]
+
+    def side_copy(src, i):
+        dev, slot = line_to(i)
+        return rcopy(src, side_r.at[slot], 28, 78 + slot, dev)
+
+    def side_arrive(slot):
+        rcopy(side_r.at[slot], side_r.at[slot], 28, 78 + slot, x_dev).wait_recv()
+
+    def side_start():
+        @pl.when(is_end == 1)
+        def _():
+            for i in (2, 1):
+                side_copy(side_rows(owner_z[i]), i).start()
+
+        side_copy(side_rows(owner_z[0]), 0).start()
+
+    def side_middle():
+        @pl.when(is_mid == 1)
+        def _():
+            for i in (2, 1):
+                side_arrive(i)
+                mine_z = gmat[2, rows_at(owner_z[i] * 2 * shard, 2 * shard, 2 * shard), right_half]
+                side_s[i - 1] = (mine_z.astype(F32) + side_r[i].astype(F32)).astype(BF16)
+                side_copy(side_s.at[i - 1], i).start()
+
+    def side_x():
+        return rcopy(side_xs, side_xr, 29, 82, x_dev)
+
+    def side_cross():
+        side_arrive(0)
+        side_arrive(3)
+
+        def total(xi):
+            at = rows_at(xi * shard, shard, shard)
+            got = gmat[2, rows_at((2 * z + xi) * shard, shard, shard), right_half].astype(F32)
+            return got + side_r[0, at, :].astype(F32) + side_r[3, at, :].astype(F32)
+
+        side_xs[...] = total(1 - x).astype(BF16)
+        side_x().start()
+        gsum[2, :, right_half] = total(x)
+
+    def side_finish():
+        side_x().wait_recv()
+        gsum[2, :, right_half] = gsum[2, :, right_half] + side_xr[...].astype(F32)
+        g_out(3).start()
 
     def backward_units(which):
         rows = rows_at(which * quarter, quarter, quarter)
@@ -1004,21 +1088,12 @@
     for t in range(width // 256):
         cols = slice(t * 256, (t + 1) * 256)
         normed_t[cols, :] = jnp.transpose(normed[:, cols])
-    qg_far(0, hidden)
-
-    def far_units(s, carry):
-        @pl.when(s == 1)
-        def _():
-            qg_last(0, hidden)
-
-        forward_units(2 * (1 - y) + lax.rem(s + c, 2))
-        return carry
-
     def down_gradient():
         grad_block(2, dmlp, act_s, False)
         g_start(3)
-
-    lax.fori_loop(0, 2, far_units, 0)
+        side_start()
+
+    far_rows(0, hidden, forward_units)
     ag_finish(3)
     rs_pair(1, False, backward_units, filler=down_gradient)
     rs_pair(1, True, backward_units)
@@ -1026,12 +1101,7 @@
     g_start(2)
     end_pump(3, 2)
     mid_pump(3, 0)
-    rs_quad(2, branch, fin.at[0])
-    end_pump(3, 1)
-    quad_far(2, fin.at[0])
-    quad_near(2)
-
-    for hh in range(2):
+    def second_norm_back(hh):
         half = halves[hh]
         mine_h = rows_at(ten * quarter + hh * (quarter // 2), quarter // 2, quarter // 2)
         d_hidden = rs_result(1, hh)
@@ -1050,10 +1120,22 @@
         sm[4:5, :] = sm[4:5, :] + jnp.sum(d_attn.astype(F32), 0, keepdims=True)
         qg_start(1, dattn, hh)
 
-    def attend_back(i, which_heads):
+    rs_quad(2, branch, fin.at[0])
+    second_norm_back(0)
+    end_pump(3, 1)
+    quad_far(2, fin.at[0])
+    quad_near(2)
+    side_middle()
+    end_pump(3, 0)
+    second_norm_back(1)
+    rs_y_start(2)
+
+    def attend_back(i, which_heads, hh=None):
         first, last_row = i * quarter, (i + 1) * quarter
         rows = slice(first, last_row)
-        got = {}
+        if hh is not None:
+            rows = rows_at(first + hh * (quarter // 2), quarter // 2, quarter // 2)
+        got, kept = {}, {}
         for h in which_heads:
             at = h // 2
             tile = slice(at * 128, (at + 1) * 128)
@@ -1065,8 +1147,14 @@
             d_probs = mm(d_scaled, v_s[at, 0:last_row, :], NT)
             d_scores = (expo.astype(F32) * (d_probs - inner)).astype(BF16)
             got[h] = mm(d_scores, k_s[at, 0:last_row, :]) * eighth
-            dk_s[at, :, 0:last_row] = dk_s[at, :, 0:last_row] + mm(q_s[h, rows, :], d_scores, TN)
-            dv_s[at, :, 0:last_row] = dv_s[at, :, 0:last_row] + mm(d_scaled, expo, TN)
+            kept[h] = (d_scores, d_scaled, expo)
+        for at, group in enumerate(((0, 1), (2,))):
+            if group[0] not in got:
+                continue
+            queries = jnp.concatenate([q_s[h, rows, :] for h in group], 0)
+            d_s, d_o, exps = [jnp.concatenate([kept[h][i] for h in group], 0) for i in range(3)]
+            dk_s[at, :, 0:last_row] = dk_s[at, :, 0:last_row] + mm(queries, d_s, TN)
+            dv_s[at, :, 0:last_row] = dv_s[at, :, 0:last_row] + mm(d_o, exps, TN)
         if 0 in got:
             dqkv[rows, 0:128] = jnp.where(low_half, got[0], got[1]).astype(BF16)
         if 2 in got:
@@ -1091,16 +1179,19 @@
 
         lax.fori_loop(0, 2, step, 0)
 
+    def back_far(which, hh):
+        rows = rows_at(which * quarter + hh * (quarter // 2), quarter // 2, quarter // 2)
+        dmix[rows, :] = mm(dattn[rows, :], w[0, :, 512:768]).astype(BF16)
+        for i in range(tokens // quarter):
+
+            @pl.when(which == i)
+            def _():
+                attend_back(i, (0, 1), hh)
+
     def near_ready(s):
         @pl.when(s == 1)
         def _():
             qg_near(1, dattn)
-
-    def far_ready(s):
-        @pl.when(s == 1)
-        def _():
-            qg_last(1, dattn)
-            end_pump(2, 1)
 
     def keys_values(at):
         if at == 0:
@@ -1122,30 +1213,31 @@
             gmat[0, cols, 512:768] = (g_qkv[:, 128:384] + gproj[cols, :]).astype(BF16)
         gx(u, zo).start()
 
-    def zero_unit(u):
+    def zero_unit(u, steps):
         def step(s, carry):
             odd, half = lax.rem(s, 2), lax.div(s, 2)
-            early = (1 - odd) * z_other(3) + odd * z_other(2)
-            late = (1 - odd) * z_other(1) + odd * z
+            first = is_end * owner_z[2] + is_mid * owner_z[0]
+            second = is_end * owner_z[1] + is_mid * owner_z[2]
+            third = is_end * owner_z[0] + is_mid * owner_z[1]
+            early = (1 - odd) * first + odd * second
+            late = (1 - odd) * third + odd * z
             zero_rows(u, (1 - half) * early + half * late)
             return carry
 
-        lax.fori_loop(0, 4, step, 0)
-
-    end_pump(3, 0)
+        lax.fori_loop(*steps, step, 0)
+
+    back_quarters(True, (0, 1, 2), True, near_ready)
     mid_pump(3, 2)
-    back_quarters(True, (0, 1, 2), True, near_ready)
+    mid_pump(2, 0)
+    end_pump(2, 2)
+    end_pump(2, 1)
     mid_pump(3, 1)
-    end_pump(2, 2)
-    mid_pump(2, 0)
-    qg_far(1, dattn)
-    rs_y_start(2)
-    back_quarters(False, (0, 1), True, far_ready)
+    far_rows(1, dattn, back_far, side_cross)
     keys_values(0)
-    zero_unit(0)
-    gproj[...] = jnp.transpose(mm(mixed[...], dattn[...], TN))
+    zero_unit(0, (0, 4))
     end_pump(2, 0)
     mid_pump(2, 2)
+    gproj[...] = jnp.transpose(mm(mixed[...], dattn[...], TN))
     back_quarters(False, (2,), False)
     keys_values(1)
     mid_pump(2, 1)
@@ -1160,34 +1252,44 @@
         sm[7:8, :] = sm[7:8, :] + jnp.sum(d_low.astype(F32), 0, keepdims=True)
         return part
 
-    rs_quad(3, first_back, xhat2)
-
-    small_x = rcopy(sm, smx, 24, 66, x_dev)
-    small_x.start()
+    end_pump(0, 2)
+    mid_pump(0, 0)
+    rs_quad(3, first_back, xhat2, lambda: end_pump(0, 1))
+
+    small_c = rcopy(sm, smp, 27, 77, c_dev)
+    small_c.start()
     quad_far(3, xhat2)
     rs_y_start(3)
-    g_pump(0, 3)
-    zero_unit(1)
+    small_c.wait_recv()
+    smx[0, 0:6, :] = sm[0:6, :] + smp[0:6, :]
+    smx[0, 6:8, :] = smp[6:8, :]
+    small_x = rcopy(smx.at[0], smx.at[1], 24, 74, cross_dev)
+    small_x.start()
+    end_pump(0, 0)
+    zero_unit(1, (0, 4))
     quad_near(3)
-    g_pump(0, 2)
+    mid_pump(0, 2)
     small_x.wait_recv()
-    smz[z] = sm[...] + smx[...]
+    smz[z, 0:6, :] = smx[0, 0:6, :] + smx[1, 0:6, :]
+    smz[z, 6:8, :] = sm[6:8, :] + smx[1, 6:8, :]
 
     def small_z(j):
-        return rcopy(smz.at[z], smz.at[z], 25, 67, z_dev(j))
+        return rcopy(smz.at[z], smz.at[z], 25, 75, z_dev(j))
 
     for j in (3, 2, 1):
         small_z(j).start()
-    g_pump(0, 1)
+    mid_pump(0, 1)
     g_finish(3)
+    side_finish()
     g_finish(2)
     for hh in range(2):
         half = halves[hh]
         mid[half, :] = mid[half, :] + BRANCH_SCALE * (rs_result(2, hh) + vec[5])
     put_out = pltpu.make_async_copy(mid, out_o, lsem.at[8])
     put_out.start()
-    g_pump(1, 3)
-    g_pump(1, 2)
+    end_pump(1, 2)
+    mid_pump(1, 0)
+    end_pump(1, 1)
 
     def first_norm_back(hh):
         half = halves[hh]
@@ -1202,28 +1304,32 @@
         )
 
     first_norm_back(0)
-    g_pump(1, 1)
+    end_pump(1, 0)
+    three = rcopy(smz.at[0:3], smz.at[0:3], 25, 75, x_dev)
+    three.wait_recv()
+    smy[0] = (smz[0] + smz[1]) + (smz[2] + smz[3])
+    small_y = rcopy(smy.at[0], smy.at[1], 26, 76, y_dev)
+    small_y.start()
+    mid_pump(1, 2)
     first_norm_back(1)
     put_grad = pltpu.make_async_copy(xhat2, grad_o, lsem.at[9])
     put_grad.start()
-    three = rcopy(smz.at[0:3], smz.at[0:3], 25, 67, x_dev)
-    three.wait_recv()
-    smy[0] = (smz[0] + smz[1]) + (smz[2] + smz[3])
-    small_y = rcopy(smy.at[0], smy.at[1], 26, 68, y_dev)
-    small_y.start()
+    mid_pump(1, 1)
     g_finish(0)
     small_y.wait_recv()
-    smc[0] = smy[0] + smy[1]
-    small_c = rcopy(smc.at[0], smc.at[1], 27, 69, c_dev)
-    small_c.start()
+    small_c.wait_send()
+    sm[0:6, :] = smy[0, 0:6, :] + smy[1, 0:6, :]
+    sm[6:8, :] = smy[0, 6:8, :]
+    put_small = pltpu.make_async_copy(sm, small_o, lsem.at[10])
+    put_small.start()
     g_finish(1)
-    small_c.wait_recv()
-    small_o[0:6, :] = smc[0, 0:6, :] + smc[1, 0:6, :]
-    small_o[6:8, :] = smy[0, 6:8, :]
 
     for u in range(4):
         ag_drain(u)
         g_drain(u)
+    three_sides = side_r.at[0:3]
+    rcopy(three_sides, three_sides, 28, 76, x_dev).wait_send()
+    side_x().wait_send()
     rcopy(ysend, yrecv, 20, 24, y_dev).wait_send()
     for k in (2, 3):
         for half in range(2):
@@ -1233,9 +1339,9 @@
     small_x.wait_send()
     three.wait_send()
     small_y.wait_send()
-    small_c.wait_send()
     put_out.wait()
     put_grad.wait()
+    put_small.wait()
 
 
 def run_block(resid, cotangent, win, wout, bias, vec, rows, n_dp):
@@ -1282,15 +1388,19 @@
         vm((3, 4, rows, width), BF16),
         vm((3, 3, rows, width), BF16),
         vm((3, 4, rows, width), BF16),
+        vm((4, 2 * rows, width // 2), BF16),
+        vm((2, 2 * rows, width // 2), BF16),
+        vm((rows, width // 2), BF16),
+        vm((rows, width // 2), BF16),
         vm((3, rows, width), F32),
         vm((8, width), F32),
         vm((8, width), F32),
+        vm((2, 8, width), F32),
         vm((4, 8, width), F32),
         vm((2, 8, width), F32),
-        vm((2, 8, width), F32),
-        pltpu.SemaphoreType.DMA((10,)),
-        pltpu.SemaphoreType.DMA((28,)),
-        pltpu.SemaphoreType.DMA((70,)),
+        pltpu.SemaphoreType.DMA((11,)),
+        pltpu.SemaphoreType.DMA((30,)),
+        pltpu.SemaphoreType.DMA((83,)),
     ]
     whole = pl.BlockSpec(memory_space=pltpu.VMEM)
     return pl.pallas_call(
@@ -1302,7 +1412,7 @@
             jax.ShapeDtypeStruct((8, width), F32),
         ),
         in_specs=[pl.BlockSpec(memory_space=pl.ANY)] * 4 + [whole] * 2,
-        out_specs=[pl.BlockSpec(memory_space=pl.ANY)] * 3 + [whole],
+        out_specs=[pl.BlockSpec(memory_space=pl.ANY)] * 4,
         scratch_shapes=scratch,
         compiler_params=pltpu.CompilerParams(
             collective_id=1, has_side_effects=True, vmem_limit_bytes=62 << 20

time: 109 us -> 101 us (0.927)
  Pallas kernels: 107 us -> 100 us
    pallas_call x1, Pallas kernels: 102 us -> 94.7 us  [run_block(): pl.pallas_call(functools.partial(block_kernel, sizes), out_shape=(jax.Sha...]
where the time goes in v5:
time: 101 us
  Pallas kernels  100 us (99%)
    pallas_call x1, Pallas kernels, run_block(): pl.pallas_call(functools.partial(block_kernel, sizes), out_shape=(jax.Sha...  94.7 us
    pallas_call x1, Pallas kernels, run_adam(): pl.pallas_call(functools.partial(adam_kernel, hc), out_shape=[jax.ShapeDt...  5.41 us

profile of v5, /device:TPU:0, one launch (start us, length us, event | category | flops | bytes accessed | tf_op | source)
XLA Modules:
  0.0 100.9 jit_solution(4263102098020424809)
XLA Ops:
  0.6 94.7 %block.1 = (f32[256,768]{1,0:T(8,128)}, f32[256,768]{1,0:T(8,128)}, f32[3,96,768]{2,1,0:T(8,128)}, f32[8,768]{1,0:T(8,128)}) custom-call(f32[1024,768]{1,0:T(8,128)} %resid_h.1, f32[1024,768]{1,0:T(8,128)} %cot_h.1, f32[7,96,192]{2,1,0:T(8,128)} %bitcast.36, f32[5,192,96]{2,1,0:T(8,128)} %bitcast.38, f32[6,1,192]{2,1,0:T(1,128)} %bitcast.46, ...), custom_call_target="tpu_custom_call" | custom-call | tf_op jit(solution)/shard_map/block/pallas_call | solution.py:1406
  95.3 5.4 %adam.1 = (f32[256,768]{1,0:T(8,128)}, f32[256,768]{1,0:T(8,128)}, f32[7,96,192]{2,1,0:T(8,128)}, f32[7,96,192]{2,1,0:T(8,128)}, f32[7,96,192]{2,1,0:T(8,128)}, ...) custom-call(f32[256,768]{1,0:T(8,128)} %get-tuple-element.32.refs_0_, ...), custom_call_target="tpu_custom_call" | custom-call | tf_op jit(solution)/shard_map/adam/pallas_call | solution.py:1517

commit v6 on v5

--- a/solution.py
+++ b/solution.py
@@ -715,12 +715,10 @@
         for hh in range(2):
             rs_y(k, hh).start()
 
-    def rs_pair(k, near, compute, prepare=None, filler=None):
+    def rs_pair(k, near, compute):
         half = 1 if near else 0
         def step(s, carry):
             yq = y if near else 1 - y
-            if prepare is not None:
-                prepare(s)
             part = compute(2 * yq + lax.rem(1 - s + c, 2))
 
             @pl.when(s == 0)
@@ -730,14 +728,8 @@
 
             @pl.when(s == 1)
             def _():
-                if filler is not None:
-                    fin[(k + 1) % 3] = part
-                    filler()
-                    kept = fin[(k + 1) % 3]
-                else:
-                    kept = part
                 rs_core(k, half).wait_recv()
-                total = kept + crecv[k, half].astype(F32)
+                total = part + crecv[k, half].astype(F32)
                 if near:
                     fin[k % 3] = total
                 else:
@@ -748,19 +740,13 @@
 
         lax.fori_loop(0, 2, step, 0)
 
-    def rs_quad(k, compute, held, prepare=None):
+    def rs_quad(k, compute, held):
         for half in range(2):
             rs_core(k - 2, half).wait_send()
 
         def step(s, carry):
             half, odd = lax.div(s, 2), lax.rem(s, 2)
             yq = half * y + (1 - half) * (1 - y)
-            if prepare is not None:
-
-                @pl.when(s == 3)
-                def _():
-                    prepare()
-
             part = compute(2 * yq + lax.rem(1 - odd + c, 2))
 
             @pl.when(odd == 0)
@@ -1088,14 +1074,12 @@
     for t in range(width // 256):
         cols = slice(t * 256, (t + 1) * 256)
         normed_t[cols, :] = jnp.transpose(normed[:, cols])
-    def down_gradient():
-        grad_block(2, dmlp, act_s, False)
-        g_start(3)
-        side_start()
-
     far_rows(0, hidden, forward_units)
     ag_finish(3)
-    rs_pair(1, False, backward_units, filler=down_gradient)
+    rs_pair(1, False, backward_units)
+    grad_block(2, dmlp, act_s, False)
+    g_start(3)
+    side_start()
     rs_pair(1, True, backward_units)
     grad_block(1, hidden, dpre, None)
     g_start(2)
@@ -1254,7 +1238,8 @@
 
     end_pump(0, 2)
     mid_pump(0, 0)
-    rs_quad(3, first_back, xhat2, lambda: end_pump(0, 1))
+    rs_quad(3, first_back, xhat2)
+    end_pump(0, 1)
 
     small_c = rcopy(sm, smp, 27, 77, c_dev)
     small_c.start()
@@ -1315,20 +1300,10 @@
     put_grad = pltpu.make_async_copy(xhat2, grad_o, lsem.at[9])
     put_grad.start()
     mid_pump(1, 1)
-    g_finish(0)
-    small_y.wait_recv()
-    small_c.wait_send()
-    sm[0:6, :] = smy[0, 0:6, :] + smy[1, 0:6, :]
-    sm[6:8, :] = smy[0, 6:8, :]
-    put_small = pltpu.make_async_copy(sm, small_o, lsem.at[10])
-    put_small.start()
-    g_finish(1)
-
     for u in range(4):
         ag_drain(u)
-        g_drain(u)
     three_sides = side_r.at[0:3]
-    rcopy(three_sides, three_sides, 28, 76, x_dev).wait_send()
+    rcopy(three_sides, three_sides, 28, 78, x_dev).wait_send()
     side_x().wait_send()
     rcopy(ysend, yrecv, 20, 24, y_dev).wait_send()
     for k in (2, 3):
@@ -1338,10 +1313,21 @@
         qg_rows(hidden, 2 * quarter, send, 36).wait_send()
     small_x.wait_send()
     three.wait_send()
+    g_finish(0)
+    for u in (3, 2, 0):
+        g_drain(u)
+    small_y.wait_recv()
+    small_c.wait_send()
+    sm[0:6, :] = smy[0, 0:6, :] + smy[1, 0:6, :]
+    sm[6:8, :] = smy[0, 6:8, :]
+    put_small = pltpu.make_async_copy(sm, small_o, lsem.at[10])
+    put_small.start()
+    g_finish(1)
+
+    g_drain(1)
     small_y.wait_send()
-    put_out.wait()
-    put_grad.wait()
-    put_small.wait()
+    for made in (put_out, put_grad, put_small):
+        made.wait()
 
 
 def run_block(resid, cotangent, win, wout, bias, vec, rows, n_dp):
@@ -1443,6 +1429,9 @@
     kinds_in = (3, 4, 5, 6, 0, 1, 2)
     copy(gsum_h.at[1], gsum.at[1], 0)
     for i in kinds_in:
+        if i == 5:
+            for a in range(2):
+                copy(passed_h[a], passed.at[a], 18)
         for a in range(3):
             copy(in_h[a].at[i], vin.at[i, a], 3 + i)
         if i == 6:
@@ -1455,8 +1444,6 @@
     for i in range(5):
         for a in range(3):
             copy(out_h[a].at[i], vout.at[i, a], 10 + i)
-    for a in range(2):
-        copy(passed_h[a], passed.at[a], 18)
 
     wait(gsum.at[1], 0)
     for i in kinds_in:
@@ -1468,6 +1455,9 @@
         for a in range(3):
             rin[i, a] = new[a]
             copy(rin.at[i, a], in_o[a].at[i], 19)
+    wait(passed, 18)
+    for a in range(2):
+        copy(passed.at[a], passed_o[a], 23)
     wait(small, 15)
     wait(vbias, 16)
     wait(vvec, 17)
@@ -1494,9 +1484,6 @@
         for a in range(3):
             rout[i, a] = new[a]
             copy(rout.at[i, a], out_o[a].at[i], 22)
-    wait(passed, 18)
-    for a in range(2):
-        copy(passed.at[a], passed_o[a], 23)
     for ref, sem in ((rin, 19), (rbias, 20), (rvec, 21), (rout, 22), (passed, 23)):
         wait(ref, sem)
 

time: 101 us -> 99.2 us (0.982)
  Pallas kernels: 100 us -> 97.9 us
    pallas_call x1, Pallas kernels: 94.7 us -> 93.3 us  [run_block(): pl.pallas_call(functools.partial(block_kernel, sizes), out_shape=(jax.Sha...]
where the time goes in v6:
time: 99.2 us; the launch traced here: 98.7 us
  Pallas kernels  97.9 us (99%)
    pallas_call x1, Pallas kernels, run_block(): pl.pallas_call(functools.partial(block_kernel, sizes), out_shape=(jax.Sha...  93.3 us
    pallas_call x1, Pallas kernels, run_adam(): pl.pallas_call(functools.partial(adam_kernel, hc), out_shape=[jax.ShapeDt...  4.59 us

profile of v6, /device:TPU:0, one launch (start us, length us, event | category | flops | bytes accessed | tf_op | source)
XLA Modules:
  0.0 98.7 jit_solution(7951308722484610216)
XLA Ops:
  0.6 93.3 %block.1 = (f32[256,768]{1,0:T(8,128)}, f32[256,768]{1,0:T(8,128)}, f32[3,96,768]{2,1,0:T(8,128)}, f32[8,768]{1,0:T(8,128)}) custom-call(f32[1024,768]{1,0:T(8,128)} %resid_h.1, f32[1024,768]{1,0:T(8,128)} %cot_h.1, f32[7,96,192]{2,1,0:T(8,128)} %bitcast.36, f32[5,192,96]{2,1,0:T(8,128)} %bitcast.38, f32[6,1,192]{2,1,0:T(1,128)} %bitcast.46, ...), custom_call_target="tpu_custom_call" | custom-call | tf_op jit(solution)/shard_map/block/pallas_call | solution.py:1392
  93.9 4.6 %adam.1 = (f32[256,768]{1,0:T(8,128)}, f32[256,768]{1,0:T(8,128)}, f32[7,96,192]{2,1,0:T(8,128)}, f32[7,96,192]{2,1,0:T(8,128)}, f32[7,96,192]{2,1,0:T(8,128)}, ...) custom-call(f32[256,768]{1,0:T(8,128)} %get-tuple-element.32.refs_0_, ...), custom_call_target="tpu_custom_call" | custom-call | tf_op jit(solution)/shard_map/adam/pallas_call | solution.py:1504

commit v7 on v6

--- a/solution.py
+++ b/solution.py
@@ -367,14 +367,16 @@
     cot_h,
     win_h,
     wout_h,
-    bias,
-    vec,
+    bias_h,
+    vec_h,
     out_o,
     grad_o,
     gsum_o,
     small_o,
     win,
     wout,
+    bias,
+    vec,
     resid,
     cot,
     inv1,
@@ -465,8 +467,12 @@
     load_wout.start()
     load_resid = pltpu.make_async_copy(resid_h, resid, lsem.at[0])
     load_cot = pltpu.make_async_copy(cot_h, cot, lsem.at[1])
+    load_vec = pltpu.make_async_copy(vec_h, vec, lsem.at[11])
+    load_bias = pltpu.make_async_copy(bias_h, bias, lsem.at[12])
+    load_vec.start()
     load_resid.start()
     load_cot.start()
+    load_bias.start()
 
     mine = rows_at(dp * shard, shard, shard)
     load_win.wait()
@@ -477,8 +483,6 @@
     tiles += [out_t[0][:, pairs], win[1, :, last], out_t[0][:, last]]
     w[0, mine, :] = jnp.concatenate(tiles, 1).astype(BF16)
 
-    w[1, mine, :] = jnp.concatenate([win[3 + i] for i in range(4)], 1).astype(BF16)
-    w[2, mine, :] = jnp.concatenate(out_t[1:], 1).astype(BF16)
     pl.semaphore_wait(barrier, len(peers))
 
     half_cols = width // 2
@@ -587,6 +591,11 @@
             ag_end_far(u, 2).start()
             ag_end_far(u, 1).start()
 
+    w[1, mine, :] = jnp.concatenate([win[3 + i] for i in range(4)], 1).astype(BF16)
+    w[2, mine, :] = jnp.concatenate(out_t[1:], 1).astype(BF16)
+
+    load_vec.wait()
+    load_bias.wait()
     load_resid.wait()
     load_cot.wait()
     gain_one, shift_one = vec[0], vec[1]
@@ -740,13 +749,19 @@
 
         lax.fori_loop(0, 2, step, 0)
 
-    def rs_quad(k, compute, held):
+    def rs_quad(k, compute, held, between=None):
         for half in range(2):
             rs_core(k - 2, half).wait_send()
 
         def step(s, carry):
             half, odd = lax.div(s, 2), lax.rem(s, 2)
             yq = half * y + (1 - half) * (1 - y)
+            if between is not None:
+
+                @pl.when(s == 2)
+                def _():
+                    between()
+
             part = compute(2 * yq + lax.rem(1 - odd + c, 2))
 
             @pl.when(odd == 0)
@@ -1116,33 +1131,36 @@
 
     def attend_back(i, which_heads, hh=None):
         first, last_row = i * quarter, (i + 1) * quarter
+        size = quarter
         rows = slice(first, last_row)
         if hh is not None:
-            rows = rows_at(first + hh * (quarter // 2), quarter // 2, quarter // 2)
-        got, kept = {}, {}
-        for h in which_heads:
-            at = h // 2
+            size = quarter // 2
+            rows = rows_at(first + hh * size, size, size)
+        for at, group in enumerate(((0, 1), (2,))):
+            if group[0] not in which_heads:
+                continue
+            count = len(group)
             tile = slice(at * 128, (at + 1) * 128)
-            d_out = dmix[rows, tile].astype(F32) * linv[h, rows, :]
-            d_out = jnp.where(low_half, d_out, 0.0) if h == 0 else jnp.where(low_half, 0.0, d_out)
-            inner = jnp.sum(d_out * mixed[rows, tile].astype(F32), -1, keepdims=True)
+            d_tile, out_tile = dmix[rows, tile].astype(F32), mixed[rows, tile].astype(F32)
+            d_out = []
+            for h in group:
+                scaled = d_tile * linv[h, rows, :]
+                d_out += [jnp.where(low_half, scaled, 0.0) if h == 0 else jnp.where(low_half, 0.0, scaled)]
+            d_out = jnp.concatenate(d_out, 0)
+            inner = jnp.sum(d_out * jnp.concatenate([out_tile] * count, 0), -1, keepdims=True)
             d_scaled = d_out.astype(BF16)
-            expo = e_s[h, rows, 0:last_row]
+            heads_here = slice(group[0], group[-1] + 1)
+            expo = e_s[heads_here, rows, 0:last_row].reshape(count * size, last_row)
+            queries = q_s[heads_here, rows, :].reshape(count * size, 2 * HD)
             d_probs = mm(d_scaled, v_s[at, 0:last_row, :], NT)
             d_scores = (expo.astype(F32) * (d_probs - inner)).astype(BF16)
-            got[h] = mm(d_scores, k_s[at, 0:last_row, :]) * eighth
-            kept[h] = (d_scores, d_scaled, expo)
-        for at, group in enumerate(((0, 1), (2,))):
-            if group[0] not in got:
-                continue
-            queries = jnp.concatenate([q_s[h, rows, :] for h in group], 0)
-            d_s, d_o, exps = [jnp.concatenate([kept[h][i] for h in group], 0) for i in range(3)]
-            dk_s[at, :, 0:last_row] = dk_s[at, :, 0:last_row] + mm(queries, d_s, TN)
-            dv_s[at, :, 0:last_row] = dv_s[at, :, 0:last_row] + mm(d_o, exps, TN)
-        if 0 in got:
-            dqkv[rows, 0:128] = jnp.where(low_half, got[0], got[1]).astype(BF16)
-        if 2 in got:
-            dqkv[rows, 384:512] = jnp.where(low_half, got[2], 0.0).astype(BF16)
+            d_q = mm(d_scores, k_s[at, 0:last_row, :]) * eighth
+            dk_s[at, :, 0:last_row] = dk_s[at, :, 0:last_row] + mm(queries, d_scores, TN)
+            dv_s[at, :, 0:last_row] = dv_s[at, :, 0:last_row] + mm(d_scaled, expo, TN)
+            if at == 0:
+                dqkv[rows, 0:128] = jnp.where(low_half, d_q[0:size], d_q[size:]).astype(BF16)
+            else:
+                dqkv[rows, 384:512] = jnp.where(low_half, d_q, 0.0).astype(BF16)
 
     def back_quarters(near, which_heads, fresh, prepare=None):
         def step(s, carry):
@@ -1236,9 +1254,12 @@
         sm[7:8, :] = sm[7:8, :] + jnp.sum(d_low.astype(F32), 0, keepdims=True)
         return part
 
-    end_pump(0, 2)
-    mid_pump(0, 0)
-    rs_quad(3, first_back, xhat2)
+
+    def first_pumps():
+        end_pump(0, 2)
+        mid_pump(0, 0)
+
+    rs_quad(3, first_back, xhat2, first_pumps)
     end_pump(0, 1)
 
     small_c = rcopy(sm, smp, 27, 77, c_dev)
@@ -1340,6 +1361,8 @@
     scratch = [
         vm(win.shape, F32),
         vm(wout.shape, F32),
+        vm(bias.shape, F32),
+        vm(vec.shape, F32),
         vm((tokens, width), F32),
         vm((tokens, width), F32),
         vm((tokens, 1), F32),
@@ -1384,11 +1407,10 @@
         vm((2, 8, width), F32),
         vm((4, 8, width), F32),
         vm((2, 8, width), F32),
-        pltpu.SemaphoreType.DMA((11,)),
+        pltpu.SemaphoreType.DMA((13,)),
         pltpu.SemaphoreType.DMA((30,)),
         pltpu.SemaphoreType.DMA((83,)),
     ]
-    whole = pl.BlockSpec(memory_space=pltpu.VMEM)
     return pl.pallas_call(
         functools.partial(block_kernel, sizes),
         out_shape=(
@@ -1397,7 +1419,7 @@
             jax.ShapeDtypeStruct((3, rows, width), F32),
             jax.ShapeDtypeStruct((8, width), F32),
         ),
-        in_specs=[pl.BlockSpec(memory_space=pl.ANY)] * 4 + [whole] * 2,
+        in_specs=[pl.BlockSpec(memory_space=pl.ANY)] * 6,
         out_specs=[pl.BlockSpec(memory_space=pl.ANY)] * 4,
         scratch_shapes=scratch,
         compiler_params=pltpu.CompilerParams(

time: 99.2 us -> 98.5 us (level)
  no operation moved by 1% of the time
where the time goes in v7:
time: 98.5 us; the launch traced here: 98.3 us
  Pallas kernels  97.5 us (99%)
    pallas_call x1, Pallas kernels, run_block(): pl.pallas_call(functools.partial(block_kernel, sizes), out_shape=(jax.Sha...  92.9 us
    pallas_call x1, Pallas kernels, run_adam(): pl.pallas_call(functools.partial(adam_kernel, hc), out_shape=[jax.ShapeDt...  4.59 us

profile of v7, /device:TPU:0, one launch (start us, length us, event | category | flops | bytes accessed | tf_op | source)
XLA Modules:
  0.0 98.3 jit_solution(14618231989864434507)
XLA Ops:
  0.6 92.9 %block.1 = (f32[256,768]{1,0:T(8,128)}, f32[256,768]{1,0:T(8,128)}, f32[3,96,768]{2,1,0:T(8,128)}, f32[8,768]{1,0:T(8,128)}) custom-call(f32[1024,768]{1,0:T(8,128)} %resid_h.1, f32[1024,768]{1,0:T(8,128)} %cot_h.1, f32[7,96,192]{2,1,0:T(8,128)} %bitcast.36, f32[5,192,96]{2,1,0:T(8,128)} %bitcast.38, f32[6,1,192]{2,1,0:T(1,128)} %bitcast.46, ...), custom_call_target="tpu_custom_call" | custom-call | tf_op jit(solution)/shard_map/block/pallas_call | solution.py:1414
  93.6 4.6 %adam.1 = (f32[256,768]{1,0:T(8,128)}, f32[256,768]{1,0:T(8,128)}, f32[7,96,192]{2,1,0:T(8,128)}, f32[7,96,192]{2,1,0:T(8,128)}, f32[7,96,192]{2,1,0:T(8,128)}, ...) custom-call(f32[256,768]{1,0:T(8,128)} %get-tuple-element.32.refs_0_, ...), custom_call_target="tpu_custom_call" | custom-call | tf_op jit(solution)/shard_map/adam/pallas_call | solution.py:1526

commit v8 on v7

--- a/solution.py
+++ b/solution.py
@@ -617,10 +617,9 @@
         return carry
 
     lax.fori_loop(0, tokens // 128, first_norm, 0)
-    for u, i in ((0, 0), (0, 1), (1, 0), (1, 1)):
+    for u, i in ((0, 0), (0, 1), (1, 1), (0, 2), (1, 0)):
         pump_mid(u, i)
     mid_start(2)
-    pump_mid(0, 2)
     pump_mid(1, 2)
     pump_end(0, 0)
     pump_end(1, 0)
@@ -629,7 +628,7 @@
     def _():
         ag_pair(2).start()
 
-    for u, i in ((0, 2), (0, 1), (1, 2), (1, 1)):
+    for u, i in ((0, 2), (0, 1), (1, 1), (1, 2)):
         pump_end(u, i)
 
     @pl.when(is_end == 1)
@@ -712,13 +711,13 @@
             mixed[rows, 128:256] = jnp.where(low_half, 0.0, got[2]).astype(BF16)
 
     def rs_core(k, half):
-        return rcopy(ps.at[k % 2, half], crecv.at[k, half], 16 + 2 * (k % 2) + half, 16 + 2 * k + half, c_dev)
+        return rcopy(ps.at[k % 2, half], crecv.at[k, half], 16 + 2 * (k % 2) + half, 16 + 2 * (k % 2) + half, c_dev)
 
     halves = [slice(0, quarter // 2), slice(quarter // 2, quarter)]
 
     def rs_y(k, hh):
         src, dst = ysend.at[k, halves[hh], :], yrecv.at[k, halves[hh], :]
-        return rcopy(src, dst, 20, 24 + 2 * k + hh, y_dev)
+        return rcopy(src, dst, 20, 20 + 2 * (k % 2) + hh, y_dev)
 
     def rs_y_start(k):
         for hh in range(2):
@@ -834,15 +833,15 @@
 
     def qg_y(g, ref, hh):
         src = q_rows(ref, ten, hh)
-        return rcopy(src, src, 21, 32 + 2 * g + hh, y_dev)
+        return rcopy(src, src, 21, 24 + hh, y_dev)
 
     def qg_c(g, ref, hh):
         src = q_rows(ref, ten, hh)
-        return rcopy(src, src, 22, 36 + g, c_dev)
+        return rcopy(src, src, 22, 26, c_dev)
 
     def qg_f(g, ref, hh):
         src = q_rows(ref, ten + 2 - 4 * y, hh)
-        return rcopy(src, src, 23, 38 + 2 * g + hh, c_dev)
+        return rcopy(src, src, 23, 27 + hh, c_dev)
 
     def qg_start(g, ref, hh):
         qg_y(g, ref, hh).start()
@@ -853,7 +852,7 @@
         return rcopy(rows, rows, send, recv, c_dev)
 
     def qg_near(g, ref):
-        qg_rows(ref, quarter, 22, 36 + g).wait_recv()
+        qg_rows(ref, quarter, 22, 26).wait_recv()
 
     def qg_far(g, ref, hh):
         qg_y(g, ref, hh).wait_recv()
@@ -937,7 +936,7 @@
     def gx(u, zi):
         b, cols = g_units[u]
         src = gmat.at[b, rows_at((2 * zi + 1 - x) * shard, shard, shard), cols]
-        return rcopy(src, xr.at[b, zi, :, cols], 8 + u, 42 + 4 * u + zi, x_dev)
+        return rcopy(src, xr.at[b, zi, :, cols], 8 + u, 29 + 4 * u + zi, x_dev)
 
     def line_to(i):
         if i == 0:
@@ -947,12 +946,12 @@
     def gz(u, i):
         b, cols = g_units[u]
         dev, slot = line_to(i)
-        return rcopy(zs.at[b, i, :, cols], zr.at[b, slot, :, cols], 12 + u, 58 + 4 * u + slot, dev)
+        return rcopy(zs.at[b, i, :, cols], zr.at[b, slot, :, cols], 12 + u, 45 + 4 * u + slot, dev)
 
     def gz_arrive(u, slot):
         b, cols = g_units[u]
         ref = zr.at[b, slot, :, cols]
-        rcopy(ref, ref, 12 + u, 58 + 4 * u + slot, x_dev).wait_recv()
+        rcopy(ref, ref, 12 + u, 45 + 4 * u + slot, x_dev).wait_recv()
 
     def g_start(u):
         @pl.when(is_end == 1)
@@ -1018,10 +1017,10 @@
 
     def side_copy(src, i):
         dev, slot = line_to(i)
-        return rcopy(src, side_r.at[slot], 28, 78 + slot, dev)
+        return rcopy(src, side_r.at[slot], 28, 65 + slot, dev)
 
     def side_arrive(slot):
-        rcopy(side_r.at[slot], side_r.at[slot], 28, 78 + slot, x_dev).wait_recv()
+        rcopy(side_r.at[slot], side_r.at[slot], 28, 65 + slot, x_dev).wait_recv()
 
     def side_start():
         @pl.when(is_end == 1)
@@ -1041,7 +1040,7 @@
                 side_copy(side_s.at[i - 1], i).start()
 
     def side_x():
-        return rcopy(side_xs, side_xr, 29, 82, x_dev)
+        return rcopy(side_xs, side_xr, 29, 69, x_dev)
 
     def side_cross():
         side_arrive(0)
@@ -1204,7 +1203,7 @@
             dqkv[:, 384:512] = jnp.where(low_half, dqkv[:, 384:512], d_v)
             dqkv[:, 640:768] = jnp.transpose(dk_s[1]).astype(BF16)
 
-    def zero_rows(u, zo):
+    def zero_rows(u, zo, send=True):
         cols = rows_at(zo * 2 * shard, 2 * shard, 2 * shard)
         left = normed_t[cols, :]
         if u == 0:
@@ -1213,9 +1212,10 @@
             g_qkv = mm(left, dqkv[:, 384:768])
             gmat[0, cols, 384:512] = g_qkv[:, 0:128].astype(BF16)
             gmat[0, cols, 512:768] = (g_qkv[:, 128:384] + gproj[cols, :]).astype(BF16)
-        gx(u, zo).start()
-
-    def zero_unit(u, steps):
+        if send:
+            gx(u, zo).start()
+
+    def zero_unit(u, steps, send=True):
         def step(s, carry):
             odd, half = lax.rem(s, 2), lax.div(s, 2)
             first = is_end * owner_z[2] + is_mid * owner_z[0]
@@ -1223,7 +1223,7 @@
             third = is_end * owner_z[0] + is_mid * owner_z[1]
             early = (1 - odd) * first + odd * second
             late = (1 - odd) * third + odd * z
-            zero_rows(u, (1 - half) * early + half * late)
+            zero_rows(u, (1 - half) * early + half * late, send)
             return carry
 
         lax.fori_loop(*steps, step, 0)
@@ -1262,17 +1262,29 @@
     rs_quad(3, first_back, xhat2, first_pumps)
     end_pump(0, 1)
 
-    small_c = rcopy(sm, smp, 27, 77, c_dev)
+    small_c = rcopy(sm, smp, 27, 64, c_dev)
     small_c.start()
     quad_far(3, xhat2)
     rs_y_start(3)
+    zero_unit(1, (0, 2), False)
     small_c.wait_recv()
     smx[0, 0:6, :] = sm[0:6, :] + smp[0:6, :]
     smx[0, 6:8, :] = smp[6:8, :]
-    small_x = rcopy(smx.at[0], smx.at[1], 24, 74, cross_dev)
+    small_x = rcopy(smx.at[0], smx.at[1], 24, 61, cross_dev)
     small_x.start()
+
+    @pl.when(is_end == 1)
+    def _():
+        for i in (2, 1):
+            gx(1, owner_z[i]).start()
+
+    @pl.when(is_mid == 1)
+    def _():
+        for i in (0, 2):
+            gx(1, owner_z[i]).start()
+
+    zero_unit(1, (2, 4))
     end_pump(0, 0)
-    zero_unit(1, (0, 4))
     quad_near(3)
     mid_pump(0, 2)
     small_x.wait_recv()
@@ -1280,7 +1292,7 @@
     smz[z, 6:8, :] = sm[6:8, :] + smx[1, 6:8, :]
 
     def small_z(j):
-        return rcopy(smz.at[z], smz.at[z], 25, 75, z_dev(j))
+        return rcopy(smz.at[z], smz.at[z], 25, 62, z_dev(j))
 
     for j in (3, 2, 1):
         small_z(j).start()
@@ -1311,10 +1323,10 @@
 
     first_norm_back(0)
     end_pump(1, 0)
-    three = rcopy(smz.at[0:3], smz.at[0:3], 25, 75, x_dev)
+    three = rcopy(smz.at[0:3], smz.at[0:3], 25, 62, x_dev)
     three.wait_recv()
     smy[0] = (smz[0] + smz[1]) + (smz[2] + smz[3])
-    small_y = rcopy(smy.at[0], smy.at[1], 26, 76, y_dev)
+    small_y = rcopy(smy.at[0], smy.at[1], 26, 63, y_dev)
     small_y.start()
     mid_pump(1, 2)
     first_norm_back(1)
@@ -1324,14 +1336,14 @@
     for u in range(4):
         ag_drain(u)
     three_sides = side_r.at[0:3]
-    rcopy(three_sides, three_sides, 28, 78, x_dev).wait_send()
+    rcopy(three_sides, three_sides, 28, 65, x_dev).wait_send()
     side_x().wait_send()
     rcopy(ysend, yrecv, 20, 24, y_dev).wait_send()
     for k in (2, 3):
         for half in range(2):
             rs_core(k, half).wait_send()
     for send in (21, 22, 23):
-        qg_rows(hidden, 2 * quarter, send, 36).wait_send()
+        qg_rows(hidden, 2 * quarter, send, 26).wait_send()
     small_x.wait_send()
     three.wait_send()
     g_finish(0)
@@ -1409,7 +1421,7 @@
         vm((2, 8, width), F32),
         pltpu.SemaphoreType.DMA((13,)),
         pltpu.SemaphoreType.DMA((30,)),
-        pltpu.SemaphoreType.DMA((83,)),
+        pltpu.SemaphoreType.DMA((70,)),
     ]
     return pl.pallas_call(
         functools.partial(block_kernel, sizes),

time: 98.5 us -> 98.4 us (level)
  no operation moved by 1% of the time
where the time goes in v8:
time: 98.4 us; the launch traced here: 98.2 us
  Pallas kernels  97.4 us (99%)
    pallas_call x1, Pallas kernels, run_block(): pl.pallas_call(functools.partial(block_kernel, sizes), out_shape=(jax.Sha...  92.8 us
    pallas_call x1, Pallas kernels, run_adam(): pl.pallas_call(functools.partial(adam_kernel, hc), out_shape=[jax.ShapeDt...  4.59 us

profile of v8, /device:TPU:0, one launch (start us, length us, event | category | flops | bytes accessed | tf_op | source)
XLA Modules:
  0.0 98.2 jit_solution(18120709842883155684)
XLA Ops:
  0.6 92.8 %block.1 = (f32[256,768]{1,0:T(8,128)}, f32[256,768]{1,0:T(8,128)}, f32[3,96,768]{2,1,0:T(8,128)}, f32[8,768]{1,0:T(8,128)}) custom-call(f32[1024,768]{1,0:T(8,128)} %resid_h.1, f32[1024,768]{1,0:T(8,128)} %cot_h.1, f32[7,96,192]{2,1,0:T(8,128)} %bitcast.36, f32[5,192,96]{2,1,0:T(8,128)} %bitcast.38, f32[6,1,192]{2,1,0:T(1,128)} %bitcast.46, ...), custom_call_target="tpu_custom_call" | custom-call | tf_op jit(solution)/shard_map/block/pallas_call | solution.py:1426
  93.5 4.6 %adam.1 = (f32[256,768]{1,0:T(8,128)}, f32[256,768]{1,0:T(8,128)}, f32[7,96,192]{2,1,0:T(8,128)}, f32[7,96,192]{2,1,0:T(8,128)}, f32[7,96,192]{2,1,0:T(8,128)}, ...) custom-call(f32[256,768]{1,0:T(8,128)} %get-tuple-element.32.refs_0_, ...), custom_call_target="tpu_custom_call" | custom-call | tf_op jit(solution)/shard_map/adam/pallas_call | solution.py:1538
